TPU v7x, 32 devices: a whole 2x2x4 slice. The times are simulated.
32 devices in a mesh: groups: 2 (over y), width: 8 (over z, x), hidden: 2 (over core).
Axes of the slice: x: 2, y: 2, z: 4, core: 2. Of those that a mesh axis runs over, the one named last changes fastest.
Arguments:
- replay_store: bfloat16 [512, 8192], P('groups', 'width'), parts along dimension 0, may hold values from -18 to 18
- replay_ids: int32 [256], P('groups'), parts along dimension 0, may hold values from 0 to 255, as said below
- excluded: int32 [32], P('groups'), parts along dimension 0, may hold values from 0 to 127, as said below
- norm_gain: float32 [8192], P('width'), may hold values from 0.1 to 1.9
- w_gate: bfloat16 [8192, 14336], P('width', 'hidden'), may hold values from -0.0625 to 0.0625
- w_up: bfloat16 [8192, 14336], P('width', 'hidden'), may hold values from -0.0625 to 0.0625
- w_down: bfloat16 [14336, 8192], P('hidden', 'width'), may hold values from -0.046875 to 0.046875
- grad_out: bfloat16 [256, 8192], P('groups', 'width'), parts along dimension 0, may hold values from -6 to 6
Outputs:
- output: bfloat16 [256, 8192], P('groups', 'width'), parts along dimension 0
- store_grad: bfloat16 [512, 8192], P('groups', 'width'), parts along dimension 0
- gain_grad: float32 [16384], P(('groups', 'width')), parts along dimension 0
- gate_grad: bfloat16 [16384, 14336], P(('groups', 'width'), 'hidden'), parts along dimension 0
- up_grad: bfloat16 [16384, 14336], P(('groups', 'width'), 'hidden'), parts along dimension 0
- down_grad: bfloat16 [28672, 8192], P(('groups', 'hidden'), 'width'), parts along dimension 0
There are 2 independent parts, one for each index of `groups`. A program takes and returns all parts, laid end to end along the dimension named above; an argument that names none is the same for every part. Nothing has to cross between parts.
Inputs may be any that keep to these rules, and one draw needn't show every extreme that they name: `replay_ids`: store rows may repeat; both ends of the range occur. `excluded`: positions may repeat; both ends of the range occur.
All inputs are finite; a program needn't handle non-finite values.
Results may differ from a plain program's by a relative error of at most 0.0068.
Values may be sent and summed in bfloat16 or wider, within the bound.
No kernel may reach another device: no remote copies, remote signals or barrier semaphores. Data moves between devices by JAX's collectives and lax.ppermute only.
A program may use at most 256 MiB of HBM per device.

v0:
```python
import jax
import jax.numpy as jnp
from jax import lax
from jax.sharding import PartitionSpec as P

D = 8192


EPS = 1e-05


def swiglu(gate_pre, up_proj):
    return (gate_pre * jax.nn.sigmoid(gate_pre) * up_proj).astype(jnp.bfloat16)


def swiglu_backward(d_hidden, gate_pre, up_proj):
    sigmoid_gate = jax.nn.sigmoid(gate_pre)
    d_gate = (d_hidden * up_proj * sigmoid_gate * (1.0 + gate_pre * (1.0 - sigmoid_gate))).astype(
        jnp.bfloat16
    )
    d_up = (d_hidden * gate_pre * sigmoid_gate).astype(jnp.bfloat16)
    return (d_gate, d_up)


def shards(replay_store, replay_ids, excluded, norm_gain, w_gate, w_up, w_down, grad_out):
    contract_last = (((1,), (1,)), ((), ()))
    contract_first = (((0,), (0,)), ((), ()))
    row_data = jnp.take(replay_store, replay_ids, axis=0)
    row_float = row_data.astype(jnp.float32)
    squares = lax.psum(jnp.sum(row_float * row_float, axis=1, keepdims=True), "width")
    inv_rms = lax.rsqrt(squares / D + EPS)
    normed = (row_float * inv_rms * norm_gain).astype(jnp.bfloat16)
    gate_part = jnp.dot(normed, w_gate, preferred_element_type=jnp.float32)
    up_part = jnp.dot(normed, w_up, preferred_element_type=jnp.float32)
    gate_pre, up_proj = (
        lax.psum_scatter(gate_part, "width", scatter_dimension=0, tiled=True),
        lax.psum_scatter(up_part, "width", scatter_dimension=0, tiled=True),
    )
    hidden = lax.all_gather(swiglu(gate_pre, up_proj), "width", axis=0, tiled=True)
    projected = lax.psum(jnp.dot(hidden, w_down, preferred_element_type=jnp.float32), "hidden")
    output = (row_float + projected).astype(jnp.bfloat16)
    token_count = grad_out.shape[0]
    positions = lax.iota(jnp.int32, token_count)
    dropped = jnp.any(positions[:, None] == excluded[None, :], axis=1)
    d_output = jnp.where(dropped[:, None], jnp.zeros_like(grad_out), grad_out)
    d_hidden_part = lax.dot_general(
        d_output, w_down, contract_last, preferred_element_type=jnp.float32
    )
    d_hidden = lax.psum_scatter(d_hidden_part, "width", scatter_dimension=0, tiled=True)
    gate_piece, up_piece = swiglu_backward(d_hidden, gate_pre, up_proj)
    d_gate, d_up = (
        lax.all_gather(gate_piece, "width", axis=0, tiled=True),
        lax.all_gather(up_piece, "width", axis=0, tiled=True),
    )
    down_grad = lax.dot_general(
        hidden, d_output, contract_first, preferred_element_type=jnp.float32
    ).astype(jnp.bfloat16)
    gate_grad = lax.dot_general(
        normed, d_gate, contract_first, preferred_element_type=jnp.float32
    ).astype(jnp.bfloat16)
    up_grad = lax.dot_general(
        normed, d_up, contract_first, preferred_element_type=jnp.float32
    ).astype(jnp.bfloat16)
    normed_part = lax.dot_general(d_gate, w_gate, contract_last, preferred_element_type=jnp.float32)
    normed_part = normed_part + lax.dot_general(
        d_up, w_up, contract_last, preferred_element_type=jnp.float32
    )
    d_normed = lax.psum(normed_part, "hidden")
    gain_grad = jnp.sum(d_normed * row_float * inv_rms, axis=0)
    scaled = d_normed * norm_gain
    inner_sum = lax.psum(jnp.sum(scaled * row_float, axis=1, keepdims=True), "width")
    d_rows = (
        d_output.astype(jnp.float32)
        + inv_rms * scaled
        - row_float * inv_rms * inv_rms * inv_rms * (inner_sum / D)
    )
    store_grad = (
        jnp.zeros(replay_store.shape, jnp.float32).at[replay_ids].add(d_rows).astype(jnp.bfloat16)
    )
    return (output, store_grad, gain_grad, gate_grad, up_grad, down_grad)


def solution(mesh):
    return jax.shard_map(
        shards,
        mesh=mesh,
        in_specs=(
            P("groups", "width"),
            P("groups"),
            P("groups"),
            P("width"),
            P("width", "hidden"),
            P("width", "hidden"),
            P("hidden", "width"),
            P("groups", "width"),
        ),
        out_specs=(
            P("groups", "width"),
            P("groups", "width"),
            P(("groups", "width")),
            P(("groups", "width"), "hidden"),
            P(("groups", "width"), "hidden"),
            P(("groups", "hidden"), "width"),
        ),
        check_vma=False,
    )
```

profile of v0, /device:TPU:0, one launch (start us, length us, event | category | flops | bytes accessed | tf_op | source)
XLA Modules:
  0.0 484.9 jit_solution(11470029436671369278)
XLA Ops:
  7.2 0.0 reduce-scatter.8.cloned.1.call-start
  7.2 0.8 fusion.21
  8.0 12.0 %fusion.22 = f32[128,7168]{1,0:T(8,128)} fusion(bf16[7168,1024]{1,0:T(8,128)(2,1)} %param.14, bf16[128,1024]{1,0:T(8,128)(2,1)} %param.15, pred[128]{0:T(512)(128)(4,1)S(1)} %fusion.21), kind=kOutput, calls=%fused_computation.44 | convolution fusion | flops 1879179264 | bytes 18612352 | tf_op jit(solution)/shard_map/dot_general | solution.py:46
  20.1 0.0 reduce-scatter.4.cloned.1.call-start
  20.2 0.9 gather_fusion
  21.0 0.2 fusion.8
  21.2 23.7 %psum.28 = f32[128,1]{0,1:T(1,128)S(1)} all-reduce(f32[128,1]{0,1:T(1,128)S(1)} %bitcast.19), channel_id=1, replica_groups=mesh['groups'=2,'width'=8,'hidden'=2] {'width'}, use_global_device_ids=true, to_apply=%region_1.2 | all-reduce | flops 128 | bytes 1024 | tf_op jit(solution)/shard_map/psum | solution.py:30
  45.0 9.5 %fusion.27 = f32[128,7168]{1,0:T(8,128)} fusion(bf16[1024,7168]{1,0:T(8,128)(2,1)} %param.12, f32[1024]{0:T(1024)S(1)} %copy-done.6, f32[128]{0:T(128)S(1)} %rsqrt_bitcast_fusion, bf16[128,1024]{1,0:T(8,128)(2,1)S(1)} %gather_fusion, pred[128]{0:T(512)(128)(4,1)S(1)} %compare_and_fusion), kind=kOutput, calls=%fused_computation.46 | convolution fusion | flops 1879703552 | bytes 18616960 | tf_op jit(solution)/shard_map/dot_general | solution.py:33
  54.5 0.0 reduce-scatter.6.cloned.1.call-start
  54.6 9.3 %fusion.25 = f32[128,7168]{1,0:T(8,128)} fusion(bf16[1024,7168]{1,0:T(8,128)(2,1)} %param.13, f32[1024]{0:T(1024)S(1)} %copy-done.6, f32[128]{0:T(128)S(1)} %rsqrt_bitcast_fusion, bf16[128,1024]{1,0:T(8,128)(2,1)S(1)} %gather_fusion, pred[128]{0:T(512)(128)(4,1)S(1)} %compare_and_fusion), kind=kOutput, calls=%fused_computation.45 | convolution fusion | flops 1879703552 | bytes 18616960 | tf_op jit(solution)/shard_map/dot_general | solution.py:34
  63.9 0.0 all-gather.4.cloned.1.call-start
  64.0 39.9 %reduce-scatter.8.cloned.1.call-done = f32[16,7168]{1,0:T(8,128)} async-done(((f32[128,7168]{1,0:T(8,128)}), f32[16,7168]{1,0:T(8,128)}) %reduce-scatter.8.cloned.1.call-update) | async-done | bytes 458768 | tf_op jit(solution)/shard_map/reduce_scatter | solution.py:49
  103.9 84.6 %reduce-scatter.4.cloned.1.call-done = f32[16,7168]{1,0:T(8,128)} async-done(((f32[128,7168]{1,0:T(8,128)}), f32[16,7168]{1,0:T(8,128)}) %reduce-scatter.4.cloned.1.call-update) | async-done | bytes 458768 | tf_op jit(solution)/shard_map/reduce_scatter | solution.py:36
  188.5 84.7 %reduce-scatter.6.cloned.1.call-done = f32[16,7168]{1,0:T(8,128)} async-done(((f32[128,7168]{1,0:T(8,128)}), f32[16,7168]{1,0:T(8,128)}) %reduce-scatter.6.cloned.1.call-update) | async-done | bytes 458768 | tf_op jit(solution)/shard_map/reduce_scatter | solution.py:37
  273.2 2.3 multiply_convert_fusion
  275.6 0.0 all-gather.6.cloned.1.call-start
  275.7 0.5 all-gather.6.cloned.1.call-update
  276.2 0.5 all-gather.8.cloned.1.call-update
  276.8 0.2 all-reduce.3.cloned.1.call-start
  277.0 44.8 %all-gather.4.cloned.1.call-done = bf16[128,7168]{1,0:T(8,128)(2,1)} async-done(((bf16[16,7168]{1,0:T(8,128)(2,1)}), bf16[128,7168]{1,0:T(8,128)(2,1)}) %all-gather.4.cloned.1.call-update) | async-done | bytes 1835024 | tf_op jit(solution)/shard_map/all_gather | solution.py:39
  321.8 8.6 %fusion.29 = f32[128,1024]{1,0:T(8,128)} fusion(bf16[128,7168]{1,0:T(8,128)(2,1)} %all-gather.4.cloned.1.call-done, bf16[7168,1024]{1,0:T(8,128)(2,1)} %param.14), kind=kOutput, calls=%fused_computation.47 | convolution fusion | flops 1879048192 | bytes 17039360 | tf_op jit(solution)/shard_map/dot_general | solution.py:40
  330.4 39.2 %all-gather.6.cloned.1.call-done = bf16[128,7168]{1,0:T(8,128)(2,1)} async-done(((bf16[16,7168]{1,0:T(8,128)(2,1)}), bf16[128,7168]{1,0:T(8,128)(2,1)}) %all-gather.6.cloned.1.call-update) | async-done | bytes 1835024 | tf_op jit(solution)/shard_map/all_gather | solution.py:52
  369.6 10.8 %fusion.30 = f32[128,1024]{1,0:T(8,128)S(1)} fusion(bf16[128,7168]{1,0:T(8,128)(2,1)} %all-gather.6.cloned.1.call-done, bf16[1024,7168]{1,0:T(8,128)(2,1)} %param.12), kind=kOutput, calls=%fused_computation.48 | convolution fusion | flops 1879048192 | bytes 17039360 | tf_op jit(solution)/shard_map/dot_general | solution.py:64
  380.5 37.1 %all-gather.8.cloned.1.call-done = bf16[128,7168]{1,0:T(8,128)(2,1)} async-done(((bf16[16,7168]{1,0:T(8,128)(2,1)}), bf16[128,7168]{1,0:T(8,128)(2,1)}) %all-gather.8.cloned.1.call-update) | async-done | bytes 1835024 | tf_op jit(solution)/shard_map/all_gather | solution.py:53
  417.6 11.5 %convolution_add_fusion = f32[128,1024]{1,0:T(8,128)} fusion(f32[128,1024]{1,0:T(8,128)S(1)} %fusion.30, bf16[128,7168]{1,0:T(8,128)(2,1)} %all-gather.8.cloned.1.call-done, bf16[1024,7168]{1,0:T(8,128)(2,1)} %param.13), kind=kOutput, calls=%fused_computation.5 | convolution fusion | flops 1879179264 | bytes 17563648 | tf_op jit(solution)/shard_map/dot_general | solution.py:65
  429.1 7.9 %convolution_convert_fusion.2 = bf16[1024,7168]{1,0:T(8,128)(2,1)} fusion(bf16[128,7168]{1,0:T(8,128)(2,1)S(1)} %copy-done.3, f32[1024]{0:T(1024)S(1)} %copy-done.6, f32[128]{0:T(128)S(1)} %rsqrt_bitcast_fusion, bf16[128,1024]{1,0:T(8,128)(2,1)S(1)} %gather_fusion, pred[128]{0:T(512)(128)(4,1)S(1)} %compare_and_fusion), kind=kOutput, calls=%fused_computation.4 | convolution fusion | flops 1887043584 | bytes 16781952 | tf_op jit(solution)/shard_map/dot_general | solution.py:58
  437.0 7.7 %convolution_convert_fusion.1 = bf16[1024,7168]{1,0:T(8,128)(2,1)} fusion(bf16[128,7168]{1,0:T(8,128)(2,1)S(1)} %copy-done.4, f32[1024]{0:T(1024)S(1)} %copy-done.6, f32[128]{0:T(128)S(1)} %rsqrt_bitcast_fusion, bf16[128,1024]{1,0:T(8,128)(2,1)S(1)} %gather_fusion, pred[128]{0:T(512)(128)(4,1)S(1)} %compare_and_fusion), kind=kOutput, calls=%fused_computation.3 | convolution fusion | flops 1887043584 | bytes 16781952 | tf_op jit(solution)/shard_map/dot_general | solution.py:61
  444.7 7.6 %convolution_convert_fusion = bf16[7168,1024]{1,0:T(8,128)(2,1)} fusion(bf16[128,7168]{1,0:T(8,128)(2,1)S(1)} %copy-done.2, bf16[128,1024]{1,0:T(8,128)(2,1)S(1)} %copy-done.5, pred[128]{0:T(512)(128)(4,1)S(1)} %fusion.21), kind=kOutput, calls=%fused_computation.2 | convolution fusion | flops 1886519296 | bytes 16777344 | tf_op jit(solution)/shard_map/dot_general | solution.py:55
  452.3 2.7 fusion.12
  455.1 19.5 %psum.31 = f32[128,1]{0,1:T(1,128)S(1)} all-reduce(f32[128,1]{0,1:T(1,128)S(1)} %bitcast.18), channel_id=1, replica_groups=mesh['groups'=2,'width'=8,'hidden'=2] {'width'}, use_global_device_ids=true, to_apply=%region_9.10 | all-reduce | flops 128 | bytes 1024 | tf_op jit(solution)/shard_map/psum | solution.py:71
  474.5 2.6 scatter_custom_fusion
  477.2 0.9 convert_element_type.40
  (28 shorter events, 0.2 us)
Async XLA Ops:
  7.2 13.0 %copy-start = (bf16[256,1024]{1,0:T(8,128)(2,1)S(1)}, bf16[256,1024]{1,0:T(8,128)(2,1)}, u32[]{:S(2)}) copy-start(bf16[256,1024]{1,0:T(8,128)(2,1)} %param.8) | copy-start | bytes 1572868
  7.2 96.7 %reduce-scatter.8.cloned.1.call-start = ((), (), s32[]{:S(2)}) async-start(), calls=%async_computation.6 | async-start | bytes 4128768 | tf_op jit(solution)/shard_map/reduce_scatter | solution.py:49
  8.0 12.1 %copy-start.7 = (s32[128]{0:T(128)S(1)}, s32[128]{0:T(128)}, u32[]{:S(2)}) copy-start(s32[128]{0:T(128)} %param.9) | copy-start | bytes 1540
  8.0 37.0 %copy-start.6 = (f32[1024]{0:T(1024)S(1)}, f32[1024]{0:T(1024)}, u32[]{:S(2)}) copy-start(f32[1024]{0:T(1024)} %param.11) | copy-start | bytes 12292
  20.1 168.4 %reduce-scatter.4.cloned.1.call-start = ((), (), s32[]{:S(2)}) async-start(), calls=%async_computation.3 | async-start | bytes 4128768 | tf_op jit(solution)/shard_map/reduce_scatter | solution.py:36
  54.5 218.7 %reduce-scatter.6.cloned.1.call-start = ((), (), s32[]{:S(2)}) async-start(), calls=%async_computation.4 | async-start | bytes 4128768 | tf_op jit(solution)/shard_map/reduce_scatter | solution.py:37
  63.9 257.9 %all-gather.4.cloned.1.call-start = ((), (), s32[]{:S(2)}) async-start(), calls=%async_computation.5 | async-start | bytes 2064384 | tf_op jit(solution)/shard_map/all_gather | solution.py:39
  275.6 94.0 %all-gather.6.cloned.1.call-start = ((), (), s32[]{:S(2)}) async-start(), calls=%async_computation.7 | async-start | bytes 2064384 | tf_op jit(solution)/shard_map/all_gather | solution.py:52
  276.2 141.4 %all-gather.8.cloned.1.call-start = ((), (), s32[]{:S(2)}) async-start(), calls=%async_computation.8 | async-start | bytes 2064384 | tf_op jit(solution)/shard_map/all_gather | solution.py:53
  276.8 175.6 %all-reduce.3.cloned.1.call-start = ((), (), s32[]{:S(2)}) async-start(), calls=%async_computation.9 | async-start | bytes 2097152 | tf_op jit(solution)/shard_map/psum | solution.py:40
  369.6 59.5 %copy-start.3 = (bf16[128,7168]{1,0:T(8,128)(2,1)S(1)}, bf16[128,7168]{1,0:T(8,128)(2,1)}, u32[]{:S(2)}) copy-start(bf16[128,7168]{1,0:T(8,128)(2,1)} %all-gather.6.cloned.1.call-done) | copy-start | bytes 5505028
  429.1 7.9 %copy-start.4 = (bf16[128,7168]{1,0:T(8,128)(2,1)S(1)}, bf16[128,7168]{1,0:T(8,128)(2,1)}, u32[]{:S(2)}) copy-start(bf16[128,7168]{1,0:T(8,128)(2,1)} %all-gather.8.cloned.1.call-done) | copy-start | bytes 5505028
  437.0 7.7 %copy-start.2 = (bf16[128,7168]{1,0:T(8,128)(2,1)S(1)}, bf16[128,7168]{1,0:T(8,128)(2,1)}, u32[]{:S(2)}) copy-start(bf16[128,7168]{1,0:T(8,128)(2,1)} %all-gather.4.cloned.1.call-done) | copy-start | bytes 5505028
  437.0 7.7 %copy-start.5 = (bf16[128,1024]{1,0:T(8,128)(2,1)S(1)}, bf16[128,1024]{1,0:T(8,128)(2,1)}, u32[]{:S(2)}) copy-start(bf16[128,1024]{1,0:T(8,128)(2,1)} %param.15) | copy-start | bytes 786436
  437.0 41.0 %copy-start.1 = (bf16[256,1024]{1,0:T(8,128)(2,1)S(1)}, bf16[256,1024]{1,0:T(8,128)(2,1)}, u32[]{:S(2)}) copy-start(bf16[256,1024]{1,0:T(8,128)(2,1)} %param.8) | copy-start | bytes 1572868
Sparse Core Ops, SparseCore 0:
  20.2 83.6 reduce-scatter.7
  108.1 80.3 reduce-scatter.3
  192.7 80.4 reduce-scatter.5
  275.9 45.8 all-gather.3
  324.4 45.1 all-gather.5
  372.2 45.2 all-gather.7
  429.2 18.6 all-reduce.2
where the time goes:
time: 485 us
  waiting for transfers between devices  332 us (68%)
  matrix products  85 us (18%)
  blocking collectives  43.2 us (9%)
  between operations  14.2 us (3%)
  other arithmetic  9.61 us (2%)
    reduce_scatter x1, waiting for transfers between devices, shards(): lax.psum_scatter(up_part, 'width', scatter_dimension=0, tiled=True)  84.7 us
    reduce_scatter x1, waiting for transfers between devices, shards(): lax.psum_scatter(gate_part, 'width', scatter_dimension=0, tiled=True)  84.6 us
    all_gather x1, waiting for transfers between devices, shards(): lax.all_gather(swiglu(gate_pre, up_proj), 'width', axis=0, tiled=True)  44.8 us
    reduce_scatter x1, waiting for transfers between devices, shards(): lax.psum_scatter(d_hidden_part, 'width', scatter_dimension=0, tiled=True)  39.9 us
    all_gather x1, waiting for transfers between devices, shards(): lax.all_gather(gate_piece, 'width', axis=0, tiled=True)  39.2 us
    all_gather x1, waiting for transfers between devices, shards(): lax.all_gather(up_piece, 'width', axis=0, tiled=True)  37.1 us
    psum x1, blocking collectives, shards(): lax.psum(jnp.sum(row_float * row_float, axis=1, keepdims=True), 'width')  23.7 us
    psum x1, blocking collectives, shards(): lax.psum(jnp.sum(scaled * row_float, axis=1, keepdims=True), 'width')  19.5 us
  transfers between devices with their start and end apart: 7, of which 6 were waited for; matrix products, arithmetic and copies ran while one was open for 13% of the time, Pallas kernels for 0%

commit v1 on v0

v1 whole, which is shorter than its diff:
```python
import functools

import jax
import jax.numpy as jnp
from jax import lax
from jax.experimental import pallas as pl
from jax.experimental.pallas import tpu as pltpu
from jax.sharding import PartitionSpec as P

EPS = 1e-05
BF16 = jnp.bfloat16
F32 = jnp.float32
CHUNKS = 4
NT = (((1,), (1,)), ((), ()))
TN = (((0,), (0,)), ((), ()))
VMEM = pl.BlockSpec(memory_space=pltpu.VMEM)
SMEM = pl.BlockSpec(memory_space=pltpu.SMEM)
ANY = pl.BlockSpec(memory_space=pl.ANY)


def cost(flops, nbytes):
    return pl.CostEstimate(flops=int(flops), bytes_accessed=int(nbytes), transcendentals=0)


def params(mib):
    return pltpu.CompilerParams(vmem_limit_bytes=mib * 1024 * 1024)


def matmul(a, b, dims=(((1,), (0,)), ((), ()))):
    return lax.dot_general(a, b, dims, preferred_element_type=F32)


def tile_of(n):
    for t in (256, 128):
        if n % t == 0:
            return t
    return n


def order(label, tokens, block):
    p = lax.broadcasted_iota(jnp.int32, (tokens, tokens), 0)
    t = lax.broadcasted_iota(jnp.int32, (tokens, tokens), 1)
    return ((p // block) ^ label) * block + p % block == t


def start_kernel(block, label, store, ids, excluded, grad_out, rows, dout, squares):
    tokens = grad_out.shape[0]
    pool = store.shape[0]
    perm = jnp.where(order(label[0], tokens, block), 1.0, 0.0).astype(BF16)
    hit = lax.broadcasted_iota(jnp.int32, (pool, tokens), 0) == ids[...]
    natural = matmul(jnp.where(hit, 1.0, 0.0).astype(BF16), store[...], TN)
    total = jnp.sum(natural * natural, axis=1, keepdims=True)
    squares[...] = jnp.transpose(jnp.broadcast_to(total, (tokens, tokens)))[:1]
    rows[...] = matmul(perm, natural.astype(BF16)).astype(BF16)
    position = lax.broadcasted_iota(jnp.int32, (tokens, excluded.shape[1]), 0)
    match = jnp.where(position == excluded[...], 1.0, 0.0)
    dropped = jnp.max(match, axis=1, keepdims=True) > 0.0
    kept = jnp.where(dropped, 0.0, grad_out[...].astype(F32)).astype(BF16)
    dout[...] = matmul(perm, kept).astype(BF16)


def norm_kernel(block, width, label, rows, squares, gain, normed, flipped):
    tokens = rows.shape[0]
    inv = lax.rsqrt(squares[...] / width + EPS)
    inv = jnp.where(order(label[0], tokens, block), inv, 0.0)
    inv = jnp.sum(inv, axis=1, keepdims=True)
    value = (rows[...].astype(F32) * inv * gain[...]).astype(BF16)
    normed[...] = value
    flipped[...] = jnp.transpose(value.astype(F32)).astype(BF16)


def down_kernel(dout, w_down, keep, send):
    half = keep.shape[0]
    part = matmul(dout[...], w_down[...], NT)
    keep[...] = part[:half]
    send[...] = part[half:].astype(BF16)


def up_kernel(normed, w_gate, w_up, keep, send):
    half = keep.shape[1]
    for k, w in enumerate((w_gate, w_up)):
        part = matmul(normed[...], w[...])
        keep[k] = part[:half]
        send[k] = part[half:].astype(BF16)


def back_kernel(first, acts, flipped, dout, w_gate, w_up, w_down, *rest):
    acc, gate_grad, up_grad, down_grad = rest[-4:]

    @pl.when(pl.program_id(0) == 0)
    def _():
        acc[...] = jnp.zeros_like(acc) if first else rest[0][...]

    hidden, d_gate, d_up = acts[0], acts[1], acts[2]
    gate_grad[...] = matmul(flipped[...], d_gate).astype(BF16)
    up_grad[...] = matmul(flipped[...], d_up).astype(BF16)
    down_grad[...] = matmul(hidden, dout[...], TN).astype(BF16)
    acc[0] += matmul(hidden, w_down[...])
    acc[1] += matmul(d_gate, w_gate[...], NT) + matmul(d_up, w_up[...], NT)


def end_kernel(block, width, label, own, other, rows, dout, gain, squares, inner, ids, output, store_grad, gain_grad):
    tokens = rows.shape[0]
    pool = store_grad.shape[0]
    places = order(label[0], tokens, block)
    perm = jnp.where(places, 1.0, 0.0).astype(BF16)
    inv = lax.rsqrt(squares[...] / width + EPS)
    inv = jnp.sum(jnp.where(places, inv, 0.0), axis=1, keepdims=True)
    inner_sum = jnp.sum(jnp.where(places, inner[...], 0.0), axis=1, keepdims=True)
    row = rows[...].astype(F32)
    result = (row + (own[0] + other[0])).astype(BF16)
    output[...] = matmul(perm, result, TN).astype(BF16)
    d_normed = own[1] + other[1]
    gain_grad[...] = jnp.sum(d_normed * row * inv, axis=0, keepdims=True)
    d_rows = dout[...].astype(F32) + inv * (d_normed * gain[...]) - row * (inv * inv * (inner_sum / width))
    hit = lax.broadcasted_iota(jnp.int32, (pool, tokens), 0) == ids[...]
    target = matmul(jnp.where(hit, 1.0, 0.0).astype(BF16), perm, NT).astype(BF16)
    total = jnp.zeros(store_grad.shape, F32)
    for _ in range(3):
        piece = d_rows.astype(BF16)
        total += matmul(target, piece)
        d_rows = d_rows - piece.astype(F32)
    store_grad[...] = total.astype(BF16)


def shards(sizes, replay_store, replay_ids, excluded, norm_gain, w_gate, w_up, w_down, grad_out):
    ways = sizes["width"]
    steps = ways.bit_length() - 1
    tokens, d_here = grad_out.shape
    ff = w_down.shape[0]
    width = ways * d_here
    block = tokens // ways
    half = tokens // 2
    pool = replay_store.shape[0]
    part = ff // CHUNKS
    tile = tile_of(part)
    tiles = part // tile
    shape = jax.ShapeDtypeStruct

    index = lax.axis_index("width")
    label = sum(((index >> s) & 1) << (steps - 1 - s) for s in range(steps))
    label = jnp.reshape(label, (1,)).astype(jnp.int32)

    def swap(x, step):
        return lax.ppermute(x, "width", [(i, i ^ (1 << step)) for i in range(ways)])

    def swap_cores(x):
        n = sizes["hidden"]
        return lax.ppermute(x, "hidden", [(i, (i + 1) % n) for i in range(n)])

    def total_over_width(x):
        for step in range(steps):
            x = x + swap(x, step)
        return x

    ids = replay_ids.reshape(1, tokens)
    gain = norm_gain.reshape(1, d_here)
    rows, dout, squares = pl.pallas_call(
        functools.partial(start_kernel, block),
        out_shape=(shape((tokens, d_here), BF16), shape((tokens, d_here), BF16), shape((1, tokens), F32)),
        in_specs=[SMEM, VMEM, VMEM, VMEM, VMEM],
        out_specs=(VMEM, VMEM, VMEM),
        compiler_params=params(16),
        cost_estimate=cost(2 * tokens * pool * d_here, 2 * pool * d_here),
        name="start",
    )(label, replay_store, ids, excluded.reshape(1, -1), grad_out)

    d_tile = tile_of(ff)
    keep, send = pl.pallas_call(
        down_kernel,
        grid=(ff // d_tile,),
        out_shape=(shape((half, ff), F32), shape((half, ff), BF16)),
        in_specs=[
            pl.BlockSpec((tokens, d_here), lambda i: (0, 0)),
            pl.BlockSpec((d_tile, d_here), lambda i: (i, 0)),
        ],
        out_specs=(pl.BlockSpec((half, d_tile), lambda i: (0, i)), pl.BlockSpec((half, d_tile), lambda i: (0, i))),
        compiler_params=params(16),
        cost_estimate=cost(2 * tokens * ff * d_here, 2 * ff * d_here + 6 * half * ff),
        name="d_hidden",
    )(dout, w_down)

    squares = total_over_width(squares)
    normed, flipped = pl.pallas_call(
        functools.partial(norm_kernel, block, width),
        out_shape=(shape((tokens, d_here), BF16), shape((d_here, tokens), BF16)),
        in_specs=[SMEM, VMEM, VMEM, VMEM],
        out_specs=(VMEM, VMEM),
        compiler_params=params(16),
        cost_estimate=cost(tokens * d_here * 4, 6 * tokens * d_here),
        name="norm",
    )(label, rows, squares, gain)

    def reduce_tokens(keep, send):
        for step in range(steps):
            total = keep + swap(send, step).astype(F32)
            rest = total.shape[-2] // 2
            if step < steps - 1:
                keep, send = total[..., :rest, :], total[..., rest:, :].astype(BF16)
        return total

    def gather_tokens(x):
        for step in reversed(range(steps)):
            x = jnp.concatenate([x, swap(x, step)], axis=-2)
        return x

    d_hidden = reduce_tokens(keep, send)

    def pre(j):
        col = lambda i: (0, j * tiles + i)
        keep, send = pl.pallas_call(
            up_kernel,
            grid=(tiles,),
            out_shape=(shape((2, half, part), F32), shape((2, half, part), BF16)),
            in_specs=[
                pl.BlockSpec((tokens, d_here), lambda i: (0, 0)),
                pl.BlockSpec((d_here, tile), col),
                pl.BlockSpec((d_here, tile), col),
            ],
            out_specs=(
                pl.BlockSpec((2, half, tile), lambda i: (0, 0, i)),
                pl.BlockSpec((2, half, tile), lambda i: (0, 0, i)),
            ),
            compiler_params=params(16),
            cost_estimate=cost(4 * tokens * part * d_here, 4 * part * d_here + 12 * half * part),
            name="gate_up",
        )(normed, w_gate, w_up)
        return reduce_tokens(keep, send)

    inner = jnp.zeros((block,), F32)
    acts = []
    for j in range(CHUNKS):
        sums = pre(j)
        gate_pre, up_proj = sums[0], sums[1]
        d_part = d_hidden[:, j * part : (j + 1) * part]
        sigmoid_gate = jax.nn.sigmoid(gate_pre)
        silu = gate_pre * sigmoid_gate
        hidden = (silu * up_proj).astype(BF16)
        d_gate = (d_part * up_proj * sigmoid_gate * (1.0 + gate_pre * (1.0 - sigmoid_gate))).astype(BF16)
        d_up = (d_part * silu).astype(BF16)
        inner = inner + jnp.sum(d_gate.astype(F32) * gate_pre + d_up.astype(F32) * up_proj, axis=1)
        acts.append(gather_tokens(jnp.stack([hidden, d_gate, d_up])))

    inner = lax.dynamic_update_slice(jnp.zeros((1, tokens), F32), inner.reshape(1, block), (0, label[0] * block))
    inner = total_over_width(inner + swap_cores(inner))

    grads = None
    acc = None
    for j in range(CHUNKS):
        col = lambda i, j=j: (0, j * tiles + i)
        row = lambda i, j=j: (j * tiles + i, 0)
        whole = lambda i: (0, 0)
        acc_spec = pl.BlockSpec((2, tokens, d_here), lambda i: (0, 0, 0))
        first = j == 0
        extra = [] if first else [acc, *grads]
        acc, *grads = pl.pallas_call(
            functools.partial(back_kernel, first),
            grid=(tiles,),
            out_shape=(
                shape((2, tokens, d_here), F32),
                shape((d_here, ff), BF16),
                shape((d_here, ff), BF16),
                shape((ff, d_here), BF16),
            ),
            in_specs=[
                pl.BlockSpec((3, tokens, tile), lambda i: (0, 0, i)),
                pl.BlockSpec((d_here, tokens), whole),
                pl.BlockSpec((tokens, d_here), whole),
                pl.BlockSpec((d_here, tile), col),
                pl.BlockSpec((d_here, tile), col),
                pl.BlockSpec((tile, d_here), row),
            ]
            + ([] if first else [acc_spec, ANY, ANY, ANY]),
            out_specs=(
                acc_spec,
                pl.BlockSpec((d_here, tile), col),
                pl.BlockSpec((d_here, tile), col),
                pl.BlockSpec((tile, d_here), row),
            ),
            input_output_aliases={} if first else {7: 1, 8: 2, 9: 3},
            compiler_params=params(24),
            cost_estimate=cost(12 * tokens * part * d_here, 12 * part * d_here),
            name="back",
        )(acts[j], flipped, dout, w_gate, w_up, w_down, *extra)

    other = swap_cores(acc)
    output, store_grad, gain_grad = pl.pallas_call(
        functools.partial(end_kernel, block, width),
        out_shape=(shape((tokens, d_here), BF16), shape((pool, d_here), BF16), shape((1, d_here), F32)),
        in_specs=[SMEM] + [VMEM] * 8,
        out_specs=(VMEM, VMEM, VMEM),
        compiler_params=params(24),
        cost_estimate=cost(2 * tokens * pool * d_here, 16 * tokens * d_here),
        name="end",
    )(label, acc, other, rows, dout, gain, squares, inner, ids)
    return (output, store_grad, gain_grad.reshape(d_here), *grads)


def solution(mesh):
    return jax.shard_map(
        functools.partial(shards, dict(mesh.shape)),
        mesh=mesh,
        in_specs=(
            P("groups", "width"),
            P("groups"),
            P("groups"),
            P("width"),
            P("width", "hidden"),
            P("width", "hidden"),
            P("hidden", "width"),
            P("groups", "width"),
        ),
        out_specs=(
            P("groups", "width"),
            P("groups", "width"),
            P(("groups", "width")),
            P(("groups", "width"), "hidden"),
            P(("groups", "width"), "hidden"),
            P(("groups", "hidden"), "width"),
        ),
        check_vma=False,
    )
```

time: 485 us -> 275 us (0.57)
  waiting for transfers between devices: 332 us -> 134 us
  matrix products: 85 us -> 0 us
  Pallas kernels: 0 us -> 67.5 us
  starting transfers between devices: 0.46 us -> 43.8 us
  blocking collectives: 43.2 us -> 0 us
  local copies, waits for them, and re-layouts: 0.9 us -> 25.1 us
  between operations: 14.2 us -> 1.12 us
  other arithmetic: 9.61 us -> 2.29 us
    reduce_scatter x3 -> x0, waiting for transfers between devices: 209 us -> none  [the longest x1 84.7 us: shards(): lax.psum_scatter(up_part, 'width', scatter_dimension=0, tiled=True)]
    ppermute x0 -> x35, waiting for transfers between devices: none -> 134 us  [the longest x33 132 us: swap(): return lax.ppermute(x, 'width', [(i, i ^ 1 << step) for i in range(ways)])]
    all_gather x3 -> x0, waiting for transfers between devices: 121 us -> none  [the longest x1 44.8 us: shards(): lax.all_gather(swiglu(gate_pre, up_proj), 'width', axis=0, tiled=True)]
    dot_general x9 -> x0, matrix products: 85 us -> none  [the longest x1 12 us: shards(): lax.dot_general(d_output, w_down, contract_last, preferred_element_type=j...]
    pallas_call x0 -> x12, Pallas kernels: none -> 67.5 us  [the longest x4 42.7 us: shards(): pl.pallas_call(functools.partial(back_kernel, first), grid=(tiles,), out_...]
    ppermute x0 -> x35, starting transfers between devices: none -> 43.8 us  [the longest x33 43.3 us: swap(): return lax.ppermute(x, 'width', [(i, i ^ 1 << step) for i in range(ways)])]
    psum x2 -> x0, blocking collectives: 43.2 us -> none  [the longest x1 23.7 us: shards(): lax.psum(jnp.sum(row_float * row_float, axis=1, keepdims=True), 'width')]
    unnamed x16 -> x30, local copies, waits for them, and re-layouts: 0.04 us -> 24.7 us
  transfers between devices with their start and end apart: 7 -> 35, of which waited for: 6 -> 26; matrix products, arithmetic and copies ran while one was open for 13% -> 1% of each run, Pallas kernels for 0% -> 19%
where the time goes in v1:
time: 275 us; the launch traced here: 274 us
  waiting for transfers between devices  134 us (49%)
  Pallas kernels  67.5 us (25%)
  starting transfers between devices  43.8 us (16%)
  local copies, waits for them, and re-layouts  25.1 us (9%)
    ppermute x33, waiting for transfers between devices, swap(): return lax.ppermute(x, 'width', [(i, i ^ 1 << step) for i in range(ways)])  132 us
    ppermute x33, starting transfers between devices, swap(): return lax.ppermute(x, 'width', [(i, i ^ 1 << step) for i in range(ways)])  43.3 us
    pallas_call x4, Pallas kernels, shards(): pl.pallas_call(functools.partial(back_kernel, first), grid=(tiles,), out_...  42.7 us
    unnamed x30, local copies, waits for them, and re-layouts  24.7 us
    pallas_call x4, Pallas kernels, pre(): pl.pallas_call(up_kernel, grid=(tiles,), out_shape=(shape((2, half, part)...  13.4 us
    pallas_call x1, Pallas kernels, shards(): pl.pallas_call(down_kernel, grid=(ff // d_tile,), out_shape=(shape((half,...  8.89 us
  transfers between devices with their start and end apart: 35, of which 26 were waited for; matrix products, arithmetic and copies ran while one was open for 1% of the time, Pallas kernels for 19%

profile of v1, /device:TPU:0, one launch (start us, length us, event | category | flops | bytes accessed | tf_op | source)
XLA Modules:
  0.0 273.9 jit_solution(2211017835649525289)
XLA Ops:
  4.4 3.0 %collective-permute-start = (f32[1,128]{1,0:T(1,128)S(1)}, f32[1,128]{1,0:T(1,128)S(1)}, u32[]{:S(2)}, u32[]{:S(2)}) collective-permute-start(f32[1,128]{1,0:T(1,128)S(1)} %get-tuple-element.41), channel_id=1, source_target_pairs={{0,2},{2,0},{4,6},{6,4},{8,10},{10,8},{12,14},{14,12},{1,3},{3,1},... | collective-permute-start | bytes 1544 | tf_op jit(solution)/shard_map/ppermute | solution.py:145
  12.6 3.0 %collective-permute-start.2 = (f32[1,128]{1,0:T(1,128)S(1)}, f32[1,128]{1,0:T(1,128)S(1)}, u32[]{:S(2)}, u32[]{:S(2)}) collective-permute-start(f32[1,128]{1,0:T(1,128)S(1)} %add.162), channel_id=1, source_target_pairs={{0,8},{2,10},{4,12},{6,14},{8,0},{10,2},{12,4},{14,6},{1,9},{3,11}... | collective-permute-start | bytes 1544 | tf_op jit(solution)/shard_map/ppermute | solution.py:145
  18.1 5.2 %copy-done = bf16[1024,7168]{1,0:T(8,128)(2,1)S(1)} copy-done((bf16[1024,7168]{1,0:T(8,128)(2,1)S(1)}, bf16[1024,7168]{1,0:T(8,128)(2,1)}, u32[]{:S(2)}) %copy-start) | copy-done | bytes 14680088
  23.3 5.2 %copy-done.1 = bf16[1024,7168]{1,0:T(8,128)(2,1)S(1)} copy-done((bf16[1024,7168]{1,0:T(8,128)(2,1)S(1)}, bf16[1024,7168]{1,0:T(8,128)(2,1)}, u32[]{:S(2)}) %copy-start.1) | copy-done | bytes 14680088
  28.4 3.4 %gate_up.4 = (f32[2,64,1792]{2,1,0:T(8,128)S(1)}, bf16[2,64,1792]{2,1,0:T(8,128)(2,1)S(1)}) custom-call(bf16[128,1024]{1,0:T(8,128)(2,1)S(1)} %get-tuple-element.42.normed, bf16[1024,7168]{1,0:T(8,128)(2,1)S(1)} %copy-done, bf16[1024,7168]{1,0:T(8,128)(2,1)S(1)} %copy-done.1), custom_call_target="tpu_custom_call" | custom-call | flops 939524096 | bytes 8716288 | tf_op jit(solution)/shard_map/gate_up/pallas_call | solution.py:211
  33.7 5.2 %copy-done.3 = bf16[7168,1024]{1,0:T(8,128)(2,1)S(1)} copy-done((bf16[7168,1024]{1,0:T(8,128)(2,1)S(1)}, bf16[7168,1024]{1,0:T(8,128)(2,1)}, u32[]{:S(2)}) %copy-start.3) | copy-done | bytes 14680088
  38.9 8.9 %d_hidden.1 = (f32[64,7168]{1,0:T(8,128)S(1)}, bf16[64,7168]{1,0:T(8,128)(2,1)S(1)}) custom-call(bf16[128,1024]{1,0:T(8,128)(2,1)S(1)} %get-tuple-element.45.dout, bf16[7168,1024]{1,0:T(8,128)(2,1)S(1)} %copy-done.3), custom_call_target="tpu_custom_call" | custom-call | flops 1879048192 | bytes 17432576 | tf_op jit(solution)/shard_map/d_hidden/pallas_call | solution.py:169
  48.1 5.2 %copy-done.2 = bf16[1024,7168]{1,0:T(8,128)(2,1)S(1)} copy-done((bf16[1024,7168]{1,0:T(8,128)(2,1)S(1)}, bf16[1024,7168]{1,0:T(8,128)(2,1)}, u32[]{:S(2)}) %copy-start.2) | copy-done | bytes 14680088
  53.3 3.4 %gate_up.5 = (f32[2,64,1792]{2,1,0:T(8,128)S(1)}, bf16[2,64,1792]{2,1,0:T(8,128)(2,1)S(1)}) custom-call(bf16[128,1024]{1,0:T(8,128)(2,1)S(1)} %get-tuple-element.42.normed, bf16[1024,7168]{1,0:T(8,128)(2,1)S(1)} %bitcast.180, bf16[1024,7168]{1,0:T(8,128)(2,1)S(1)} %copy-done.2), custom_call_target="tpu_custom_call" | custom-call | flops 939524096 | bytes 8716288 | tf_op jit(solution)/shard_map/gate_up/pallas_call | solution.py:211
  58.5 3.4 %gate_up.6 = (f32[2,64,1792]{2,1,0:T(8,128)S(1)}, bf16[2,64,1792]{2,1,0:T(8,128)(2,1)S(1)}) custom-call(bf16[128,1024]{1,0:T(8,128)(2,1)S(1)} %get-tuple-element.42.normed, bf16[1024,7168]{1,0:T(8,128)(2,1)S(1)} %bitcast.180, bf16[1024,7168]{1,0:T(8,128)(2,1)S(1)} %copy-done.2), custom_call_target="tpu_custom_call" | custom-call | flops 939524096 | bytes 8716288 | tf_op jit(solution)/shard_map/gate_up/pallas_call | solution.py:211
  62.1 3.3 %gate_up.7 = (f32[2,64,1792]{2,1,0:T(8,128)S(1)}, bf16[2,64,1792]{2,1,0:T(8,128)(2,1)S(1)}) custom-call(bf16[128,1024]{1,0:T(8,128)(2,1)S(1)} %get-tuple-element.42.normed, bf16[1024,7168]{1,0:T(8,128)(2,1)S(1)} %bitcast.180, bf16[1024,7168]{1,0:T(8,128)(2,1)S(1)} %copy-done.2), custom_call_target="tpu_custom_call" | custom-call | flops 939524096 | bytes 8716288 | tf_op jit(solution)/shard_map/gate_up/pallas_call | solution.py:211
  69.1 11.9 %collective-permute-done.12 = bf16[2,64,1792]{2,1,0:T(8,128)(2,1)S(1)} collective-permute-done((bf16[2,64,1792]{2,1,0:T(8,128)(2,1)S(1)}, bf16[2,64,1792]{2,1,0:T(8,128)(2,1)S(1)}, u32[]{:S(2)}, u32[]{:S(2)}) %collective-permute-start.12) | collective-permute-done | bytes 458784 | tf_op jit(solution)/shard_map/ppermute | solution.py:145
  82.7 8.1 %collective-permute-done.18 = bf16[2,64,1792]{2,1,0:T(8,128)(2,1)S(1)} collective-permute-done((bf16[2,64,1792]{2,1,0:T(8,128)(2,1)S(1)}, bf16[2,64,1792]{2,1,0:T(8,128)(2,1)S(1)}, u32[]{:S(2)}, u32[]{:S(2)}) %collective-permute-start.18) | collective-permute-done | bytes 458784 | tf_op jit(solution)/shard_map/ppermute | solution.py:145
  92.5 3.2 %collective-permute-done.24 = bf16[2,64,1792]{2,1,0:T(8,128)(2,1)S(1)} collective-permute-done((bf16[2,64,1792]{2,1,0:T(8,128)(2,1)S(1)}, bf16[2,64,1792]{2,1,0:T(8,128)(2,1)S(1)}, u32[]{:S(2)}, u32[]{:S(2)}) %collective-permute-start.24) | collective-permute-done | bytes 458784 | tf_op jit(solution)/shard_map/ppermute | solution.py:145
  108.2 6.3 %collective-permute-done.14 = bf16[2,16,1792]{2,1,0:T(8,128)(2,1)S(1)} collective-permute-done((bf16[2,16,1792]{2,1,0:T(8,128)(2,1)S(1)}, bf16[2,16,1792]{2,1,0:T(8,128)(2,1)S(1)}, u32[]{:S(2)}, u32[]{:S(2)}) %collective-permute-start.14) | collective-permute-done | bytes 114720 | tf_op jit(solution)/shard_map/ppermute | solution.py:145
  117.4 9.9 %collective-permute-done.7 = bf16[32,7168]{1,0:T(8,128)(2,1)S(1)} collective-permute-done((bf16[32,7168]{1,0:T(8,128)(2,1)S(1)}, bf16[32,7168]{1,0:T(8,128)(2,1)S(1)}, u32[]{:S(2)}, u32[]{:S(2)}) %collective-permute-start.7) | collective-permute-done | bytes 458784 | tf_op jit(solution)/shard_map/ppermute | solution.py:145
  128.8 8.7 %collective-permute-done.8 = bf16[16,7168]{1,0:T(8,128)(2,1)S(1)} collective-permute-done((bf16[16,7168]{1,0:T(8,128)(2,1)S(1)}, bf16[16,7168]{1,0:T(8,128)(2,1)S(1)}, u32[]{:S(2)}, u32[]{:S(2)}) %collective-permute-start.8) | collective-permute-done | bytes 229408 | tf_op jit(solution)/shard_map/ppermute | solution.py:145
  144.2 15.2 %collective-permute-done.27 = bf16[3,16,1792]{2,1,0:T(8,128)(2,1)S(1)} collective-permute-done((bf16[3,16,1792]{2,1,0:T(8,128)(2,1)S(1)}, bf16[3,16,1792]{2,1,0:T(8,128)(2,1)S(1)}, u32[]{:S(2)}, u32[]{:S(2)}) %collective-permute-start.27) | collective-permute-done | bytes 172064 | tf_op jit(solution)/shard_map/ppermute | solution.py:145
  159.5 3.7 %collective-permute-done.21 = bf16[3,16,1792]{2,1,0:T(8,128)(2,1)S(1)} collective-permute-done((bf16[3,16,1792]{2,1,0:T(8,128)(2,1)S(1)}, bf16[3,16,1792]{2,1,0:T(8,128)(2,1)S(1)}, u32[]{:S(2)}, u32[]{:S(2)}) %collective-permute-start.21) | collective-permute-done | bytes 172064 | tf_op jit(solution)/shard_map/ppermute | solution.py:145
  163.2 3.6 %collective-permute-done.15 = bf16[3,16,1792]{2,1,0:T(8,128)(2,1)S(1)} collective-permute-done((bf16[3,16,1792]{2,1,0:T(8,128)(2,1)S(1)}, bf16[3,16,1792]{2,1,0:T(8,128)(2,1)S(1)}, u32[]{:S(2)}, u32[]{:S(2)}) %collective-permute-start.15) | collective-permute-done | bytes 172064 | tf_op jit(solution)/shard_map/ppermute | solution.py:145
  169.6 7.3 %collective-permute-done.28 = bf16[3,32,1792]{2,1,0:T(8,128)(2,1)S(1)} collective-permute-done((bf16[3,32,1792]{2,1,0:T(8,128)(2,1)S(1)}, bf16[3,32,1792]{2,1,0:T(8,128)(2,1)S(1)}, u32[]{:S(2)}, u32[]{:S(2)}) %collective-permute-start.28) | collective-permute-done | bytes 344096 | tf_op jit(solution)/shard_map/ppermute | solution.py:145
  178.3 5.9 %collective-permute-done.22 = bf16[3,32,1792]{2,1,0:T(8,128)(2,1)S(1)} collective-permute-done((bf16[3,32,1792]{2,1,0:T(8,128)(2,1)S(1)}, bf16[3,32,1792]{2,1,0:T(8,128)(2,1)S(1)}, u32[]{:S(2)}, u32[]{:S(2)}) %collective-permute-start.22) | collective-permute-done | bytes 344096 | tf_op jit(solution)/shard_map/ppermute | solution.py:145
  185.7 5.9 %collective-permute-done.16 = bf16[3,32,1792]{2,1,0:T(8,128)(2,1)S(1)} collective-permute-done((bf16[3,32,1792]{2,1,0:T(8,128)(2,1)S(1)}, bf16[3,32,1792]{2,1,0:T(8,128)(2,1)S(1)}, u32[]{:S(2)}, u32[]{:S(2)}) %collective-permute-start.16) | collective-permute-done | bytes 344096 | tf_op jit(solution)/shard_map/ppermute | solution.py:145
  193.1 5.8 %collective-permute-done.10 = bf16[3,32,1792]{2,1,0:T(8,128)(2,1)S(1)} collective-permute-done((bf16[3,32,1792]{2,1,0:T(8,128)(2,1)S(1)}, bf16[3,32,1792]{2,1,0:T(8,128)(2,1)S(1)}, u32[]{:S(2)}, u32[]{:S(2)}) %collective-permute-start.10) | collective-permute-done | bytes 344096 | tf_op jit(solution)/shard_map/ppermute | solution.py:145
  200.5 9.6 %collective-permute-done.23 = bf16[3,64,1792]{2,1,0:T(8,128)(2,1)S(1)} collective-permute-done((bf16[3,64,1792]{2,1,0:T(8,128)(2,1)S(1)}, bf16[3,64,1792]{2,1,0:T(8,128)(2,1)S(1)}, u32[]{:S(2)}, u32[]{:S(2)}) %collective-permute-start.23) | collective-permute-done | bytes 688160 | tf_op jit(solution)/shard_map/ppermute | solution.py:145
  210.1 9.9 %back.4 = (f32[2,128,1024]{2,1,0:T(8,128)S(1)}, bf16[1024,7168]{1,0:T(8,128)(2,1)}, bf16[1024,7168]{1,0:T(8,128)(2,1)}, bf16[7168,1024]{1,0:T(8,128)(2,1)}) custom-call(bf16[3,128,1792]{2,1,0:T(8,128)(2,1)S(1)} %pad_maximum_fusion.3.acts, bf16[1024,128]{1,0:T(8,128)(2,1)S(1)} %get-tuple-element.48.flipped, bf16[128,1024]{1,0:T(8,128)(2,1)S(1)} %get-tuple-element.45.dout, ...), custom_call_target="tpu_custom_call" | custom-call | flops 2818572288 | bytes 22020096 | tf_op jit(solution)/shard_map/back/pallas_call | solution.py:256
  220.0 4.7 %collective-permute-done.17 = bf16[3,64,1792]{2,1,0:T(8,128)(2,1)S(1)} collective-permute-done((bf16[3,64,1792]{2,1,0:T(8,128)(2,1)S(1)}, bf16[3,64,1792]{2,1,0:T(8,128)(2,1)S(1)}, u32[]{:S(2)}, u32[]{:S(2)}) %collective-permute-start.17) | collective-permute-done | bytes 688160 | tf_op jit(solution)/shard_map/ppermute | solution.py:145
  224.9 10.9 %back.5 = (f32[2,128,1024]{2,1,0:T(8,128)S(1)}, bf16[1024,7168]{1,0:T(8,128)(2,1)}, bf16[1024,7168]{1,0:T(8,128)(2,1)}, bf16[7168,1024]{1,0:T(8,128)(2,1)}) custom-call(bf16[3,128,1792]{2,1,0:T(8,128)(2,1)S(1)} %pad_maximum_fusion.2.acts, ...), custom_call_target="tpu_custom_call", output_to_operand_aliasing={{1}: (7, {}), {2}: (8, {}), {3}: (9, {})} | custom-call | flops 2818572288 | bytes 22020096 | tf_op jit(solution)/shard_map/back/pallas_call | solution.py:256
  235.8 10.9 %back.6 = (f32[2,128,1024]{2,1,0:T(8,128)S(1)}, bf16[1024,7168]{1,0:T(8,128)(2,1)}, bf16[1024,7168]{1,0:T(8,128)(2,1)}, bf16[7168,1024]{1,0:T(8,128)(2,1)}) custom-call(bf16[3,128,1792]{2,1,0:T(8,128)(2,1)S(1)} %pad_maximum_fusion.1.acts, ...), custom_call_target="tpu_custom_call", output_to_operand_aliasing={{1}: (7, {}), {2}: (8, {}), {3}: (9, {})} | custom-call | flops 2818572288 | bytes 22020096 | tf_op jit(solution)/shard_map/back/pallas_call | solution.py:256
  246.8 10.9 %back.7 = (f32[2,128,1024]{2,1,0:T(8,128)S(1)}, bf16[1024,7168]{1,0:T(8,128)(2,1)}, bf16[1024,7168]{1,0:T(8,128)(2,1)}, bf16[7168,1024]{1,0:T(8,128)(2,1)}) custom-call(bf16[3,128,1792]{2,1,0:T(8,128)(2,1)S(1)} %pad_maximum_fusion.acts, bf16[1024,128]{1,0:T(8,128)(2,1)S(1)} %get-tuple-element.48.flipped, ...), custom_call_target="tpu_custom_call", output_to_operand_aliasing={{1}: (7, {}), {2}: (8, {}), {3}: (9, {})} | custom-call | flops 2818572288 | bytes 22020096 | tf_op jit(solution)/shard_map/back/pallas_call | solution.py:256
  264.2 3.5 %collective-permute-done.33 = f32[1,128]{1,0:T(1,128)S(1)} collective-permute-done((f32[1,128]{1,0:T(1,128)S(1)}, f32[1,128]{1,0:T(1,128)S(1)}, u32[]{:S(2)}, u32[]{:S(2)}) %collective-permute-start.33) | collective-permute-done | bytes 544 | tf_op jit(solution)/shard_map/ppermute | solution.py:145
  268.0 4.2 %collective-permute-done.34 = f32[1,128]{1,0:T(1,128)S(1)} collective-permute-done((f32[1,128]{1,0:T(1,128)S(1)}, f32[1,128]{1,0:T(1,128)S(1)}, u32[]{:S(2)}, u32[]{:S(2)}) %collective-permute-start.34) | collective-permute-done | bytes 544 | tf_op jit(solution)/shard_map/ppermute | solution.py:145
  (138 shorter events, 63.9 us)
Async XLA Ops:
  4.4 4.5 %collective-permute-start = (f32[1,128]{1,0:T(1,128)S(1)}, f32[1,128]{1,0:T(1,128)S(1)}, u32[]{:S(2)}, u32[]{:S(2)}) collective-permute-start(f32[1,128]{1,0:T(1,128)S(1)} %get-tuple-element.41), channel_id=1, source_target_pairs={{0,2},{2,0},{4,6},{6,4},{8,10},{10,8},{12,14},{14,12},{1,3},{3,1},... | collective-permute-start | bytes 1544 | tf_op jit(solution)/shard_map/ppermute | solution.py:145
  9.0 3.6 %collective-permute-start.1 = (f32[1,128]{1,0:T(1,128)S(1)}, f32[1,128]{1,0:T(1,128)S(1)}, u32[]{:S(2)}, u32[]{:S(2)}) collective-permute-start(f32[1,128]{1,0:T(1,128)S(1)} %add.161), channel_id=1, source_target_pairs={{0,4},{2,6},{4,0},{6,2},{8,12},{10,14},{12,8},{14,10},{1,5},{3,7},... | collective-permute-start | bytes 1544 | tf_op jit(solution)/shard_map/ppermute | solution.py:145
  12.6 4.6 %collective-permute-start.2 = (f32[1,128]{1,0:T(1,128)S(1)}, f32[1,128]{1,0:T(1,128)S(1)}, u32[]{:S(2)}, u32[]{:S(2)}) collective-permute-start(f32[1,128]{1,0:T(1,128)S(1)} %add.162), channel_id=1, source_target_pairs={{0,8},{2,10},{4,12},{6,14},{8,0},{10,2},{12,4},{14,6},{1,9},{3,11}... | collective-permute-start | bytes 1544 | tf_op jit(solution)/shard_map/ppermute | solution.py:145
  31.8 35.5 %collective-permute-start.3 = (bf16[2,64,1792]{2,1,0:T(8,128)(2,1)S(1)}, bf16[2,64,1792]{2,1,0:T(8,128)(2,1)S(1)}, u32[]{:S(2)}, u32[]{:S(2)}) collective-permute-start(bf16[2,64,1792]{2,1,0:T(8,128)(2,1)S(1)} %get-tuple-element.44), channel_id=1, source_target_pairs={{0,2},{2,0},{4,6},{6,4},{8,10},{10,8},{12,14},{14,12},{1,3},{3,1},... | collective-permute-start | bytes 1376264 | tf_op jit(solution)/shard_map/ppermute | solution.py:145
  47.8 69.2 %collective-permute-start.6 = (bf16[64,7168]{1,0:T(8,128)(2,1)S(1)}, bf16[64,7168]{1,0:T(8,128)(2,1)S(1)}, u32[]{:S(2)}, u32[]{:S(2)}) collective-permute-start(bf16[64,7168]{1,0:T(8,128)(2,1)S(1)} %get-tuple-element.47), channel_id=1, source_target_pairs={{0,2},{2,0},{4,6},{6,4},{8,10},{10,8},{12,14},{14,12},{1,3},{3,1},... | collective-permute-start | bytes 2752520 | tf_op jit(solution)/shard_map/ppermute | solution.py:145
  56.6 24.3 %collective-permute-start.12 = (bf16[2,64,1792]{2,1,0:T(8,128)(2,1)S(1)}, bf16[2,64,1792]{2,1,0:T(8,128)(2,1)S(1)}, u32[]{:S(2)}, u32[]{:S(2)}) collective-permute-start(bf16[2,64,1792]{2,1,0:T(8,128)(2,1)S(1)} %get-tuple-element.50), channel_id=1, source_target_pairs={{0,2},{2,0},{4,6},{6,4},{8,10},{10,8},{12,14},{14,12},{1,3},{3,1},... | collective-permute-start | bytes 1376264 | tf_op jit(solution)/shard_map/ppermute | solution.py:145
  61.9 28.9 %collective-permute-start.18 = (bf16[2,64,1792]{2,1,0:T(8,128)(2,1)S(1)}, bf16[2,64,1792]{2,1,0:T(8,128)(2,1)S(1)}, u32[]{:S(2)}, u32[]{:S(2)}) collective-permute-start(bf16[2,64,1792]{2,1,0:T(8,128)(2,1)S(1)} %get-tuple-element.52), channel_id=1, source_target_pairs={{0,2},{2,0},{4,6},{6,4},{8,10},{10,8},{12,14},{14,12},{1,3},{3,1},... | collective-permute-start | bytes 1376264 | tf_op jit(solution)/shard_map/ppermute | solution.py:145
  65.5 30.2 %collective-permute-start.24 = (bf16[2,64,1792]{2,1,0:T(8,128)(2,1)S(1)}, bf16[2,64,1792]{2,1,0:T(8,128)(2,1)S(1)}, u32[]{:S(2)}, u32[]{:S(2)}) collective-permute-start(bf16[2,64,1792]{2,1,0:T(8,128)(2,1)S(1)} %get-tuple-element.54), channel_id=1, source_target_pairs={{0,2},{2,0},{4,6},{6,4},{8,10},{10,8},{12,14},{14,12},{1,3},{3,1},... | collective-permute-start | bytes 1376264 | tf_op jit(solution)/shard_map/ppermute | solution.py:145
  67.5 30.0 %collective-permute-start.4 = (bf16[2,32,1792]{2,1,0:T(8,128)(2,1)S(1)}, bf16[2,32,1792]{2,1,0:T(8,128)(2,1)S(1)}, u32[]{:S(2)}, u32[]{:S(2)}) collective-permute-start(bf16[2,32,1792]{2,1,0:T(8,128)(2,1)S(1)} %slice.231), channel_id=1, source_target_pairs={{0,4},{2,6},{4,0},{6,2},{8,12},{10,14},{12,8},{14,10},{1,5},{3,7},... | collective-permute-start | bytes 688136 | tf_op jit(solution)/shard_map/ppermute | solution.py:145
  81.1 19.1 %collective-permute-start.13 = (bf16[2,32,1792]{2,1,0:T(8,128)(2,1)S(1)}, bf16[2,32,1792]{2,1,0:T(8,128)(2,1)S(1)}, u32[]{:S(2)}, u32[]{:S(2)}) collective-permute-start(bf16[2,32,1792]{2,1,0:T(8,128)(2,1)S(1)} %slice.229), channel_id=1, source_target_pairs={{0,4},{2,6},{4,0},{6,2},{8,12},{10,14},{12,8},{14,10},{1,5},{3,7},... | collective-permute-start | bytes 688136 | tf_op jit(solution)/shard_map/ppermute | solution.py:145
  90.9 11.5 %collective-permute-start.19 = (bf16[2,32,1792]{2,1,0:T(8,128)(2,1)S(1)}, bf16[2,32,1792]{2,1,0:T(8,128)(2,1)S(1)}, u32[]{:S(2)}, u32[]{:S(2)}) collective-permute-start(bf16[2,32,1792]{2,1,0:T(8,128)(2,1)S(1)} %slice.228), channel_id=1, source_target_pairs={{0,4},{2,6},{4,0},{6,2},{8,12},{10,14},{12,8},{14,10},{1,5},{3,7},... | collective-permute-start | bytes 688136 | tf_op jit(solution)/shard_map/ppermute | solution.py:145
  95.8 11.1 %collective-permute-start.25 = (bf16[2,32,1792]{2,1,0:T(8,128)(2,1)S(1)}, bf16[2,32,1792]{2,1,0:T(8,128)(2,1)S(1)}, u32[]{:S(2)}, u32[]{:S(2)}) collective-permute-start(bf16[2,32,1792]{2,1,0:T(8,128)(2,1)S(1)} %slice.227), channel_id=1, source_target_pairs={{0,4},{2,6},{4,0},{6,2},{8,12},{10,14},{12,8},{14,10},{1,5},{3,7},... | collective-permute-start | bytes 688136 | tf_op jit(solution)/shard_map/ppermute | solution.py:145
  97.5 10.6 %collective-permute-start.5 = (bf16[2,16,1792]{2,1,0:T(8,128)(2,1)S(1)}, bf16[2,16,1792]{2,1,0:T(8,128)(2,1)S(1)}, u32[]{:S(2)}, u32[]{:S(2)}) collective-permute-start(bf16[2,16,1792]{2,1,0:T(8,128)(2,1)S(1)} %slice.235), channel_id=1, source_target_pairs={{0,8},{2,10},{4,12},{6,14},{8,0},{10,2},{12,4},{14,6},{1,9},{3,11}... | collective-permute-start | bytes 344072 | tf_op jit(solution)/shard_map/ppermute | solution.py:145
  100.2 14.2 %collective-permute-start.14 = (bf16[2,16,1792]{2,1,0:T(8,128)(2,1)S(1)}, bf16[2,16,1792]{2,1,0:T(8,128)(2,1)S(1)}, u32[]{:S(2)}, u32[]{:S(2)}) collective-permute-start(bf16[2,16,1792]{2,1,0:T(8,128)(2,1)S(1)} %slice.234), channel_id=1, source_target_pairs={{0,8},{2,10},{4,12},{6,14},{8,0},{10,2},{12,4},{14,6},{1,9},{3,11}... | collective-permute-start | bytes 344072 | tf_op jit(solution)/shard_map/ppermute | solution.py:145
  102.4 14.6 %collective-permute-start.20 = (bf16[2,16,1792]{2,1,0:T(8,128)(2,1)S(1)}, bf16[2,16,1792]{2,1,0:T(8,128)(2,1)S(1)}, u32[]{:S(2)}, u32[]{:S(2)}) collective-permute-start(bf16[2,16,1792]{2,1,0:T(8,128)(2,1)S(1)} %slice.233), channel_id=1, source_target_pairs={{0,8},{2,10},{4,12},{6,14},{8,0},{10,2},{12,4},{14,6},{1,9},{3,11}... | collective-permute-start | bytes 344072 | tf_op jit(solution)/shard_map/ppermute | solution.py:145
  106.9 10.0 %collective-permute-start.26 = (bf16[2,16,1792]{2,1,0:T(8,128)(2,1)S(1)}, bf16[2,16,1792]{2,1,0:T(8,128)(2,1)S(1)}, u32[]{:S(2)}, u32[]{:S(2)}) collective-permute-start(bf16[2,16,1792]{2,1,0:T(8,128)(2,1)S(1)} %slice.232), channel_id=1, source_target_pairs={{0,8},{2,10},{4,12},{6,14},{8,0},{10,2},{12,4},{14,6},{1,9},{3,11}... | collective-permute-start | bytes 344072 | tf_op jit(solution)/shard_map/ppermute | solution.py:145
  117.2 10.1 %collective-permute-start.7 = (bf16[32,7168]{1,0:T(8,128)(2,1)S(1)}, bf16[32,7168]{1,0:T(8,128)(2,1)S(1)}, u32[]{:S(2)}, u32[]{:S(2)}) collective-permute-start(bf16[32,7168]{1,0:T(8,128)(2,1)S(1)} %slice.226), channel_id=1, source_target_pairs={{0,4},{2,6},{4,0},{6,2},{8,12},{10,14},{12,8},{14,10},{1,5},{3,7},... | collective-permute-start | bytes 1376264 | tf_op jit(solution)/shard_map/ppermute | solution.py:145
  127.4 10.0 %collective-permute-start.8 = (bf16[16,7168]{1,0:T(8,128)(2,1)S(1)}, bf16[16,7168]{1,0:T(8,128)(2,1)S(1)}, u32[]{:S(2)}, u32[]{:S(2)}) collective-permute-start(bf16[16,7168]{1,0:T(8,128)(2,1)S(1)} %slice.230), channel_id=1, source_target_pairs={{0,8},{2,10},{4,12},{6,14},{8,0},{10,2},{12,4},{14,6},{1,9},{3,11}... | collective-permute-start | bytes 688136 | tf_op jit(solution)/shard_map/ppermute | solution.py:145
  138.0 21.4 %collective-permute-start.27 = (bf16[3,16,1792]{2,1,0:T(8,128)(2,1)S(1)}, bf16[3,16,1792]{2,1,0:T(8,128)(2,1)S(1)}, u32[]{:S(2)}, u32[]{:S(2)}) collective-permute-start(bf16[3,16,1792]{2,1,0:T(8,128)(2,1)S(1)} %pad_maximum_fusion.15), channel_id=1, source_target_pairs={{0,8},{2,10},{4,12},{6,14},{8,0},{10,2},{12,4},{14,6},{1,9},{3,11}... | collective-permute-start | bytes 516104 | tf_op jit(solution)/shard_map/ppermute | solution.py:145
  138.1 25.1 %collective-permute-start.21 = (bf16[3,16,1792]{2,1,0:T(8,128)(2,1)S(1)}, bf16[3,16,1792]{2,1,0:T(8,128)(2,1)S(1)}, u32[]{:S(2)}, u32[]{:S(2)}) collective-permute-start(bf16[3,16,1792]{2,1,0:T(8,128)(2,1)S(1)} %pad_maximum_fusion.14), channel_id=1, source_target_pairs={{0,8},{2,10},{4,12},{6,14},{8,0},{10,2},{12,4},{14,6},{1,9},{3,11}... | collective-permute-start | bytes 516104 | tf_op jit(solution)/shard_map/ppermute | solution.py:145
  141.1 25.7 %collective-permute-start.15 = (bf16[3,16,1792]{2,1,0:T(8,128)(2,1)S(1)}, bf16[3,16,1792]{2,1,0:T(8,128)(2,1)S(1)}, u32[]{:S(2)}, u32[]{:S(2)}) collective-permute-start(bf16[3,16,1792]{2,1,0:T(8,128)(2,1)S(1)} %pad_maximum_fusion.13), channel_id=1, source_target_pairs={{0,8},{2,10},{4,12},{6,14},{8,0},{10,2},{12,4},{14,6},{1,9},{3,11}... | collective-permute-start | bytes 516104 | tf_op jit(solution)/shard_map/ppermute | solution.py:145
  141.2 28.3 %collective-permute-start.9 = (bf16[3,16,1792]{2,1,0:T(8,128)(2,1)S(1)}, bf16[3,16,1792]{2,1,0:T(8,128)(2,1)S(1)}, u32[]{:S(2)}, u32[]{:S(2)}) collective-permute-start(bf16[3,16,1792]{2,1,0:T(8,128)(2,1)S(1)} %pad_maximum_fusion.12), channel_id=1, source_target_pairs={{0,8},{2,10},{4,12},{6,14},{8,0},{10,2},{12,4},{14,6},{1,9},{3,11}... | collective-permute-start | bytes 516104 | tf_op jit(solution)/shard_map/ppermute | solution.py:145
  159.4 17.5 %collective-permute-start.28 = (bf16[3,32,1792]{2,1,0:T(8,128)(2,1)S(1)}, bf16[3,32,1792]{2,1,0:T(8,128)(2,1)S(1)}, u32[]{:S(2)}, u32[]{:S(2)}) collective-permute-start(bf16[3,32,1792]{2,1,0:T(8,128)(2,1)S(1)} %pad_maximum_fusion.11), channel_id=1, source_target_pairs={{0,4},{2,6},{4,0},{6,2},{8,12},{10,14},{12,8},{14,10},{1,5},{3,7},... | collective-permute-start | bytes 1032200 | tf_op jit(solution)/shard_map/ppermute | solution.py:145
  163.2 21.1 %collective-permute-start.22 = (bf16[3,32,1792]{2,1,0:T(8,128)(2,1)S(1)}, bf16[3,32,1792]{2,1,0:T(8,128)(2,1)S(1)}, u32[]{:S(2)}, u32[]{:S(2)}) collective-permute-start(bf16[3,32,1792]{2,1,0:T(8,128)(2,1)S(1)} %pad_maximum_fusion.10), channel_id=1, source_target_pairs={{0,4},{2,6},{4,0},{6,2},{8,12},{10,14},{12,8},{14,10},{1,5},{3,7},... | collective-permute-start | bytes 1032200 | tf_op jit(solution)/shard_map/ppermute | solution.py:145
  166.9 24.7 %collective-permute-start.16 = (bf16[3,32,1792]{2,1,0:T(8,128)(2,1)S(1)}, bf16[3,32,1792]{2,1,0:T(8,128)(2,1)S(1)}, u32[]{:S(2)}, u32[]{:S(2)}) collective-permute-start(bf16[3,32,1792]{2,1,0:T(8,128)(2,1)S(1)} %pad_maximum_fusion.9), channel_id=1, source_target_pairs={{0,4},{2,6},{4,0},{6,2},{8,12},{10,14},{12,8},{14,10},{1,5},{3,7},... | collective-permute-start | bytes 1032200 | tf_op jit(solution)/shard_map/ppermute | solution.py:145
  169.5 29.4 %collective-permute-start.10 = (bf16[3,32,1792]{2,1,0:T(8,128)(2,1)S(1)}, bf16[3,32,1792]{2,1,0:T(8,128)(2,1)S(1)}, u32[]{:S(2)}, u32[]{:S(2)}) collective-permute-start(bf16[3,32,1792]{2,1,0:T(8,128)(2,1)S(1)} %pad_maximum_fusion.8), channel_id=1, source_target_pairs={{0,4},{2,6},{4,0},{6,2},{8,12},{10,14},{12,8},{14,10},{1,5},{3,7},... | collective-permute-start | bytes 1032200 | tf_op jit(solution)/shard_map/ppermute | solution.py:145
  176.9 23.5 %collective-permute-start.29 = (bf16[3,64,1792]{2,1,0:T(8,128)(2,1)S(1)}, bf16[3,64,1792]{2,1,0:T(8,128)(2,1)S(1)}, u32[]{:S(2)}, u32[]{:S(2)}) collective-permute-start(bf16[3,64,1792]{2,1,0:T(8,128)(2,1)S(1)} %pad_maximum_fusion.7), channel_id=1, source_target_pairs={{0,2},{2,0},{4,6},{6,4},{8,10},{10,8},{12,14},{14,12},{1,3},{3,1},... | collective-permute-start | bytes 2064392 | tf_op jit(solution)/shard_map/ppermute | solution.py:145
  184.3 25.8 %collective-permute-start.23 = (bf16[3,64,1792]{2,1,0:T(8,128)(2,1)S(1)}, bf16[3,64,1792]{2,1,0:T(8,128)(2,1)S(1)}, u32[]{:S(2)}, u32[]{:S(2)}) collective-permute-start(bf16[3,64,1792]{2,1,0:T(8,128)(2,1)S(1)} %pad_maximum_fusion.6), channel_id=1, source_target_pairs={{0,2},{2,0},{4,6},{6,4},{8,10},{10,8},{12,14},{14,12},{1,3},{3,1},... | collective-permute-start | bytes 2064392 | tf_op jit(solution)/shard_map/ppermute | solution.py:145
  191.6 33.1 %collective-permute-start.17 = (bf16[3,64,1792]{2,1,0:T(8,128)(2,1)S(1)}, bf16[3,64,1792]{2,1,0:T(8,128)(2,1)S(1)}, u32[]{:S(2)}, u32[]{:S(2)}) collective-permute-start(bf16[3,64,1792]{2,1,0:T(8,128)(2,1)S(1)} %pad_maximum_fusion.5), channel_id=1, source_target_pairs={{0,2},{2,0},{4,6},{6,4},{8,10},{10,8},{12,14},{14,12},{1,3},{3,1},... | collective-permute-start | bytes 2064392 | tf_op jit(solution)/shard_map/ppermute | solution.py:145
  198.9 47.8 %collective-permute-start.11 = (bf16[3,64,1792]{2,1,0:T(8,128)(2,1)S(1)}, bf16[3,64,1792]{2,1,0:T(8,128)(2,1)S(1)}, u32[]{:S(2)}, u32[]{:S(2)}) collective-permute-start(bf16[3,64,1792]{2,1,0:T(8,128)(2,1)S(1)} %pad_maximum_fusion.4), channel_id=1, source_target_pairs={{0,2},{2,0},{4,6},{6,4},{8,10},{10,8},{12,14},{14,12},{1,3},{3,1},... | collective-permute-start | bytes 2064392 | tf_op jit(solution)/shard_map/ppermute | solution.py:145
  257.8 14.4 %collective-permute-start.30 = (f32[2,128,1024]{2,1,0:T(8,128)S(1)}, f32[2,128,1024]{2,1,0:T(8,128)S(1)}, u32[]{:S(2)}, u32[]{:S(2)}) collective-permute-start(f32[2,128,1024]{2,1,0:T(8,128)S(1)} %get-tuple-element.67.own), channel_id=1, source_target_pairs={{0,1},{1,0},{2,3},{3,2},{4,5},{5,4},{6,7},{7,6},{8,9},{9,8},{10,11... | collective-permute-start | bytes 3145736 | tf_op jit(solution)/shard_map/ppermute | solution.py:149
  267.7 4.4 %collective-permute-start.34 = (f32[1,128]{1,0:T(1,128)S(1)}, f32[1,128]{1,0:T(1,128)S(1)}, u32[]{:S(2)}, u32[]{:S(2)}) collective-permute-start(f32[1,128]{1,0:T(1,128)S(1)} %add.202), channel_id=1, source_target_pairs={{0,8},{2,10},{4,12},{6,14},{8,0},{10,2},{12,4},{14,6},{1,9},{3,11}... | collective-permute-start | bytes 1544 | tf_op jit(solution)/shard_map/ppermute | solution.py:145
  (18 other events, 153.2 us)

commit v2 on v0

v2 whole, which is shorter than its diff:
```python
import functools

import jax
import jax.numpy as jnp
from jax import lax
from jax.experimental import pallas as pl
from jax.experimental.pallas import tpu as pltpu
from jax.sharding import PartitionSpec as P

EPS = 1e-05
BF16 = jnp.bfloat16
F32 = jnp.float32
COUNTS = (2, 2, 2, 1)
SWAPPED = (False, False, False, False)
DOWN = ((0, 1), (2, 3))
ORDER = (
    ("D", 0), ("Q", 1), ("Q", 2), ("D", 1), ("N",), ("F", 0), ("F", 1), ("H", 0, 0), ("F", 2), ("H", 1, 0),
    ("H", 0, 1), ("F", 3), ("W", 0), ("H", 2, 0), ("H", 1, 1), ("J", 0, 2), ("W", 1), ("H", 2, 1),
    ("J", 0, 1), ("H", 3, 0), ("J", 1, 2), ("W", 2), ("H", 3, 1), ("J", 1, 1), ("J", 2, 2), ("B", 0),
    ("W", 3), ("J", 2, 1), ("J", 3, 2), ("B", 1), ("J", 3, 1), ("B", 2), ("B", 3),
)
START_MIB, HEAD_MIB, FORE_MIB, BACK_MIB = 60, 44, 44, 44
NT = (((1,), (1,)), ((), ()))
TN = (((0,), (0,)), ((), ()))
VMEM = pl.BlockSpec(memory_space=pltpu.VMEM)
SMEM = pl.BlockSpec(memory_space=pltpu.SMEM)
ANY = pl.BlockSpec(memory_space=pl.ANY)


def cost(flops, nbytes):
    return pl.CostEstimate(flops=int(flops), bytes_accessed=int(nbytes), transcendentals=0)


def params(mib):
    return pltpu.CompilerParams(vmem_limit_bytes=mib * 1024 * 1024)


def matmul(a, b, dims=(((1,), (0,)), ((), ()))):
    return lax.dot_general(a, b, dims, preferred_element_type=F32)


def order(label, tokens, block):
    p = lax.broadcasted_iota(jnp.int32, (tokens, tokens), 0)
    t = lax.broadcasted_iota(jnp.int32, (tokens, tokens), 1)
    return ((p // block) ^ label) * block + p % block == t


def split_rows(part, swapped):
    half = part.shape[0] // 2
    if not swapped:
        return part[:half], part[half:]
    q = half // 2
    return (
        jnp.concatenate([part[:q], part[half : half + q]], axis=0),
        jnp.concatenate([part[q:half], part[half + q :]], axis=0),
    )


def join_rows(own, other, swapped):
    if not swapped:
        return jnp.concatenate([own, other], axis=0)
    q = own.shape[0] // 2
    return jnp.concatenate([own[:q], other[:q], own[q:], other[q:]], axis=0)


def down_copies(spans, w_down, w_buf, sems):
    copies, at = [], 0
    for k, (first, size) in enumerate(spans):
        copies.append(pltpu.make_async_copy(w_down.at[pl.ds(first, size)], w_buf.at[pl.ds(at, size)], sems.at[k]))
        at += size
    return copies


def down_products(spans, copies, swapped, dout, w_buf, keep, send):
    at = 0
    for (_, size), copy in zip(spans, copies):
        copy.wait()
        here = slice(at, at + size)
        kept, sent = split_rows(matmul(dout[...], w_buf[here], NT), swapped)
        keep[0, :, here] = kept
        send[0, :, here] = sent.astype(BF16)
        at += size


def start_kernel(block, label, ids, excluded, store, grad_out, rows, dout, squares, pool_buf, grad_buf, sems):
    copies = [
        pltpu.make_async_copy(store, pool_buf, sems.at[0]),
        pltpu.make_async_copy(grad_out, grad_buf, sems.at[1]),
    ]
    for copy in copies:
        copy.start()
    tokens = grad_buf.shape[0]
    pool = pool_buf.shape[0]
    perm = jnp.where(order(label[0], tokens, block), 1.0, 0.0).astype(BF16)
    position = lax.broadcasted_iota(jnp.int32, (tokens, excluded.shape[1]), 0)
    match = jnp.where(position == excluded[...], 1.0, 0.0)
    dropped = jnp.max(match, axis=1, keepdims=True) > 0.0
    hit = lax.broadcasted_iota(jnp.int32, (pool, tokens), 0) == ids[...]
    hit = jnp.where(hit, 1.0, 0.0).astype(BF16)
    copies[0].wait()
    natural = matmul(hit, pool_buf[...], TN)
    total = jnp.sum(natural * natural, axis=1, keepdims=True)
    squares[...] = jnp.transpose(jnp.broadcast_to(total, (tokens, tokens)))[:1]
    rows[...] = matmul(perm, natural.astype(BF16)).astype(BF16)
    copies[1].wait()
    kept = jnp.where(dropped, 0.0, grad_buf[...].astype(F32)).astype(BF16)
    dout[...] = matmul(perm, kept).astype(BF16)


def down_kernel(spans, swapped, dout, w_down, *rest):
    keep, send, w_buf, sems = rest[-4:]
    copies = down_copies(spans, w_down, w_buf, sems)
    for copy in copies:
        copy.start()
    down_products(spans, copies, swapped, dout, w_buf, keep, send)


def add_kernel(own, other, *rest):
    rest[-1][...] = own[...] + other[...]


def norm_kernel(block, width, label, rows, squares, other, gain, *rest):
    normed, flipped, total = rest[-3:]
    tokens = rows.shape[0]
    total[...] = squares[...] + other[...]
    inv = lax.rsqrt(total[...] / width + EPS)
    inv = jnp.where(order(label[0], tokens, block), inv, 0.0)
    inv = jnp.sum(inv, axis=1, keepdims=True)
    value = (rows[...].astype(F32) * inv * gain[...]).astype(BF16)
    normed[...] = value
    flipped[...] = jnp.transpose(value.astype(F32)).astype(BF16)


def fore_kernel(swapped, normed, w_gate, w_up, *rest):
    keep, send = rest[-2:]
    for k, w in enumerate((w_gate, w_up)):
        kept, sent = split_rows(matmul(normed[...], w[...]), swapped)
        keep[k] = kept
        send[k] = sent.astype(BF16)


def halve_kernel(spans, *refs):
    keep, send = refs[-2:]
    rest = keep.shape[1]
    k = 0
    for n, span in enumerate(spans):
        kept, received = refs[2 * n], refs[2 * n + 1]
        for unit in range(kept.shape[0]):
            total = kept[unit, :, span] + received[unit, :, span].astype(F32)
            keep[k] = total[:rest]
            send[k] = total[rest:].astype(BF16)
            k += 1


def swiglu_kernel(last, kept, received, inner, *rest):
    acts, inner_out = rest[-2:]
    d_hidden, gate_pre, up_proj = (kept[k] + received[k].astype(F32) for k in range(3))
    part = gate_pre.shape[1]
    sigmoid_gate = jax.nn.sigmoid(gate_pre)
    silu = gate_pre * sigmoid_gate
    d_gate = (d_hidden * up_proj * sigmoid_gate * (1.0 + gate_pre * (1.0 - sigmoid_gate))).astype(BF16)
    d_up = (d_hidden * silu).astype(BF16)
    acts[0, :, :part] = (silu * up_proj).astype(BF16)
    acts[1, :, :part] = d_gate
    acts[2, :, :part] = d_up
    terms = d_gate.astype(F32) * gate_pre + d_up.astype(F32) * up_proj
    total = inner[...] + jnp.broadcast_to(jnp.sum(terms, axis=1, keepdims=True), inner.shape)
    inner_out[...] = total
    if last:
        for k in range(3):
            piece = total.astype(BF16)
            acts[k, :, part:] = piece
            total = total - piece.astype(F32)


def join_kernel(own, other, *rest):
    rows = own.shape[1]
    out = rest[-1]
    out[:, :rows] = own[...]
    out[:, rows:] = other[...]


def back_kernel(first, last, swapped, own, other, flipped, dout, w_gate, w_up, w_down, *rest):
    acc, gate_grad, up_grad, down_grad = rest[-4:]
    tokens = dout.shape[0]
    step = pl.program_id(0)

    @pl.when(step == 0)
    def _():
        acc[...] = jnp.zeros_like(acc) if first else rest[0][...]

    hidden, d_gate, d_up = (join_rows(own[k], other[k], swapped) for k in range(3))
    gate_grad[...] = matmul(flipped[...], d_gate).astype(BF16)
    up_grad[...] = matmul(flipped[...], d_up).astype(BF16)
    down_grad[...] = matmul(hidden, dout[...], TN).astype(BF16)
    acc[:tokens] += matmul(hidden, w_down[...])
    acc[tokens : 2 * tokens] += matmul(d_gate, w_gate[...], NT) + matmul(d_up, w_up[...], NT)
    if last:

        @pl.when(step == 0)
        def _():
            places = 0 if first else 4
            pieces = [sum(x[k].astype(F32) for k in range(3)) for x in rest[places : places + 2]]
            inner = jnp.transpose(join_rows(*pieces, swapped))[:8]
            acc[2 * tokens :, :tokens] = inner


def end_kernel(block, width, label, own, other, rows, dout, gain, squares, ids, output, store_grad, gain_grad):
    tokens = rows.shape[0]
    pool = store_grad.shape[0]
    places = order(label[0], tokens, block)
    perm = jnp.where(places, 1.0, 0.0).astype(BF16)
    inv = lax.rsqrt(squares[...] / width + EPS)
    inv = jnp.sum(jnp.where(places, inv, 0.0), axis=1, keepdims=True)
    here = lax.broadcasted_iota(jnp.int32, (tokens, tokens), 0) == lax.broadcasted_iota(jnp.int32, (tokens, tokens), 1)
    inner = own[2 * tokens : 2 * tokens + 1, :tokens] + other[2 * tokens : 2 * tokens + 1, :tokens]
    inner = jnp.sum(jnp.where(here, inner, 0.0), axis=1, keepdims=True)
    row = rows[...].astype(F32)
    result = (row + (own[:tokens] + other[:tokens])).astype(BF16)
    output[...] = matmul(perm, result, TN).astype(BF16)
    d_normed = own[tokens : 2 * tokens] + other[tokens : 2 * tokens]
    gain_grad[...] = jnp.sum(d_normed * row * inv, axis=0, keepdims=True)
    d_rows = dout[...].astype(F32) + inv * (d_normed * gain[...]) - row * (inv * inv * (inner / width))
    hit = lax.broadcasted_iota(jnp.int32, (pool, tokens), 0) == ids[...]
    target = matmul(jnp.where(hit, 1.0, 0.0).astype(BF16), perm, NT).astype(BF16)
    total = jnp.zeros(store_grad.shape, F32)
    for _ in range(3):
        piece = d_rows.astype(BF16)
        total += matmul(target, piece)
        d_rows = d_rows - piece.astype(F32)
    store_grad[...] = total.astype(BF16)


def shards(sizes, replay_store, replay_ids, excluded, norm_gain, w_gate, w_up, w_down, grad_out):
    ways = sizes["width"]
    steps = ways.bit_length() - 1
    tokens, d_here = grad_out.shape
    ff = w_down.shape[0]
    width = ways * d_here
    block = tokens // ways
    half = tokens // 2
    pool = replay_store.shape[0]
    tile = ff // sum(COUNTS)
    shape = jax.ShapeDtypeStruct

    index = lax.axis_index("width")
    label = sum(((index >> s) & 1) << (steps - 1 - s) for s in range(steps))
    label = jnp.reshape(label, (1,)).astype(jnp.int32)

    def swap(x, step):
        return lax.ppermute(x, "width", [(i, i ^ (1 << step)) for i in range(ways)])

    def swap_cores(x):
        n = sizes["hidden"]
        return lax.ppermute(x, "hidden", [(i, (i + 1) % n) for i in range(n)])

    ids = replay_ids.reshape(1, tokens)
    gain = norm_gain.reshape(1, d_here)
    routes = [[1, 0, *range(2, steps)] if swapped else list(range(steps)) for swapped in SWAPPED]
    chunks = len(COUNTS)
    parts = [count * tile for count in COUNTS]
    firsts = [sum(parts[:j]) for j in range(chunks)]
    token, held, arrived = [], [], {}

    def kernel(body, out_shape, in_specs, out_specs, ins, name, mib=24, flops=0, moved=0, **more):
        after = token[-1:] + held
        held.clear()
        outs = pl.pallas_call(
            body,
            out_shape=out_shape,
            in_specs=list(in_specs) + [ANY] * len(after),
            out_specs=out_specs,
            compiler_params=params(mib),
            cost_estimate=cost(0, 0),
            name=name,
            **more,
        )(*ins, *after)
        token.append(outs[0])
        return outs

    def down_shapes(group):
        wide = sum(parts[j] for j in group)
        return (shape((1, half, wide), F32), shape((1, half, wide), BF16)), [
            pltpu.VMEM((wide, d_here), BF16),
            pltpu.SemaphoreType.DMA((len(group),)),
        ]

    down_parts = {}

    def down_done(g, group, keep, send):
        recv = arrived["D", g] = swap(send, routes[group[0]][0])
        at = 0
        for j in group:
            down_parts[j] = (keep, recv, slice(at, at + parts[j]))
            at += parts[j]

    rows, dout, squares = kernel(
        functools.partial(start_kernel, block),
        (shape((tokens, d_here), BF16), shape((tokens, d_here), BF16), shape((1, tokens), F32)),
        [SMEM, VMEM, VMEM, ANY, ANY],
        (VMEM,) * 3,
        [label, ids, excluded.reshape(1, -1), replay_store, grad_out],
        "start",
        mib=START_MIB,
        scratch_shapes=[
            pltpu.VMEM((pool, d_here), BF16),
            pltpu.VMEM((tokens, d_here), BF16),
            pltpu.SemaphoreType.DMA((2,)),
        ],
    )

    def down(g):
        group = DOWN[g]
        out_shape, scratch = down_shapes(group)
        spans = [(firsts[j], parts[j]) for j in group]
        keep, send = kernel(
            functools.partial(down_kernel, spans, SWAPPED[group[0]]),
            out_shape,
            [VMEM, ANY],
            (VMEM, VMEM),
            [dout, w_down],
            "d_hidden",
            mib=HEAD_MIB,
            scratch_shapes=scratch,
        )
        down_done(g, group, keep, send)

    state = {"inner": jnp.zeros((block, 128), F32), "acc": None, "grads": None, "swiglu": 0, "back": 0}
    state["squares"] = squares

    arrived["Q", 0] = swap(squares, 0)

    def square(step):
        for k in range(step, steps if step == 2 else step + 1):
            (state["squares"],) = kernel(
                add_kernel,
                (shape((1, tokens), F32),),
                [VMEM, VMEM],
                (VMEM,),
                [state["squares"], arrived["Q", min(k, 3) - 1]],
                "squares",
            )
            arrived["Q", min(k, 2)] = swap(state["squares"], k)

    def norm():
        normed, flipped, state["squares"] = kernel(
            functools.partial(norm_kernel, block, width),
            (shape((tokens, d_here), BF16), shape((d_here, tokens), BF16), shape((1, tokens), F32)),
            [SMEM, VMEM, VMEM, VMEM, VMEM],
            (VMEM, VMEM, VMEM),
            [label, rows, state["squares"], arrived["Q", 2], gain],
            "norm",
        )
        return normed, flipped

    sums, acts, others = {}, {}, {}
    def fore(j):
        part = parts[j]
        out = pl.BlockSpec((2, half, tile), lambda i: (0, 0, i))
        col = pl.BlockSpec((d_here, tile), lambda i: (0, firsts[j] // tile + i))
        keep, send = kernel(
            functools.partial(fore_kernel, SWAPPED[j]),
            (shape((2, half, part), F32), shape((2, half, part), BF16)),
            [pl.BlockSpec((tokens, d_here), lambda i: (0, 0)), col, col],
            (out, out),
            [state["normed"][0], w_gate, w_up],
            "gate_up",
            mib=FORE_MIB,
            flops=4 * tokens * part * d_here,
            moved=4 * part * d_here,
            grid=(COUNTS[j],),
        )
        arrived["F", j] = swap(send, routes[j][0])
        sums[j] = [down_parts[j], (keep, arrived["F", j], slice(0, part))]

    def halve(j, at):
        for step in range(at, steps - 1 if at else 1):
            pairs = sums[j]
            units = sum(kept.shape[0] for kept, _, _ in pairs)
            rows_here = pairs[0][0].shape[1]
            part = parts[j]
            keep, send = kernel(
                functools.partial(halve_kernel, [span for _, _, span in pairs]),
                (shape((units, rows_here // 2, part), F32), shape((units, rows_here // 2, part), BF16)),
                [VMEM] * (2 * len(pairs)),
                (VMEM, VMEM),
                [x for kept, received, _ in pairs for x in (kept, received)],
                "halve",
            )
            arrived["H", j, at] = swap(send, routes[j][step + 1])
            sums[j] = [(keep, arrived["H", j, at], slice(0, part))]

    def swiglu(j):
        state["swiglu"] += 1
        last = state["swiglu"] == chunks
        state["last"] = j if last else None
        keep, recv, _ = sums[j][0]
        acts[j], state["inner"] = kernel(
            functools.partial(swiglu_kernel, last),
            (shape((3, block, parts[j] + (128 if last else 0)), BF16), shape((block, 128), F32)),
            [VMEM] * 3,
            (VMEM, VMEM),
            [keep, recv, state["inner"]],
            "swiglu",
        )
        others[j] = arrived["W", j] = swap(acts[j], routes[j][steps - 1])

    def join(j, at):
        for step in reversed(range(at, steps if at > 1 else 2)):
            own, other = acts[j], others[j]
            if own.shape[1] % 16:
                acts[j] = jnp.concatenate([own, other], axis=1)
            else:
                (acts[j],) = kernel(
                    join_kernel,
                    (shape((3, 2 * own.shape[1], own.shape[2]), BF16),),
                    [VMEM, VMEM],
                    (VMEM,),
                    [own, other],
                    "join",
                )
            others[j] = arrived["J", j, at] = swap(acts[j], routes[j][step - 1])

    def back(j):
        state["back"] += 1
        first, last = state["back"] == 1, j == state["last"]
        own, other = acts[j], others[j]
        start = firsts[j] // tile
        col = pl.BlockSpec((d_here, tile), lambda i: (0, start + i))
        row = pl.BlockSpec((tile, d_here), lambda i: (start + i, 0))
        whole = lambda i: (0, 0)
        acc_spec = pl.BlockSpec((2 * tokens + 8, d_here), whole)
        piece = pl.BlockSpec((3, half, tile), lambda i: (0, 0, i))
        ins = [own, other, state["normed"][1], dout, w_gate, w_up, w_down]
        specs = [
            piece,
            piece,
            pl.BlockSpec((d_here, tokens), whole),
            pl.BlockSpec((tokens, d_here), whole),
            col,
            col,
            row,
        ]
        alias = {}
        if not first:
            ins += [state["acc"], *state["grads"]]
            specs += [acc_spec, ANY, ANY, ANY]
            alias = {8: 1, 9: 2, 10: 3}
        if last:
            extra = pl.BlockSpec((3, half, 128), lambda i: (0, 0, parts[j] // 128))
            ins += [own, other]
            specs += [extra, extra]
        state["acc"], *state["grads"] = kernel(
            functools.partial(back_kernel, first, last, SWAPPED[j]),
            (
                shape((2 * tokens + 8, d_here), F32),
                shape((d_here, ff), BF16),
                shape((d_here, ff), BF16),
                shape((ff, d_here), BF16),
            ),
            specs,
            (acc_spec, col, col, row),
            ins,
            "back",
            mib=BACK_MIB,
            flops=12 * tokens * parts[j] * d_here,
            moved=12 * parts[j] * d_here,
            grid=(COUNTS[j],),
            input_output_aliases=alias,
        )

    tasks = {"D": down, "Q": square, "F": fore, "H": halve, "W": swiglu, "J": join, "B": back}
    for task, *where in ORDER:
        if task == "A":
            held.append(arrived[tuple(where)])
        elif task == "N":
            state["normed"] = norm()
        else:
            tasks[task](*where)
    acc, grads = state["acc"], state["grads"]

    other = swap_cores(acc)
    output, store_grad, gain_grad = pl.pallas_call(
        functools.partial(end_kernel, block, width),
        out_shape=(shape((tokens, d_here), BF16), shape((pool, d_here), BF16), shape((1, d_here), F32)),
        in_specs=[SMEM] + [VMEM] * 7,
        out_specs=(VMEM, VMEM, VMEM),
        compiler_params=params(32),
        cost_estimate=cost(2 * tokens * pool * d_here, 16 * tokens * d_here),
        name="end",
    )(label, acc, other, rows, dout, gain, state["squares"], ids)
    return (output, store_grad, gain_grad.reshape(d_here), *grads)


def solution(mesh):
    return jax.shard_map(
        functools.partial(shards, dict(mesh.shape)),
        mesh=mesh,
        in_specs=(
            P("groups", "width"),
            P("groups"),
            P("groups"),
            P("width"),
            P("width", "hidden"),
            P("width", "hidden"),
            P("hidden", "width"),
            P("groups", "width"),
        ),
        out_specs=(
            P("groups", "width"),
            P("groups", "width"),
            P(("groups", "width")),
            P(("groups", "width"), "hidden"),
            P(("groups", "width"), "hidden"),
            P(("groups", "hidden"), "width"),
        ),
        check_vma=False,
    )
```

time: 485 us -> 187 us (0.39)
  waiting for transfers between devices: 332 us -> 72 us
  matrix products: 85 us -> 0 us
  Pallas kernels: 0 us -> 73.2 us
  blocking collectives: 43.2 us -> 0 us
  starting transfers between devices: 0.46 us -> 38.6 us
  between operations: 14.2 us -> 0.97 us
  other arithmetic: 9.61 us -> 0 us
    reduce_scatter x3 -> x0, waiting for transfers between devices: 209 us -> none  [the longest x1 84.7 us: shards(): lax.psum_scatter(up_part, 'width', scatter_dimension=0, tiled=True)]
    all_gather x3 -> x0, waiting for transfers between devices: 121 us -> none  [the longest x1 44.8 us: shards(): lax.all_gather(swiglu(gate_pre, up_proj), 'width', axis=0, tiled=True)]
    dot_general x9 -> x0, matrix products: 85 us -> none  [the longest x1 12 us: shards(): lax.dot_general(d_output, w_down, contract_last, preferred_element_type=j...]
    pallas_call x0 -> x35, Pallas kernels: none -> 73.2 us  [the longest x34 71.5 us: kernel(): pl.pallas_call(body, out_shape=out_shape, in_specs=list(in_specs) + [ANY]...]
    ppermute x0 -> x30, waiting for transfers between devices: none -> 72 us  [the longest x29 69.3 us: swap(): return lax.ppermute(x, 'width', [(i, i ^ 1 << step) for i in range(ways)])]
    psum x2 -> x0, blocking collectives: 43.2 us -> none  [the longest x1 23.7 us: shards(): lax.psum(jnp.sum(row_float * row_float, axis=1, keepdims=True), 'width')]
    ppermute x0 -> x30, starting transfers between devices: none -> 38.6 us  [the longest x29 38.5 us: swap(): return lax.ppermute(x, 'width', [(i, i ^ 1 << step) for i in range(ways)])]
  transfers between devices with their start and end apart: 7 -> 30, of which waited for: 6 -> 11; matrix products, arithmetic and copies ran while one was open for 13% -> 0% of each run, Pallas kernels for 0% -> 33%
where the time goes in v2:
time: 187 us
  Pallas kernels  73.2 us (39%)
  waiting for transfers between devices  72 us (39%)
  starting transfers between devices  38.6 us (21%)
  local copies, waits for them, and re-layouts  1.92 us (1%)
    pallas_call x34, Pallas kernels, kernel(): pl.pallas_call(body, out_shape=out_shape, in_specs=list(in_specs) + [ANY]...  71.5 us
    ppermute x29, waiting for transfers between devices, swap(): return lax.ppermute(x, 'width', [(i, i ^ 1 << step) for i in range(ways)])  69.3 us
    ppermute x29, starting transfers between devices, swap(): return lax.ppermute(x, 'width', [(i, i ^ 1 << step) for i in range(ways)])  38.5 us
  transfers between devices with their start and end apart: 30, of which 11 were waited for; matrix products, arithmetic and copies ran while one was open for 0% of the time, Pallas kernels for 33%

profile of v2, /device:TPU:0, one launch (start us, length us, event | category | flops | bytes accessed | tf_op | source)
XLA Modules:
  0.0 186.7 jit_solution(17263342568919367130)
XLA Ops:
  0.6 3.1 %start.1 = (bf16[128,1024]{1,0:T(8,128)(2,1)}, bf16[128,1024]{1,0:T(8,128)(2,1)}, f32[1,128]{1,0:T(1,128)}) custom-call(s32[1]{0:T(128)} %bitcast.label, s32[1,128]{1,0:T(1,128)} %bitcast.7, s32[1,16]{1,0:T(1,128)} %bitcast.9, bf16[256,1024]{1,0:T(8,128)(2,1)} %store.1, bf16[128,1024]{1,0:T(8,128)(2,1)} %grad_out.1), custom_call_target="tpu_custom_call" | custom-call | tf_op jit(solution)/shard_map/start/pallas_call | solution.py:268
  3.7 3.0 %collective-permute-start = (f32[1,128]{1,0:T(1,128)}, f32[1,128]{1,0:T(1,128)S(1)}, u32[]{:S(2)}, u32[]{:S(2)}) collective-permute-start(f32[1,128]{1,0:T(1,128)} %get-tuple-element.67.own), channel_id=1, source_target_pairs={{0,2},{2,0},{4,6},{6,4},{8,10},{10,8},{12,14},{14,12},{1,3},{3,1},... | collective-permute-start | bytes 1544 | tf_op jit(solution)/shard_map/ppermute | solution.py:251
  8.7 5.3 %d_hidden.2 = (f32[1,64,4096]{2,1,0:T(8,128)S(1)}, bf16[1,64,4096]{2,1,0:T(8,128)(2,1)S(1)}) custom-call(bf16[128,1024]{1,0:T(8,128)(2,1)S(1)} %copy-done, bf16[7168,1024]{1,0:T(8,128)(2,1)} %w_down.11, bf16[128,1024]{1,0:T(8,128)(2,1)S(1)} %copy-done.2), custom_call_target="tpu_custom_call" | custom-call | tf_op jit(solution)/shard_map/d_hidden/pallas_call | solution.py:268
  15.6 2.0 %collective-permute-done.1.other = f32[1,128]{1,0:T(1,128)S(1)} collective-permute-done((f32[1,128]{1,0:T(1,128)S(1)}, f32[1,128]{1,0:T(1,128)S(1)}, u32[]{:S(2)}, u32[]{:S(2)}) %collective-permute-start.1) | collective-permute-done | bytes 544 | tf_op jit(solution)/shard_map/ppermute | solution.py:251
  17.6 2.6 %collective-permute-start.3 = (f32[1,128]{1,0:T(1,128)S(1)}, f32[1,128]{1,0:T(1,128)S(1)}, u32[]{:S(2)}, u32[]{:S(2)}) collective-permute-start(f32[1,128]{1,0:T(1,128)S(1)} %squares.3.rest_0_), channel_id=1, source_target_pairs={{0,8},{2,10},{4,12},{6,14},{8,0},{10,2},{12,4},{14,6},{1,9},{3,11}... | collective-permute-start | bytes 1544 | tf_op jit(solution)/shard_map/ppermute | solution.py:251
  20.7 4.5 %d_hidden.3 = (f32[1,64,3072]{2,1,0:T(8,128)S(1)}, bf16[1,64,3072]{2,1,0:T(8,128)(2,1)S(1)}) custom-call(bf16[128,1024]{1,0:T(8,128)(2,1)S(1)} %copy-done.1, bf16[7168,1024]{1,0:T(8,128)(2,1)} %w_down.11, f32[1,128]{1,0:T(1,128)S(1)} %squares.3.rest_0_), custom_call_target="tpu_custom_call" | custom-call | tf_op jit(solution)/shard_map/d_hidden/pallas_call | solution.py:268
  25.5 4.5 %gate_up.4 = (f32[2,64,2048]{2,1,0:T(8,128)S(1)}, bf16[2,64,2048]{2,1,0:T(8,128)(2,1)S(1)}) custom-call(bf16[128,1024]{1,0:T(8,128)(2,1)S(1)} %get-tuple-element.72.normed.rest_0_, bf16[1024,7168]{1,0:T(8,128)(2,1)} %w_gate.15, bf16[1024,7168]{1,0:T(8,128)(2,1)} %w_up.15, bf16[128,1024]{1,0:T(8,128)(2,1)S(1)} %get-tuple-element.72.normed.rest_0_), custom_call_target="tpu_custom_call" | custom-call | tf_op jit(solution)/shard_map/gate_up/pallas_call | solution.py:268
  31.5 4.3 %gate_up.5 = (f32[2,64,2048]{2,1,0:T(8,128)S(1)}, bf16[2,64,2048]{2,1,0:T(8,128)(2,1)S(1)}) custom-call(bf16[128,1024]{1,0:T(8,128)(2,1)S(1)} %get-tuple-element.72.normed.rest_0_, bf16[1024,7168]{1,0:T(8,128)(2,1)} %w_gate.15, bf16[1024,7168]{1,0:T(8,128)(2,1)} %w_up.15, f32[2,64,2048]{2,1,0:T(8,128)S(1)} %get-tuple-element.74.rest_0_.refs_2_), custom_call_target="tpu_custom_call" | custom-call | tf_op jit(solution)/shard_map/gate_up/pallas_call | solution.py:268
  36.4 8.5 %collective-permute-done.5.refs_3_ = bf16[2,64,2048]{2,1,0:T(8,128)(2,1)S(1)} collective-permute-done((bf16[2,64,2048]{2,1,0:T(8,128)(2,1)S(1)}, bf16[2,64,2048]{2,1,0:T(8,128)(2,1)S(1)}, u32[]{:S(2)}, u32[]{:S(2)}) %collective-permute-start.5) | collective-permute-done | bytes 524320 | tf_op jit(solution)/shard_map/ppermute | solution.py:251
  46.7 4.3 %gate_up.6 = (f32[2,64,2048]{2,1,0:T(8,128)S(1)}, bf16[2,64,2048]{2,1,0:T(8,128)(2,1)S(1)}) custom-call(bf16[128,1024]{1,0:T(8,128)(2,1)S(1)} %get-tuple-element.72.normed.rest_0_, bf16[1024,7168]{1,0:T(8,128)(2,1)} %w_gate.15, bf16[1024,7168]{1,0:T(8,128)(2,1)} %w_up.15, f32[3,32,2048]{2,1,0:T(8,128)S(1)} %get-tuple-element.77.rest_0_.refs_0_), custom_call_target="tpu_custom_call" | custom-call | tf_op jit(solution)/shard_map/gate_up/pallas_call | solution.py:268
  53.1 3.1 %collective-permute-done.7.refs_3_ = bf16[2,64,2048]{2,1,0:T(8,128)(2,1)S(1)} collective-permute-done((bf16[2,64,2048]{2,1,0:T(8,128)(2,1)S(1)}, bf16[2,64,2048]{2,1,0:T(8,128)(2,1)S(1)}, u32[]{:S(2)}, u32[]{:S(2)}) %collective-permute-start.7) | collective-permute-done | bytes 524320 | tf_op jit(solution)/shard_map/ppermute | solution.py:251
  58.3 3.0 %gate_up.7 = (f32[2,64,1024]{2,1,0:T(8,128)S(1)}, bf16[2,64,1024]{2,1,0:T(8,128)(2,1)S(1)}) custom-call(bf16[128,1024]{1,0:T(8,128)(2,1)S(1)} %get-tuple-element.72.normed.rest_0_, bf16[1024,7168]{1,0:T(8,128)(2,1)} %w_gate.15, bf16[1024,7168]{1,0:T(8,128)(2,1)} %w_up.15, f32[3,16,2048]{2,1,0:T(8,128)S(1)} %get-tuple-element.82.rest_0_.kept), custom_call_target="tpu_custom_call" | custom-call | tf_op jit(solution)/shard_map/gate_up/pallas_call | solution.py:268
  61.3 3.4 %collective-permute-done.9.received = bf16[3,16,2048]{2,1,0:T(8,128)(2,1)S(1)} collective-permute-done((bf16[3,16,2048]{2,1,0:T(8,128)(2,1)S(1)}, bf16[3,16,2048]{2,1,0:T(8,128)(2,1)S(1)}, u32[]{:S(2)}, u32[]{:S(2)}) %collective-permute-start.9) | collective-permute-done | bytes 196640 | tf_op jit(solution)/shard_map/ppermute | solution.py:251
  65.8 8.5 %collective-permute-done.2.refs_1_ = bf16[1,64,3072]{2,1,0:T(8,128)(2,1)S(1)} collective-permute-done((bf16[1,64,3072]{2,1,0:T(8,128)(2,1)S(1)}, bf16[1,64,3072]{2,1,0:T(8,128)(2,1)S(1)}, u32[]{:S(2)}, u32[]{:S(2)}) %collective-permute-start.2) | collective-permute-done | bytes 393248 | tf_op jit(solution)/shard_map/ppermute | solution.py:251
  77.2 2.6 %collective-permute-start.8 = (bf16[2,64,1024]{2,1,0:T(8,128)(2,1)S(1)}, bf16[2,64,1024]{2,1,0:T(8,128)(2,1)S(1)}, u32[]{:S(2)}, u32[]{:S(2)}) collective-permute-start(bf16[2,64,1024]{2,1,0:T(8,128)(2,1)S(1)} %get-tuple-element.84), channel_id=1, source_target_pairs={{0,2},{2,0},{4,6},{6,4},{8,10},{10,8},{12,14},{14,12},{1,3},{3,1},... | collective-permute-start | bytes 786440 | tf_op jit(solution)/shard_map/ppermute | solution.py:251
  79.8 16.0 %collective-permute-done.15.received = bf16[3,16,2048]{2,1,0:T(8,128)(2,1)S(1)} collective-permute-done((bf16[3,16,2048]{2,1,0:T(8,128)(2,1)S(1)}, bf16[3,16,2048]{2,1,0:T(8,128)(2,1)S(1)}, u32[]{:S(2)}, u32[]{:S(2)}) %collective-permute-start.15) | collective-permute-done | bytes 196640 | tf_op jit(solution)/shard_map/ppermute | solution.py:251
  96.0 3.4 %collective-permute-start.18 = (bf16[3,16,2048]{2,1,0:T(8,128)(2,1)S(1)}, bf16[3,16,2048]{2,1,0:T(8,128)(2,1)S(1)}, u32[]{:S(2)}, u32[]{:S(2)}) collective-permute-start(bf16[3,16,2048]{2,1,0:T(8,128)(2,1)S(1)} %get-tuple-element.94.refs_2_.own), channel_id=1, source_target_pairs={{0,8},{2,10},{4,12},{6,14},{8,0},{10,2},{12,4},{14,6},{1,9},{3,11}... | collective-permute-start | bytes 589832 | tf_op jit(solution)/shard_map/ppermute | solution.py:251
  99.7 6.1 %collective-permute-done.18.other = bf16[3,16,2048]{2,1,0:T(8,128)(2,1)S(1)} collective-permute-done((bf16[3,16,2048]{2,1,0:T(8,128)(2,1)S(1)}, bf16[3,16,2048]{2,1,0:T(8,128)(2,1)S(1)}, u32[]{:S(2)}, u32[]{:S(2)}) %collective-permute-start.18) | collective-permute-done | bytes 196640 | tf_op jit(solution)/shard_map/ppermute | solution.py:251
  106.0 2.9 %collective-permute-start.17 = (bf16[3,16,2048]{2,1,0:T(8,128)(2,1)S(1)}, bf16[3,16,2048]{2,1,0:T(8,128)(2,1)S(1)}, u32[]{:S(2)}, u32[]{:S(2)}) collective-permute-start(bf16[3,16,2048]{2,1,0:T(8,128)(2,1)S(1)} %get-tuple-element.98), channel_id=1, source_target_pairs={{0,8},{2,10},{4,12},{6,14},{8,0},{10,2},{12,4},{14,6},{1,9},{3,11}... | collective-permute-start | bytes 589832 | tf_op jit(solution)/shard_map/ppermute | solution.py:251
  109.1 10.6 %collective-permute-done.17.received = bf16[3,16,2048]{2,1,0:T(8,128)(2,1)S(1)} collective-permute-done((bf16[3,16,2048]{2,1,0:T(8,128)(2,1)S(1)}, bf16[3,16,2048]{2,1,0:T(8,128)(2,1)S(1)}, u32[]{:S(2)}, u32[]{:S(2)}) %collective-permute-start.17) | collective-permute-done | bytes 196640 | tf_op jit(solution)/shard_map/ppermute | solution.py:251
  119.9 3.4 %collective-permute-start.21 = (bf16[3,16,2048]{2,1,0:T(8,128)(2,1)S(1)}, bf16[3,16,2048]{2,1,0:T(8,128)(2,1)S(1)}, u32[]{:S(2)}, u32[]{:S(2)}) collective-permute-start(bf16[3,16,2048]{2,1,0:T(8,128)(2,1)S(1)} %get-tuple-element.100.refs_2_.own), channel_id=1, source_target_pairs={{0,8},{2,10},{4,12},{6,14},{8,0},{10,2},{12,4},{14,6},{1,9},{3,11}... | collective-permute-start | bytes 589832 | tf_op jit(solution)/shard_map/ppermute | solution.py:251
  123.3 4.9 %collective-permute-done.16.refs_1_ = bf16[3,32,1024]{2,1,0:T(8,128)(2,1)S(1)} collective-permute-done((bf16[3,32,1024]{2,1,0:T(8,128)(2,1)S(1)}, bf16[3,32,1024]{2,1,0:T(8,128)(2,1)S(1)}, u32[]{:S(2)}, u32[]{:S(2)}) %collective-permute-start.16) | collective-permute-done | bytes 196640 | tf_op jit(solution)/shard_map/ppermute | solution.py:251
  128.4 2.0 %collective-permute-start.24 = (bf16[3,32,2048]{2,1,0:T(8,128)(2,1)S(1)}, bf16[3,32,2048]{2,1,0:T(8,128)(2,1)S(1)}, u32[]{:S(2)}, u32[]{:S(2)}) collective-permute-start(bf16[3,32,2048]{2,1,0:T(8,128)(2,1)S(1)} %join.12.rest_0_.own), channel_id=1, source_target_pairs={{0,4},{2,6},{4,0},{6,2},{8,12},{10,14},{12,8},{14,10},{1,5},{3,7},... | collective-permute-start | bytes 1179656 | tf_op jit(solution)/shard_map/ppermute | solution.py:251
  130.4 2.2 %collective-permute-start.19 = (bf16[3,16,1024]{2,1,0:T(8,128)(2,1)S(1)}, bf16[3,16,1024]{2,1,0:T(8,128)(2,1)S(1)}, u32[]{:S(2)}, u32[]{:S(2)}) collective-permute-start(bf16[3,16,1024]{2,1,0:T(8,128)(2,1)S(1)} %get-tuple-element.102), channel_id=1, source_target_pairs={{0,8},{2,10},{4,12},{6,14},{8,0},{10,2},{12,4},{14,6},{1,9},{3,11}... | collective-permute-start | bytes 294920 | tf_op jit(solution)/shard_map/ppermute | solution.py:251
  132.6 10.3 %back.4 = (f32[264,1024]{1,0:T(8,128)S(1)}, bf16[1024,7168]{1,0:T(8,128)(2,1)}, bf16[1024,7168]{1,0:T(8,128)(2,1)}, bf16[7168,1024]{1,0:T(8,128)(2,1)}) custom-call(bf16[3,64,2048]{2,1,0:T(8,128)(2,1)S(1)} %join.9.refs_4_.own, bf16[3,64,2048]{2,1,0:T(8,128)(2,1)S(1)} %collective-permute-done.20.other, bf16[1024,128]{1,0:T(8,128)(2,1)S(1)} %get-tuple-element.104.flipped, ...), custom_call_target="tpu_custom_call" | custom-call | tf_op jit(solution)/shard_map/back/pallas_call | solution.py:268
  143.7 1.7 collective-permute-start.28
  145.4 6.3 %collective-permute-done.23.other = bf16[3,16,1152]{2,1,0:T(8,128)(2,1)S(1)} collective-permute-done((bf16[3,16,1152]{2,1,0:T(8,128)(2,1)S(1)}, bf16[3,16,1152]{2,1,0:T(8,128)(2,1)S(1)}, u32[]{:S(2)}, u32[]{:S(2)}) %collective-permute-start.23) | collective-permute-done | bytes 110624 | tf_op jit(solution)/shard_map/ppermute | solution.py:251
  151.9 11.7 %back.5 = (f32[264,1024]{1,0:T(8,128)S(1)}, bf16[1024,7168]{1,0:T(8,128)(2,1)}, bf16[1024,7168]{1,0:T(8,128)(2,1)}, bf16[7168,1024]{1,0:T(8,128)(2,1)}) custom-call(bf16[3,64,2048]{2,1,0:T(8,128)(2,1)S(1)} %join.11.rest_0_.own, bf16[3,64,2048]{2,1,0:T(8,128)(2,1)S(1)} %collective-permute-done.26.other, ...), custom_call_target="tpu_custom_call", output_to_operand_aliasing={{1}: (8, {}), {2}: (9, {}), {3}: (10, {})} | custom-call | tf_op jit(solution)/shard_map/back/pallas_call | solution.py:268
  164.2 11.7 %back.6 = (f32[264,1024]{1,0:T(8,128)S(1)}, bf16[1024,7168]{1,0:T(8,128)(2,1)}, bf16[1024,7168]{1,0:T(8,128)(2,1)}, bf16[7168,1024]{1,0:T(8,128)(2,1)}) custom-call(bf16[3,64,2048]{2,1,0:T(8,128)(2,1)S(1)} %join.13.rest_0_.own, bf16[3,64,2048]{2,1,0:T(8,128)(2,1)S(1)} %collective-permute-done.28.other, ...), custom_call_target="tpu_custom_call", output_to_operand_aliasing={{1}: (8, {}), {2}: (9, {}), {3}: (10, {})} | custom-call | tf_op jit(solution)/shard_map/back/pallas_call | solution.py:268
  175.9 6.3 %back.7 = (f32[264,1024]{1,0:T(8,128)S(1)}, bf16[1024,7168]{1,0:T(8,128)(2,1)}, bf16[1024,7168]{1,0:T(8,128)(2,1)}, bf16[7168,1024]{1,0:T(8,128)(2,1)}) custom-call(bf16[3,64,1152]{2,1,0:T(8,128)(2,1)S(1)} %join.15.rest_4_.own, ...), custom_call_target="tpu_custom_call", output_to_operand_aliasing={{1}: (8, {}), {2}: (9, {}), {3}: (10, {})} | custom-call | tf_op jit(solution)/shard_map/back/pallas_call | solution.py:268
  182.3 2.7 %collective-permute-done.29.other = f32[264,1024]{1,0:T(8,128)S(1)} collective-permute-done((f32[264,1024]{1,0:T(8,128)S(1)}, f32[264,1024]{1,0:T(8,128)S(1)}, u32[]{:S(2)}, u32[]{:S(2)}) %collective-permute-start.29) | collective-permute-done | bytes 1081376 | tf_op jit(solution)/shard_map/ppermute | solution.py:255
  185.0 1.8 end.1
  (78 shorter events, 19.2 us)
Async XLA Ops:
  3.7 10.2 %collective-permute-start = (f32[1,128]{1,0:T(1,128)}, f32[1,128]{1,0:T(1,128)S(1)}, u32[]{:S(2)}, u32[]{:S(2)}) collective-permute-start(f32[1,128]{1,0:T(1,128)} %get-tuple-element.67.own), channel_id=1, source_target_pairs={{0,2},{2,0},{4,6},{6,4},{8,10},{10,8},{12,14},{14,12},{1,3},{3,1},... | collective-permute-start | bytes 1544 | tf_op jit(solution)/shard_map/ppermute | solution.py:251
  8.6 16.6 %copy-start.3 = (bf16[128,1024]{1,0:T(8,128)(2,1)S(1)}, bf16[128,1024]{1,0:T(8,128)(2,1)}, u32[]{:S(2)}) copy-start(bf16[128,1024]{1,0:T(8,128)(2,1)} %get-tuple-element.68.rest_0_.rows) | copy-start | bytes 786436
  8.7 16.6 %copy-start.4 = (f32[1024]{0:T(1024)S(1)}, f32[1024]{0:T(1024)}, u32[]{:S(2)}) copy-start(f32[1024]{0:T(1024)} %param.11) | copy-start | bytes 12292
  14.0 3.6 %collective-permute-start.1 = (f32[1,128]{1,0:T(1,128)S(1)}, f32[1,128]{1,0:T(1,128)S(1)}, u32[]{:S(2)}, u32[]{:S(2)}) collective-permute-start(f32[1,128]{1,0:T(1,128)S(1)} %squares.2.own.rest_0_), channel_id=1, source_target_pairs={{0,4},{2,6},{4,0},{6,2},{8,12},{10,14},{12,8},{14,10},{1,5},{3,7},... | collective-permute-start | bytes 1544 | tf_op jit(solution)/shard_map/ppermute | solution.py:251
  17.6 7.7 %collective-permute-start.3 = (f32[1,128]{1,0:T(1,128)S(1)}, f32[1,128]{1,0:T(1,128)S(1)}, u32[]{:S(2)}, u32[]{:S(2)}) collective-permute-start(f32[1,128]{1,0:T(1,128)S(1)} %squares.3.rest_0_), channel_id=1, source_target_pairs={{0,8},{2,10},{4,12},{6,14},{8,0},{10,2},{12,4},{14,6},{1,9},{3,11}... | collective-permute-start | bytes 1544 | tf_op jit(solution)/shard_map/ppermute | solution.py:251
  20.1 16.3 %collective-permute-start.4 = (bf16[1,64,4096]{2,1,0:T(8,128)(2,1)S(1)}, bf16[1,64,4096]{2,1,0:T(8,128)(2,1)S(1)}, u32[]{:S(2)}, u32[]{:S(2)}) collective-permute-start(bf16[1,64,4096]{2,1,0:T(8,128)(2,1)S(1)} %get-tuple-element.73), channel_id=1, source_target_pairs={{0,2},{2,0},{4,6},{6,4},{8,10},{10,8},{12,14},{14,12},{1,3},{3,1},... | collective-permute-start | bytes 1572872 | tf_op jit(solution)/shard_map/ppermute | solution.py:251
  30.0 14.9 %collective-permute-start.5 = (bf16[2,64,2048]{2,1,0:T(8,128)(2,1)S(1)}, bf16[2,64,2048]{2,1,0:T(8,128)(2,1)S(1)}, u32[]{:S(2)}, u32[]{:S(2)}) collective-permute-start(bf16[2,64,2048]{2,1,0:T(8,128)(2,1)S(1)} %get-tuple-element.75), channel_id=1, source_target_pairs={{0,2},{2,0},{4,6},{6,4},{8,10},{10,8},{12,14},{14,12},{1,3},{3,1},... | collective-permute-start | bytes 1572872 | tf_op jit(solution)/shard_map/ppermute | solution.py:251
  35.8 20.3 %collective-permute-start.7 = (bf16[2,64,2048]{2,1,0:T(8,128)(2,1)S(1)}, bf16[2,64,2048]{2,1,0:T(8,128)(2,1)S(1)}, u32[]{:S(2)}, u32[]{:S(2)}) collective-permute-start(bf16[2,64,2048]{2,1,0:T(8,128)(2,1)S(1)} %get-tuple-element.79), channel_id=1, source_target_pairs={{0,2},{2,0},{4,6},{6,4},{8,10},{10,8},{12,14},{14,12},{1,3},{3,1},... | collective-permute-start | bytes 1572872 | tf_op jit(solution)/shard_map/ppermute | solution.py:251
  45.0 11.2 %collective-permute-start.6 = (bf16[3,32,2048]{2,1,0:T(8,128)(2,1)S(1)}, bf16[3,32,2048]{2,1,0:T(8,128)(2,1)S(1)}, u32[]{:S(2)}, u32[]{:S(2)}) collective-permute-start(bf16[3,32,2048]{2,1,0:T(8,128)(2,1)S(1)} %get-tuple-element.78), channel_id=1, source_target_pairs={{0,4},{2,6},{4,0},{6,2},{8,12},{10,14},{12,8},{14,10},{1,5},{3,7},... | collective-permute-start | bytes 1179656 | tf_op jit(solution)/shard_map/ppermute | solution.py:251
  51.0 23.3 %collective-permute-start.12 = (bf16[2,64,2048]{2,1,0:T(8,128)(2,1)S(1)}, bf16[2,64,2048]{2,1,0:T(8,128)(2,1)S(1)}, u32[]{:S(2)}, u32[]{:S(2)}) collective-permute-start(bf16[2,64,2048]{2,1,0:T(8,128)(2,1)S(1)} %get-tuple-element.88), channel_id=1, source_target_pairs={{0,2},{2,0},{4,6},{6,4},{8,10},{10,8},{12,14},{14,12},{1,3},{3,1},... | collective-permute-start | bytes 1572872 | tf_op jit(solution)/shard_map/ppermute | solution.py:251
  52.5 21.7 %collective-permute-start.2 = (bf16[1,64,3072]{2,1,0:T(8,128)(2,1)S(1)}, bf16[1,64,3072]{2,1,0:T(8,128)(2,1)S(1)}, u32[]{:S(2)}, u32[]{:S(2)}) collective-permute-start(bf16[1,64,3072]{2,1,0:T(8,128)(2,1)S(1)} %get-tuple-element.71), channel_id=1, source_target_pairs={{0,2},{2,0},{4,6},{6,4},{8,10},{10,8},{12,14},{14,12},{1,3},{3,1},... | collective-permute-start | bytes 1179656 | tf_op jit(solution)/shard_map/ppermute | solution.py:251
  56.3 8.3 %collective-permute-start.9 = (bf16[3,16,2048]{2,1,0:T(8,128)(2,1)S(1)}, bf16[3,16,2048]{2,1,0:T(8,128)(2,1)S(1)}, u32[]{:S(2)}, u32[]{:S(2)}) collective-permute-start(bf16[3,16,2048]{2,1,0:T(8,128)(2,1)S(1)} %get-tuple-element.85), channel_id=1, source_target_pairs={{0,8},{2,10},{4,12},{6,14},{8,0},{10,2},{12,4},{14,6},{1,9},{3,11}... | collective-permute-start | bytes 589832 | tf_op jit(solution)/shard_map/ppermute | solution.py:251
  56.8 19.2 %collective-permute-start.11 = (bf16[3,32,2048]{2,1,0:T(8,128)(2,1)S(1)}, bf16[3,32,2048]{2,1,0:T(8,128)(2,1)S(1)}, u32[]{:S(2)}, u32[]{:S(2)}) collective-permute-start(bf16[3,32,2048]{2,1,0:T(8,128)(2,1)S(1)} %get-tuple-element.87), channel_id=1, source_target_pairs={{0,4},{2,6},{4,0},{6,2},{8,12},{10,14},{12,8},{14,10},{1,5},{3,7},... | collective-permute-start | bytes 1179656 | tf_op jit(solution)/shard_map/ppermute | solution.py:251
  64.9 11.2 %collective-permute-start.10 = (bf16[3,16,2048]{2,1,0:T(8,128)(2,1)S(1)}, bf16[3,16,2048]{2,1,0:T(8,128)(2,1)S(1)}, u32[]{:S(2)}, u32[]{:S(2)}) collective-permute-start(bf16[3,16,2048]{2,1,0:T(8,128)(2,1)S(1)} %get-tuple-element.86.refs_4_.own), channel_id=1, source_target_pairs={{0,8},{2,10},{4,12},{6,14},{8,0},{10,2},{12,4},{14,6},{1,9},{3,11}... | collective-permute-start | bytes 589832 | tf_op jit(solution)/shard_map/ppermute | solution.py:251
  74.4 25.1 %collective-permute-start.14 = (bf16[3,32,2048]{2,1,0:T(8,128)(2,1)S(1)}, bf16[3,32,2048]{2,1,0:T(8,128)(2,1)S(1)}, u32[]{:S(2)}, u32[]{:S(2)}) collective-permute-start(bf16[3,32,2048]{2,1,0:T(8,128)(2,1)S(1)} %get-tuple-element.91), channel_id=1, source_target_pairs={{0,4},{2,6},{4,0},{6,2},{8,12},{10,14},{12,8},{14,10},{1,5},{3,7},... | collective-permute-start | bytes 1179656 | tf_op jit(solution)/shard_map/ppermute | solution.py:251
  76.1 23.4 %collective-permute-start.13 = (bf16[3,32,2048]{2,1,0:T(8,128)(2,1)S(1)}, bf16[3,32,2048]{2,1,0:T(8,128)(2,1)S(1)}, u32[]{:S(2)}, u32[]{:S(2)}) collective-permute-start(bf16[3,32,2048]{2,1,0:T(8,128)(2,1)S(1)} %join.8.rest_0_.own), channel_id=1, source_target_pairs={{0,4},{2,6},{4,0},{6,2},{8,12},{10,14},{12,8},{14,10},{1,5},{3,7},... | collective-permute-start | bytes 1179656 | tf_op jit(solution)/shard_map/ppermute | solution.py:251
  76.6 19.1 %collective-permute-start.15 = (bf16[3,16,2048]{2,1,0:T(8,128)(2,1)S(1)}, bf16[3,16,2048]{2,1,0:T(8,128)(2,1)S(1)}, u32[]{:S(2)}, u32[]{:S(2)}) collective-permute-start(bf16[3,16,2048]{2,1,0:T(8,128)(2,1)S(1)} %get-tuple-element.92), channel_id=1, source_target_pairs={{0,8},{2,10},{4,12},{6,14},{8,0},{10,2},{12,4},{14,6},{1,9},{3,11}... | collective-permute-start | bytes 589832 | tf_op jit(solution)/shard_map/ppermute | solution.py:251
  77.2 22.4 %collective-permute-start.8 = (bf16[2,64,1024]{2,1,0:T(8,128)(2,1)S(1)}, bf16[2,64,1024]{2,1,0:T(8,128)(2,1)S(1)}, u32[]{:S(2)}, u32[]{:S(2)}) collective-permute-start(bf16[2,64,1024]{2,1,0:T(8,128)(2,1)S(1)} %get-tuple-element.84), channel_id=1, source_target_pairs={{0,2},{2,0},{4,6},{6,4},{8,10},{10,8},{12,14},{14,12},{1,3},{3,1},... | collective-permute-start | bytes 786440 | tf_op jit(solution)/shard_map/ppermute | solution.py:251
  96.0 9.8 %collective-permute-start.18 = (bf16[3,16,2048]{2,1,0:T(8,128)(2,1)S(1)}, bf16[3,16,2048]{2,1,0:T(8,128)(2,1)S(1)}, u32[]{:S(2)}, u32[]{:S(2)}) collective-permute-start(bf16[3,16,2048]{2,1,0:T(8,128)(2,1)S(1)} %get-tuple-element.94.refs_2_.own), channel_id=1, source_target_pairs={{0,8},{2,10},{4,12},{6,14},{8,0},{10,2},{12,4},{14,6},{1,9},{3,11}... | collective-permute-start | bytes 589832 | tf_op jit(solution)/shard_map/ppermute | solution.py:251
  105.8 22.4 %collective-permute-start.22 = (bf16[3,32,2048]{2,1,0:T(8,128)(2,1)S(1)}, bf16[3,32,2048]{2,1,0:T(8,128)(2,1)S(1)}, u32[]{:S(2)}, u32[]{:S(2)}) collective-permute-start(bf16[3,32,2048]{2,1,0:T(8,128)(2,1)S(1)} %join.10.rest_0_.own), channel_id=1, source_target_pairs={{0,4},{2,6},{4,0},{6,2},{8,12},{10,14},{12,8},{14,10},{1,5},{3,7},... | collective-permute-start | bytes 1179656 | tf_op jit(solution)/shard_map/ppermute | solution.py:251
  105.9 26.7 %collective-permute-start.20 = (bf16[3,64,2048]{2,1,0:T(8,128)(2,1)S(1)}, bf16[3,64,2048]{2,1,0:T(8,128)(2,1)S(1)}, u32[]{:S(2)}, u32[]{:S(2)}) collective-permute-start(bf16[3,64,2048]{2,1,0:T(8,128)(2,1)S(1)} %join.9.refs_4_.own), channel_id=1, source_target_pairs={{0,2},{2,0},{4,6},{6,4},{8,10},{10,8},{12,14},{14,12},{1,3},{3,1},... | collective-permute-start | bytes 2359304 | tf_op jit(solution)/shard_map/ppermute | solution.py:251
  106.0 13.7 %collective-permute-start.17 = (bf16[3,16,2048]{2,1,0:T(8,128)(2,1)S(1)}, bf16[3,16,2048]{2,1,0:T(8,128)(2,1)S(1)}, u32[]{:S(2)}, u32[]{:S(2)}) collective-permute-start(bf16[3,16,2048]{2,1,0:T(8,128)(2,1)S(1)} %get-tuple-element.98), channel_id=1, source_target_pairs={{0,8},{2,10},{4,12},{6,14},{8,0},{10,2},{12,4},{14,6},{1,9},{3,11}... | collective-permute-start | bytes 589832 | tf_op jit(solution)/shard_map/ppermute | solution.py:251
  108.9 19.3 %collective-permute-start.16 = (bf16[3,32,1024]{2,1,0:T(8,128)(2,1)S(1)}, bf16[3,32,1024]{2,1,0:T(8,128)(2,1)S(1)}, u32[]{:S(2)}, u32[]{:S(2)}) collective-permute-start(bf16[3,32,1024]{2,1,0:T(8,128)(2,1)S(1)} %get-tuple-element.97), channel_id=1, source_target_pairs={{0,4},{2,6},{4,0},{6,2},{8,12},{10,14},{12,8},{14,10},{1,5},{3,7},... | collective-permute-start | bytes 589832 | tf_op jit(solution)/shard_map/ppermute | solution.py:251
  119.9 8.5 %collective-permute-start.21 = (bf16[3,16,2048]{2,1,0:T(8,128)(2,1)S(1)}, bf16[3,16,2048]{2,1,0:T(8,128)(2,1)S(1)}, u32[]{:S(2)}, u32[]{:S(2)}) collective-permute-start(bf16[3,16,2048]{2,1,0:T(8,128)(2,1)S(1)} %get-tuple-element.100.refs_2_.own), channel_id=1, source_target_pairs={{0,8},{2,10},{4,12},{6,14},{8,0},{10,2},{12,4},{14,6},{1,9},{3,11}... | collective-permute-start | bytes 589832 | tf_op jit(solution)/shard_map/ppermute | solution.py:251
  128.3 23.6 %collective-permute-start.26 = (bf16[3,64,2048]{2,1,0:T(8,128)(2,1)S(1)}, bf16[3,64,2048]{2,1,0:T(8,128)(2,1)S(1)}, u32[]{:S(2)}, u32[]{:S(2)}) collective-permute-start(bf16[3,64,2048]{2,1,0:T(8,128)(2,1)S(1)} %join.11.rest_0_.own), channel_id=1, source_target_pairs={{0,2},{2,0},{4,6},{6,4},{8,10},{10,8},{12,14},{14,12},{1,3},{3,1},... | collective-permute-start | bytes 2359304 | tf_op jit(solution)/shard_map/ppermute | solution.py:251
  128.4 15.3 %collective-permute-start.24 = (bf16[3,32,2048]{2,1,0:T(8,128)(2,1)S(1)}, bf16[3,32,2048]{2,1,0:T(8,128)(2,1)S(1)}, u32[]{:S(2)}, u32[]{:S(2)}) collective-permute-start(bf16[3,32,2048]{2,1,0:T(8,128)(2,1)S(1)} %join.12.rest_0_.own), channel_id=1, source_target_pairs={{0,4},{2,6},{4,0},{6,2},{8,12},{10,14},{12,8},{14,10},{1,5},{3,7},... | collective-permute-start | bytes 1179656 | tf_op jit(solution)/shard_map/ppermute | solution.py:251
  130.4 12.6 %collective-permute-start.19 = (bf16[3,16,1024]{2,1,0:T(8,128)(2,1)S(1)}, bf16[3,16,1024]{2,1,0:T(8,128)(2,1)S(1)}, u32[]{:S(2)}, u32[]{:S(2)}) collective-permute-start(bf16[3,16,1024]{2,1,0:T(8,128)(2,1)S(1)} %get-tuple-element.102), channel_id=1, source_target_pairs={{0,8},{2,10},{4,12},{6,14},{8,0},{10,2},{12,4},{14,6},{1,9},{3,11}... | collective-permute-start | bytes 294920 | tf_op jit(solution)/shard_map/ppermute | solution.py:251
  143.7 20.4 %collective-permute-start.28 = (bf16[3,64,2048]{2,1,0:T(8,128)(2,1)S(1)}, bf16[3,64,2048]{2,1,0:T(8,128)(2,1)S(1)}, u32[]{:S(2)}, u32[]{:S(2)}) collective-permute-start(bf16[3,64,2048]{2,1,0:T(8,128)(2,1)S(1)} %join.13.rest_0_.own), channel_id=1, source_target_pairs={{0,2},{2,0},{4,6},{6,4},{8,10},{10,8},{12,14},{14,12},{1,3},{3,1},... | collective-permute-start | bytes 2359304 | tf_op jit(solution)/shard_map/ppermute | solution.py:251
  145.4 6.4 %collective-permute-start.23 = (bf16[3,16,1152]{2,1,0:T(8,128)(2,1)S(1)}, bf16[3,16,1152]{2,1,0:T(8,128)(2,1)S(1)}, u32[]{:S(2)}, u32[]{:S(2)}) collective-permute-start(bf16[3,16,1152]{2,1,0:T(8,128)(2,1)S(1)} %get-tuple-element.106.rest_0_.own), channel_id=1, source_target_pairs={{0,8},{2,10},{4,12},{6,14},{8,0},{10,2},{12,4},{14,6},{1,9},{3,11}... | collective-permute-start | bytes 331784 | tf_op jit(solution)/shard_map/ppermute | solution.py:251
  151.8 11.8 %collective-permute-start.25 = (bf16[3,32,1152]{2,1,0:T(8,128)(2,1)S(1)}, bf16[3,32,1152]{2,1,0:T(8,128)(2,1)S(1)}, u32[]{:S(2)}, u32[]{:S(2)}) collective-permute-start(bf16[3,32,1152]{2,1,0:T(8,128)(2,1)S(1)} %join.14.rest_4_.own), channel_id=1, source_target_pairs={{0,4},{2,6},{4,0},{6,2},{8,12},{10,14},{12,8},{14,10},{1,5},{3,7},... | collective-permute-start | bytes 663560 | tf_op jit(solution)/shard_map/ppermute | solution.py:251
  163.6 12.3 %collective-permute-start.27 = (bf16[3,64,1152]{2,1,0:T(8,128)(2,1)S(1)}, bf16[3,64,1152]{2,1,0:T(8,128)(2,1)S(1)}, u32[]{:S(2)}, u32[]{:S(2)}) collective-permute-start(bf16[3,64,1152]{2,1,0:T(8,128)(2,1)S(1)} %join.15.rest_4_.own), channel_id=1, source_target_pairs={{0,2},{2,0},{4,6},{6,4},{8,10},{10,8},{12,14},{14,12},{1,3},{3,1},... | collective-permute-start | bytes 1327112 | tf_op jit(solution)/shard_map/ppermute | solution.py:251
  182.2 2.8 %collective-permute-start.29 = (f32[264,1024]{1,0:T(8,128)S(1)}, f32[264,1024]{1,0:T(8,128)S(1)}, u32[]{:S(2)}, u32[]{:S(2)}) collective-permute-start(f32[264,1024]{1,0:T(8,128)S(1)} %get-tuple-element.118.own), channel_id=1, source_target_pairs={{0,1},{1,0},{2,3},{3,2},{4,5},{5,4},{6,7},{7,6},{8,9},{9,8},{10,11... | collective-permute-start | bytes 3244040 | tf_op jit(solution)/shard_map/ppermute | solution.py:255
  (5 other events, 33.2 us)

commit v3 on v2

v3 whole, which is shorter than its diff:
```python
import functools

import jax
import jax.numpy as jnp
from jax import lax
from jax.experimental import pallas as pl
from jax.experimental.pallas import tpu as pltpu
from jax.sharding import PartitionSpec as P

EPS = 1e-05
BF16 = jnp.bfloat16
F32 = jnp.float32
COUNTS = (2, 2, 2, 1)
SWAPPED = (False, False, False, False)
ORDER = (
    ("F", 1),
    ("H", 0, 0),
    ("F", 2),
    ("H", 0, 1),
    ("H", 1, 0),
    ("F", 3),
    ("W", 0),
    ("J", 0, 2),
    ("H", 1, 1),
    ("H", 2, 0),
    ("J", 0, 1),
    ("W", 1),
    ("J", 1, 2),
    ("H", 2, 1),
    ("H", 3, 0),
    ("W", 2),
    ("H", 3, 1),
    ("J", 1, 1),
    ("J", 2, 2),
    ("B", 0),
    ("W", 3),
    ("J", 2, 1),
    ("J", 3, 2),
    ("B", 1),
    ("J", 3, 1),
    ("B", 2),
    ("B", 3),
)
COSTS = (0,) * len(ORDER)
START_MIB, FORE_MIB, BACK_MIB = 44, 44, 44
NN = (((1,), (0,)), ((), ()))
NT = (((1,), (1,)), ((), ()))
TN = (((0,), (0,)), ((), ()))
VMEM = pl.BlockSpec(memory_space=pltpu.VMEM)
SMEM = pl.BlockSpec(memory_space=pltpu.SMEM)
ANY = pl.BlockSpec(memory_space=pl.ANY)


def cost(flops, nbytes):
    return pl.CostEstimate(flops=int(flops), bytes_accessed=int(nbytes), transcendentals=0)


def params(mib):
    return pltpu.CompilerParams(vmem_limit_bytes=mib * 1024 * 1024)


def matmul(a, b, dims=NN):
    return lax.dot_general(a, b, dims, preferred_element_type=F32)


def order(label, tokens, block):
    p = lax.broadcasted_iota(jnp.int32, (tokens, tokens), 0)
    t = lax.broadcasted_iota(jnp.int32, (tokens, tokens), 1)
    return ((p // block) ^ label) * block + p % block == t


def split_rows(part, swapped):
    half = part.shape[0] // 2
    if not swapped:
        return part[:half], part[half:]
    q = half // 2
    return (
        jnp.concatenate([part[:q], part[half : half + q]], axis=0),
        jnp.concatenate([part[q:half], part[half + q :]], axis=0),
    )


def join_rows(own, other, swapped):
    if not swapped:
        return jnp.concatenate([own, other], axis=0)
    q = own.shape[0] // 2
    return jnp.concatenate([own[:q], other[:q], own[q:], other[q:]], axis=0)


def start_kernel(block, span, tile, swapped, label, ids, excluded, gain, store, grad_out, w_down, w_gate, w_up, *rest):
    rows, dout, scaled, flipped, keep, send, pool_buf, grad_buf, wd, wg, wu, sems, w_sems = rest
    copies = [
        pltpu.make_async_copy(store, pool_buf, sems.at[0]),
        pltpu.make_async_copy(grad_out, grad_buf, sems.at[1]),
    ]
    w_copies = []
    for at in range(0, span[1], tile):
        there, here = pl.ds(span[0] + at, tile), pl.ds(at, tile)
        n = len(w_copies)
        w_copies.append(pltpu.make_async_copy(w_down.at[there], wd.at[here], w_sems.at[n]))
        w_copies.append(pltpu.make_async_copy(w_gate.at[:, there], wg.at[:, here], w_sems.at[n + 1]))
        w_copies.append(pltpu.make_async_copy(w_up.at[:, there], wu.at[:, here], w_sems.at[n + 2]))
    for copy in copies + w_copies:
        copy.start()
    tokens = grad_buf.shape[0]
    pool = pool_buf.shape[0]
    perm = jnp.where(order(label[0], tokens, block), 1.0, 0.0).astype(BF16)
    position = lax.broadcasted_iota(jnp.int32, (tokens, excluded.shape[1]), 0)
    match = jnp.where(position == excluded[...], 1.0, 0.0)
    dropped = jnp.max(match, axis=1, keepdims=True) > 0.0
    hit = lax.broadcasted_iota(jnp.int32, (pool, tokens), 0) == ids[...]
    hit = jnp.where(hit, 1.0, 0.0).astype(BF16)
    copies[0].wait()
    natural = matmul(hit, pool_buf[...], TN)
    row = matmul(perm, natural.astype(BF16))
    squares = jnp.broadcast_to(jnp.sum(row * row, axis=1, keepdims=True), (tokens, 128))
    put_pieces(*split_rows(squares, swapped), keep, send, span[1])
    rows[...] = row.astype(BF16)
    value = (row * gain[...]).astype(BF16)
    scaled[...] = value
    flipped[...] = jnp.transpose(value.astype(F32)).astype(BF16)
    copies[1].wait()
    kept = jnp.where(dropped, 0.0, grad_buf[...].astype(F32)).astype(BF16)
    dout[...] = matmul(perm, kept).astype(BF16)
    for n, copy in enumerate(w_copies):
        copy.wait()
        k = n % 3
        here = slice(n // 3 * tile, (n // 3 + 1) * tile)
        part = matmul(dout[...], wd[here], NT) if k == 0 else matmul(scaled[...], (wg if k == 1 else wu)[:, here])
        kept, sent = split_rows(part, swapped)
        keep[k, :, here] = kept
        send[k, :, here] = sent.astype(BF16)


def put_pieces(kept, sent, keep, send, at):
    for k in range(3):
        keep[k, :, at:] = kept if k == 0 else jnp.zeros_like(kept)
        piece = sent.astype(BF16)
        send[k, :, at:] = piece
        sent = sent - piece.astype(F32)


def fore_kernel(swapped, refs, keep, send):
    for k, (x, w, dims) in enumerate(refs):
        kept, sent = split_rows(matmul(x[...], w[...], dims), swapped)
        keep[k] = kept
        send[k] = sent.astype(BF16)


def all_kernel(swapped, normed, dout, w_down, w_gate, w_up, *rest):
    fore_kernel(swapped, [(dout, w_down, NT), (normed, w_gate, NN), (normed, w_up, NN)], *rest[-2:])


def halve_kernel(part, kept, received, *rest):
    keep, send = rest[-2:]
    rows = keep.shape[1]
    for k in range(3):
        total = kept[k, :, :part] + received[k, :, :part].astype(F32)
        keep[k, :, :part] = total[:rows]
        send[k, :, :part] = total[rows:].astype(BF16)
    if keep.shape[2] > part:
        total = sum(kept[k, :, part:] + received[k, :, part:].astype(F32) for k in range(3))
        put_pieces(total[:rows], total[rows:], keep, send, part)


def swiglu_kernel(part, last, width, kept, received, inner, inv_rms, *rest):
    acts, inner_out, inv_out = rest[-3:]
    d_hidden, gate_pre, up_proj = (kept[k, :, :part] + received[k, :, :part].astype(F32) for k in range(3))
    if kept.shape[2] > part:
        squares = sum(kept[k, :, part:] + received[k, :, part:].astype(F32) for k in range(3))
        inv = lax.rsqrt(squares / width + EPS)
    else:
        inv = inv_rms[...]
    inv_out[...] = inv
    inv = inv[:, :1]
    gate_pre = gate_pre * inv
    up_proj = up_proj * inv
    sigmoid_gate = jax.nn.sigmoid(gate_pre)
    silu = gate_pre * sigmoid_gate
    d_scaled = d_hidden * inv
    d_gate = (d_scaled * up_proj * sigmoid_gate * (1.0 + gate_pre * (1.0 - sigmoid_gate))).astype(BF16)
    d_up = (d_scaled * silu).astype(BF16)
    acts[0, :, :part] = (silu * up_proj).astype(BF16)
    acts[1, :, :part] = d_gate
    acts[2, :, :part] = d_up
    terms = d_gate.astype(F32) * gate_pre + d_up.astype(F32) * up_proj
    total = inner[...] + jnp.broadcast_to(inv * jnp.sum(terms, axis=1, keepdims=True), inner.shape)
    inner_out[...] = total
    if last:
        for k in range(3):
            piece = total.astype(BF16)
            acts[k, :, part:] = piece
            total = total - piece.astype(F32)


def join_kernel(own, other, *rest):
    rows = own.shape[1]
    out = rest[-1]
    out[:, :rows] = own[...]
    out[:, rows:] = other[...]


def back_kernel(first, last, swapped, own, other, flipped, dout, w_gate, w_up, w_down, *rest):
    acc, gate_grad, up_grad, down_grad = rest[-4:]
    tokens = dout.shape[0]
    step = pl.program_id(0)

    @pl.when(step == 0)
    def _():
        acc[...] = jnp.zeros_like(acc) if first else rest[0][...]

    hidden, d_gate, d_up = (join_rows(own[k], other[k], swapped) for k in range(3))
    gate_grad[...] = matmul(flipped[...], d_gate).astype(BF16)
    up_grad[...] = matmul(flipped[...], d_up).astype(BF16)
    down_grad[...] = matmul(hidden, dout[...], TN).astype(BF16)
    acc[:tokens] += matmul(hidden, w_down[...])
    acc[tokens : 2 * tokens] += matmul(d_gate, w_gate[...], NT) + matmul(d_up, w_up[...], NT)
    if last:

        @pl.when(step == 0)
        def _():
            places = 0 if first else 4
            pieces = [sum(x[k].astype(F32) for k in range(3)) for x in rest[places : places + 2]]
            inner = jnp.transpose(join_rows(*pieces, swapped))[:8]
            acc[2 * tokens :, :tokens] = inner


def end_kernel(block, width, label, own, other, rows, dout, gain, ids, output, store_grad, gain_grad):
    tokens = rows.shape[0]
    pool = store_grad.shape[0]
    places = order(label[0], tokens, block)
    perm = jnp.where(places, 1.0, 0.0).astype(BF16)
    here = lax.broadcasted_iota(jnp.int32, (tokens, tokens), 0) == lax.broadcasted_iota(jnp.int32, (tokens, tokens), 1)
    inner = own[2 * tokens : 2 * tokens + 1, :tokens] + other[2 * tokens : 2 * tokens + 1, :tokens]
    inner = jnp.sum(jnp.where(here, inner, 0.0), axis=1, keepdims=True)
    row = rows[...].astype(F32)
    result = (row + (own[:tokens] + other[:tokens])).astype(BF16)
    output[...] = matmul(perm, result, TN).astype(BF16)
    d_normed = own[tokens : 2 * tokens] + other[tokens : 2 * tokens]
    gain_grad[...] = jnp.sum(d_normed * row, axis=0, keepdims=True)
    d_rows = dout[...].astype(F32) + d_normed * gain[...] - row * (inner / width)
    hit = lax.broadcasted_iota(jnp.int32, (pool, tokens), 0) == ids[...]
    target = matmul(jnp.where(hit, 1.0, 0.0).astype(BF16), perm, NT).astype(BF16)
    total = jnp.zeros(store_grad.shape, F32)
    for _ in range(3):
        piece = d_rows.astype(BF16)
        total += matmul(target, piece)
        d_rows = d_rows - piece.astype(F32)
    store_grad[...] = total.astype(BF16)


def shards(sizes, replay_store, replay_ids, excluded, norm_gain, w_gate, w_up, w_down, grad_out):
    ways = sizes["width"]
    steps = ways.bit_length() - 1
    tokens, d_here = grad_out.shape
    ff = w_down.shape[0]
    width = ways * d_here
    block = tokens // ways
    half = tokens // 2
    pool = replay_store.shape[0]
    tile = ff // sum(COUNTS)
    shape = jax.ShapeDtypeStruct

    index = lax.axis_index("width")
    label = sum(((index >> s) & 1) << (steps - 1 - s) for s in range(steps))
    label = jnp.reshape(label, (1,)).astype(jnp.int32)

    def swap(x, step):
        return lax.ppermute(x, "width", [(i, i ^ (1 << step)) for i in range(ways)])

    def swap_cores(x):
        n = sizes["hidden"]
        return lax.ppermute(x, "hidden", [(i, (i + 1) % n) for i in range(n)])

    ids = replay_ids.reshape(1, tokens)
    gain = norm_gain.reshape(1, d_here)
    routes = [[1, 0, *range(2, steps)] if swapped else list(range(steps)) for swapped in SWAPPED]
    chunks = len(COUNTS)
    parts = [count * tile for count in COUNTS]
    firsts = [sum(parts[:j]) for j in range(chunks)]
    token, held, arrived = [], [], {}

    state = {"cost": 0}

    def kernel(body, out_shape, in_specs, out_specs, ins, name, mib=24, **more):
        after = token[-1:] + held
        held.clear()
        outs = pl.pallas_call(
            body,
            out_shape=out_shape,
            in_specs=list(in_specs) + [ANY] * len(after),
            out_specs=out_specs,
            compiler_params=params(mib),
            cost_estimate=cost(0, 1e6 * state["cost"]),
            name=name,
            **more,
        )(*ins, *after)
        token.append(outs[0])
        return outs

    part = parts[0]
    side = pltpu.VMEM((d_here, part), BF16)
    rows, dout, scaled, flipped, keep, send = kernel(
        functools.partial(start_kernel, block, (firsts[0], part), tile, SWAPPED[0]),
        (
            shape((tokens, d_here), BF16),
            shape((tokens, d_here), BF16),
            shape((tokens, d_here), BF16),
            shape((d_here, tokens), BF16),
            shape((3, half, part + 128), F32),
            shape((3, half, part + 128), BF16),
        ),
        [SMEM, VMEM, VMEM, VMEM] + [ANY] * 5,
        (VMEM,) * 6,
        [label, ids, excluded.reshape(1, -1), gain, replay_store, grad_out, w_down, w_gate, w_up],
        "start",
        mib=START_MIB,
        scratch_shapes=[
            pltpu.VMEM((pool, d_here), BF16),
            pltpu.VMEM((tokens, d_here), BF16),
            pltpu.VMEM((part, d_here), BF16),
            side,
            side,
            pltpu.SemaphoreType.DMA((2,)),
            pltpu.SemaphoreType.DMA((3 * COUNTS[0],)),
        ],
    )
    zeros = jnp.zeros((block, 128), F32)
    state |= {"inner": zeros, "inv": zeros, "acc": None, "grads": None, "swiglu": 0, "back": 0}
    arrived["F", 0] = swap(send, routes[0][0])
    sums, acts, others = {0: (keep, arrived["F", 0])}, {}, {}

    def fore(j):
        part = parts[j]
        whole = pl.BlockSpec((tokens, d_here), lambda i: (0, 0))
        col = pl.BlockSpec((d_here, tile), lambda i: (0, firsts[j] // tile + i))
        row = pl.BlockSpec((tile, d_here), lambda i: (firsts[j] // tile + i, 0))
        n = 3
        out = pl.BlockSpec((n, half, tile), lambda i: (0, 0, i))
        keep, send = kernel(
            functools.partial(all_kernel, SWAPPED[j]),
            (shape((n, half, part), F32), shape((n, half, part), BF16)),
            [whole, whole, row, col, col],
            (out, out),
            [scaled, dout, w_down, w_gate, w_up],
            "fore",
            mib=FORE_MIB,
            grid=(COUNTS[j],),
        )
        arrived["F", j] = swap(send, routes[j][0])
        sums[j] = keep, arrived["F", j]

    def halve(j, at):
        for step in range(at, steps - 1 if at else 1):
            kept, received = sums[j]
            here = (3, kept.shape[1] // 2, kept.shape[2])
            keep, send = kernel(
                functools.partial(halve_kernel, parts[j]),
                (shape(here, F32), shape(here, BF16)),
                [VMEM, VMEM],
                (VMEM, VMEM),
                [kept, received],
                "halve",
            )
            arrived["H", j, at] = swap(send, routes[j][step + 1])
            sums[j] = keep, arrived["H", j, at]

    def swiglu(j):
        state["swiglu"] += 1
        last = state["swiglu"] == chunks
        state["last"] = j if last else None
        acts[j], state["inner"], state["inv"] = kernel(
            functools.partial(swiglu_kernel, parts[j], last, width),
            (shape((3, block, parts[j] + (128 if last else 0)), BF16), shape((block, 128), F32), shape((block, 128), F32)),
            [VMEM] * 4,
            (VMEM,) * 3,
            [*sums[j], state["inner"], state["inv"]],
            "swiglu",
        )
        others[j] = arrived["W", j] = swap(acts[j], routes[j][steps - 1])

    def join(j, at):
        for step in reversed(range(at, steps if at > 1 else 2)):
            own, other = acts[j], others[j]
            if own.shape[1] % 16:
                acts[j] = jnp.concatenate([own, other], axis=1)
            else:
                (acts[j],) = kernel(
                    join_kernel,
                    (shape((3, 2 * own.shape[1], own.shape[2]), BF16),),
                    [VMEM, VMEM],
                    (VMEM,),
                    [own, other],
                    "join",
                )
            others[j] = arrived["J", j, at] = swap(acts[j], routes[j][step - 1])

    def back(j):
        state["back"] += 1
        first, last = state["back"] == 1, j == state["last"]
        own, other = acts[j], others[j]
        start = firsts[j] // tile
        col = pl.BlockSpec((d_here, tile), lambda i: (0, start + i))
        row = pl.BlockSpec((tile, d_here), lambda i: (start + i, 0))
        whole = lambda i: (0, 0)
        acc_spec = pl.BlockSpec((2 * tokens + 8, d_here), whole)
        piece = pl.BlockSpec((3, half, tile), lambda i: (0, 0, i))
        ins = [own, other, flipped, dout, w_gate, w_up, w_down]
        specs = [
            piece,
            piece,
            pl.BlockSpec((d_here, tokens), whole),
            pl.BlockSpec((tokens, d_here), whole),
            col,
            col,
            row,
        ]
        alias = {}
        if not first:
            ins += [state["acc"], *state["grads"]]
            specs += [acc_spec, ANY, ANY, ANY]
            alias = {8: 1, 9: 2, 10: 3}
        if last:
            extra = pl.BlockSpec((3, half, 128), lambda i: (0, 0, parts[j] // 128))
            ins += [own, other]
            specs += [extra, extra]
        state["acc"], *state["grads"] = kernel(
            functools.partial(back_kernel, first, last, SWAPPED[j]),
            (
                shape((2 * tokens + 8, d_here), F32),
                shape((d_here, ff), BF16),
                shape((d_here, ff), BF16),
                shape((ff, d_here), BF16),
            ),
            specs,
            (acc_spec, col, col, row),
            ins,
            "back",
            mib=BACK_MIB,
            grid=(COUNTS[j],),
            input_output_aliases=alias,
        )

    tasks = {"F": fore, "H": halve, "W": swiglu, "J": join, "B": back}
    for (task, *where), state["cost"] in zip(ORDER, COSTS):
        if task == "A":
            held.append(arrived[tuple(where)])
        else:
            tasks[task](*where)
    acc, grads = state["acc"], state["grads"]

    other = swap_cores(acc)
    output, store_grad, gain_grad = pl.pallas_call(
        functools.partial(end_kernel, block, width),
        out_shape=(shape((tokens, d_here), BF16), shape((pool, d_here), BF16), shape((1, d_here), F32)),
        in_specs=[SMEM] + [VMEM] * 6,
        out_specs=(VMEM, VMEM, VMEM),
        compiler_params=params(32),
        cost_estimate=cost(2 * tokens * pool * d_here, 16 * tokens * d_here),
        name="end",
    )(label, acc, other, rows, dout, gain, ids)
    return (output, store_grad, gain_grad.reshape(d_here), *grads)


def solution(mesh):
    return jax.shard_map(
        functools.partial(shards, dict(mesh.shape)),
        mesh=mesh,
        in_specs=(
            P("groups", "width"),
            P("groups"),
            P("groups"),
            P("width"),
            P("width", "hidden"),
            P("width", "hidden"),
            P("hidden", "width"),
            P("groups", "width"),
        ),
        out_specs=(
            P("groups", "width"),
            P("groups", "width"),
            P(("groups", "width")),
            P(("groups", "width"), "hidden"),
            P(("groups", "width"), "hidden"),
            P(("groups", "hidden"), "width"),
        ),
        check_vma=False,
    )
```

time: 187 us -> 178 us (0.952)
  Pallas kernels: 73.2 us -> 66.5 us
  waiting for transfers between devices: 72 us -> 67.4 us
  local copies, waits for them, and re-layouts: 1.92 us -> 3.99 us
    pallas_call x34 -> x28, Pallas kernels: 71.5 us -> 64.8 us  [kernel(): pl.pallas_call(body, out_shape=out_shape, in_specs=list(in_specs) + [ANY]...]
    ppermute x29 -> x24, waiting for transfers between devices: 69.3 us -> 64.7 us  [swap(): return lax.ppermute(x, 'width', [(i, i ^ 1 << step) for i in range(ways)])]
    unnamed x14, local copies, waits for them, and re-layouts: 1.92 us -> 3.99 us
    ppermute x29 -> x24, starting transfers between devices: 38.5 us -> 39.1 us  [swap(): return lax.ppermute(x, 'width', [(i, i ^ 1 << step) for i in range(ways)])]
  transfers between devices with their start and end apart: 30 -> 25, of which waited for: 11 -> 12; matrix products, arithmetic and copies ran while one was open for 0% -> 0% of each run, Pallas kernels for 33% -> 30%
where the time goes in v3:
time: 178 us
  waiting for transfers between devices  67.4 us (38%)
  Pallas kernels  66.5 us (37%)
  starting transfers between devices  39.2 us (22%)
  local copies, waits for them, and re-layouts  3.99 us (2%)
    pallas_call x28, Pallas kernels, kernel(): pl.pallas_call(body, out_shape=out_shape, in_specs=list(in_specs) + [ANY]...  64.8 us
    ppermute x24, waiting for transfers between devices, swap(): return lax.ppermute(x, 'width', [(i, i ^ 1 << step) for i in range(ways)])  64.7 us
    ppermute x24, starting transfers between devices, swap(): return lax.ppermute(x, 'width', [(i, i ^ 1 << step) for i in range(ways)])  39.1 us
    unnamed x14, local copies, waits for them, and re-layouts  3.99 us
  transfers between devices with their start and end apart: 25, of which 12 were waited for; matrix products, arithmetic and copies ran while one was open for 0% of the time, Pallas kernels for 30%

profile of v3, /device:TPU:0, one launch (start us, length us, event | category | flops | bytes accessed | tf_op | source)
XLA Modules:
  0.0 177.9 jit_solution(1518578081012665370)
XLA Ops:
  4.6 5.3 %start.1 = (bf16[128,1024]{1,0:T(8,128)(2,1)S(1)}, bf16[128,1024]{1,0:T(8,128)(2,1)S(1)}, bf16[128,1024]{1,0:T(8,128)(2,1)S(1)}, bf16[1024,128]{1,0:T(8,128)(2,1...) custom-call(s32[1]{0:T(128)} %bitcast.label, s32[1,128]{1,0:T(1,128)S(1)} %bitcast.7, ...), custom_call_target="tpu_custom_call" | custom-call | tf_op jit(solution)/shard_map/start/pallas_call | solution.py:288
  10.0 3.0 %collective-permute-start.1 = (bf16[3,64,2176]{2,1,0:T(8,128)(2,1)S(1)}, bf16[3,64,2176]{2,1,0:T(8,128)(2,1)S(1)}, u32[]{:S(2)}, u32[]{:S(2)}) collective-permute-start(bf16[3,64,2176]{2,1,0:T(8,128)(2,1)S(1)} %get-tuple-element.69), channel_id=1, source_target_pairs={{0,2},{2,0},{4,6},{6,4},{8,10},{10,8},{12,14},{14,12},{1,3},{3,1},... | collective-permute-start | bytes 2506760 | tf_op jit(solution)/shard_map/ppermute | solution.py:269
  13.0 6.2 %fore.3 = (f32[3,64,2048]{2,1,0:T(8,128)S(1)}, bf16[3,64,2048]{2,1,0:T(8,128)(2,1)S(1)}) custom-call(bf16[128,1024]{1,0:T(8,128)(2,1)S(1)} %get-tuple-element.63.normed, bf16[128,1024]{1,0:T(8,128)(2,1)S(1)} %get-tuple-element.64.dout, bf16[7168,1024]{1,0:T(8,128)(2,1)} %w_down.15, bf16[1024,7168]{1,0:T(8,128)(2,1)} %w_gate.15, bf16[1024,7168]{1,0:T(8,128)(2,1)} %w_up.15, ...), custom_call_target="tpu_custom_call" | custom-call | tf_op jit(solution)/shard_map/fore/pallas_call | solution.py:288
  19.3 13.1 %collective-permute-done.1.received = bf16[3,64,2176]{2,1,0:T(8,128)(2,1)S(1)} collective-permute-done((bf16[3,64,2176]{2,1,0:T(8,128)(2,1)S(1)}, bf16[3,64,2176]{2,1,0:T(8,128)(2,1)S(1)}, u32[]{:S(2)}, u32[]{:S(2)}) %collective-permute-start.1) | collective-permute-done | bytes 835616 | tf_op jit(solution)/shard_map/ppermute | solution.py:269
  32.6 2.2 %collective-permute-start.2 = (bf16[3,32,2176]{2,1,0:T(8,128)(2,1)S(1)}, bf16[3,32,2176]{2,1,0:T(8,128)(2,1)S(1)}, u32[]{:S(2)}, u32[]{:S(2)}) collective-permute-start(bf16[3,32,2176]{2,1,0:T(8,128)(2,1)S(1)} %get-tuple-element.71), channel_id=1, source_target_pairs={{0,4},{2,6},{4,0},{6,2},{8,12},{10,14},{12,8},{14,10},{1,5},{3,7},... | collective-permute-start | bytes 1253384 | tf_op jit(solution)/shard_map/ppermute | solution.py:269
  34.8 6.2 %fore.4 = (f32[3,64,2048]{2,1,0:T(8,128)S(1)}, bf16[3,64,2048]{2,1,0:T(8,128)(2,1)S(1)}) custom-call(bf16[128,1024]{1,0:T(8,128)(2,1)S(1)} %get-tuple-element.63.normed, bf16[128,1024]{1,0:T(8,128)(2,1)S(1)} %get-tuple-element.64.dout, bf16[7168,1024]{1,0:T(8,128)(2,1)} %w_down.15, bf16[1024,7168]{1,0:T(8,128)(2,1)} %w_gate.15, bf16[1024,7168]{1,0:T(8,128)(2,1)} %w_up.15, ...), custom_call_target="tpu_custom_call" | custom-call | tf_op jit(solution)/shard_map/fore/pallas_call | solution.py:288
  42.7 3.0 %collective-permute-start.6 = (bf16[3,16,2176]{2,1,0:T(8,128)(2,1)S(1)}, bf16[3,16,2176]{2,1,0:T(8,128)(2,1)S(1)}, u32[]{:S(2)}, u32[]{:S(2)}) collective-permute-start(bf16[3,16,2176]{2,1,0:T(8,128)(2,1)S(1)} %get-tuple-element.79), channel_id=1, source_target_pairs={{0,8},{2,10},{4,12},{6,14},{8,0},{10,2},{12,4},{14,6},{1,9},{3,11}... | collective-permute-start | bytes 626696 | tf_op jit(solution)/shard_map/ppermute | solution.py:269
  45.7 3.6 %collective-permute-done.received = bf16[3,64,2048]{2,1,0:T(8,128)(2,1)S(1)} collective-permute-done((bf16[3,64,2048]{2,1,0:T(8,128)(2,1)S(1)}, bf16[3,64,2048]{2,1,0:T(8,128)(2,1)S(1)}, u32[]{:S(2)}, u32[]{:S(2)}) %collective-permute-start) | collective-permute-done | bytes 786464 | tf_op jit(solution)/shard_map/ppermute | solution.py:269
  49.4 4.3 %fore.5 = (f32[3,64,1024]{2,1,0:T(8,128)S(1)}, bf16[3,64,1024]{2,1,0:T(8,128)(2,1)S(1)}) custom-call(bf16[128,1024]{1,0:T(8,128)(2,1)S(1)} %get-tuple-element.63.normed, bf16[128,1024]{1,0:T(8,128)(2,1)S(1)} %get-tuple-element.64.dout, bf16[7168,1024]{1,0:T(8,128)(2,1)} %w_down.15, bf16[1024,7168]{1,0:T(8,128)(2,1)} %w_gate.15, bf16[1024,7168]{1,0:T(8,128)(2,1)} %w_up.15, ...), custom_call_target="tpu_custom_call" | custom-call | tf_op jit(solution)/shard_map/fore/pallas_call | solution.py:288
  54.0 3.2 %collective-permute-start.7 = (bf16[3,16,2048]{2,1,0:T(8,128)(2,1)S(1)}, bf16[3,16,2048]{2,1,0:T(8,128)(2,1)S(1)}, u32[]{:S(2)}, u32[]{:S(2)}) collective-permute-start(bf16[3,16,2048]{2,1,0:T(8,128)(2,1)S(1)} %get-tuple-element.80.own.rest_0_), channel_id=1, source_target_pairs={{0,8},{2,10},{4,12},{6,14},{8,0},{10,2},{12,4},{14,6},{1,9},{3,11}... | collective-permute-start | bytes 589832 | tf_op jit(solution)/shard_map/ppermute | solution.py:269
  57.2 1.6 collective-permute-start.5
  58.8 5.7 %collective-permute-done.7.other = bf16[3,16,2048]{2,1,0:T(8,128)(2,1)S(1)} collective-permute-done((bf16[3,16,2048]{2,1,0:T(8,128)(2,1)S(1)}, bf16[3,16,2048]{2,1,0:T(8,128)(2,1)S(1)}, u32[]{:S(2)}, u32[]{:S(2)}) %collective-permute-start.7) | collective-permute-done | bytes 196640 | tf_op jit(solution)/shard_map/ppermute | solution.py:269
  65.2 8.1 %collective-permute-done.5.received = bf16[3,32,2048]{2,1,0:T(8,128)(2,1)S(1)} collective-permute-done((bf16[3,32,2048]{2,1,0:T(8,128)(2,1)S(1)}, bf16[3,32,2048]{2,1,0:T(8,128)(2,1)S(1)}, u32[]{:S(2)}, u32[]{:S(2)}) %collective-permute-start.5) | collective-permute-done | bytes 393248 | tf_op jit(solution)/shard_map/ppermute | solution.py:269
  73.6 2.5 %collective-permute-start.8 = (bf16[3,32,2048]{2,1,0:T(8,128)(2,1)S(1)}, bf16[3,32,2048]{2,1,0:T(8,128)(2,1)S(1)}, u32[]{:S(2)}, u32[]{:S(2)}) collective-permute-start(bf16[3,32,2048]{2,1,0:T(8,128)(2,1)S(1)} %get-tuple-element.83), channel_id=1, source_target_pairs={{0,4},{2,6},{4,0},{6,2},{8,12},{10,14},{12,8},{14,10},{1,5},{3,7},... | collective-permute-start | bytes 1179656 | tf_op jit(solution)/shard_map/ppermute | solution.py:269
  76.1 1.6 collective-permute-start.3
  77.8 8.1 %collective-permute-done.10.other = bf16[3,32,2048]{2,1,0:T(8,128)(2,1)S(1)} collective-permute-done((bf16[3,32,2048]{2,1,0:T(8,128)(2,1)S(1)}, bf16[3,32,2048]{2,1,0:T(8,128)(2,1)S(1)}, u32[]{:S(2)}, u32[]{:S(2)}) %collective-permute-start.10) | collective-permute-done | bytes 393248 | tf_op jit(solution)/shard_map/ppermute | solution.py:269
  87.4 8.9 %collective-permute-done.11.other = bf16[3,16,2048]{2,1,0:T(8,128)(2,1)S(1)} collective-permute-done((bf16[3,16,2048]{2,1,0:T(8,128)(2,1)S(1)}, bf16[3,16,2048]{2,1,0:T(8,128)(2,1)S(1)}, u32[]{:S(2)}, u32[]{:S(2)}) %collective-permute-start.11) | collective-permute-done | bytes 196640 | tf_op jit(solution)/shard_map/ppermute | solution.py:269
  96.7 1.6 collective-permute-start.15
  98.4 2.1 %collective-permute-start.12 = (bf16[3,32,1024]{2,1,0:T(8,128)(2,1)S(1)}, bf16[3,32,1024]{2,1,0:T(8,128)(2,1)S(1)}, u32[]{:S(2)}, u32[]{:S(2)}) collective-permute-start(bf16[3,32,1024]{2,1,0:T(8,128)(2,1)S(1)} %get-tuple-element.90), channel_id=1, source_target_pairs={{0,4},{2,6},{4,0},{6,2},{8,12},{10,14},{12,8},{14,10},{1,5},{3,7},... | collective-permute-start | bytes 589832 | tf_op jit(solution)/shard_map/ppermute | solution.py:269
  100.4 9.7 %collective-permute-done.13.received = bf16[3,16,2048]{2,1,0:T(8,128)(2,1)S(1)} collective-permute-done((bf16[3,16,2048]{2,1,0:T(8,128)(2,1)S(1)}, bf16[3,16,2048]{2,1,0:T(8,128)(2,1)S(1)}, u32[]{:S(2)}, u32[]{:S(2)}) %collective-permute-start.13) | collective-permute-done | bytes 196640 | tf_op jit(solution)/shard_map/ppermute | solution.py:269
  110.5 3.4 %collective-permute-start.16 = (bf16[3,16,2048]{2,1,0:T(8,128)(2,1)S(1)}, bf16[3,16,2048]{2,1,0:T(8,128)(2,1)S(1)}, u32[]{:S(2)}, u32[]{:S(2)}) collective-permute-start(bf16[3,16,2048]{2,1,0:T(8,128)(2,1)S(1)} %get-tuple-element.94.rest_0_.own), channel_id=1, source_target_pairs={{0,8},{2,10},{4,12},{6,14},{8,0},{10,2},{12,4},{14,6},{1,9},{3,11}... | collective-permute-start | bytes 589832 | tf_op jit(solution)/shard_map/ppermute | solution.py:269
  116.2 2.9 %collective-permute-done.16.other = bf16[3,16,2048]{2,1,0:T(8,128)(2,1)S(1)} collective-permute-done((bf16[3,16,2048]{2,1,0:T(8,128)(2,1)S(1)}, bf16[3,16,2048]{2,1,0:T(8,128)(2,1)S(1)}, u32[]{:S(2)}, u32[]{:S(2)}) %collective-permute-start.16) | collective-permute-done | bytes 196640 | tf_op jit(solution)/shard_map/ppermute | solution.py:269
  119.1 2.8 %collective-permute-start.19 = (bf16[3,32,2048]{2,1,0:T(8,128)(2,1)S(1)}, bf16[3,32,2048]{2,1,0:T(8,128)(2,1)S(1)}, u32[]{:S(2)}, u32[]{:S(2)}) collective-permute-start(bf16[3,32,2048]{2,1,0:T(8,128)(2,1)S(1)} %join.12.rest_0_.own), channel_id=1, source_target_pairs={{0,4},{2,6},{4,0},{6,2},{8,12},{10,14},{12,8},{14,10},{1,5},{3,7},... | collective-permute-start | bytes 1179656 | tf_op jit(solution)/shard_map/ppermute | solution.py:269
  122.7 10.3 %back.4 = (f32[264,1024]{1,0:T(8,128)S(1)}, bf16[1024,7168]{1,0:T(8,128)(2,1)}, bf16[1024,7168]{1,0:T(8,128)(2,1)}, bf16[7168,1024]{1,0:T(8,128)(2,1)}) custom-call(bf16[3,64,2048]{2,1,0:T(8,128)(2,1)S(1)} %join.9.rest_0_.own, bf16[3,64,2048]{2,1,0:T(8,128)(2,1)S(1)} %collective-permute-done.15.other, bf16[1024,128]{1,0:T(8,128)(2,1)S(1)} %get-tuple-element.99.flipped, ...), custom_call_target="tpu_custom_call" | custom-call | tf_op jit(solution)/shard_map/back/pallas_call | solution.py:288
  135.4 2.1 %collective-permute-start.18 = (bf16[3,16,1152]{2,1,0:T(8,128)(2,1)S(1)}, bf16[3,16,1152]{2,1,0:T(8,128)(2,1)S(1)}, u32[]{:S(2)}, u32[]{:S(2)}) collective-permute-start(bf16[3,16,1152]{2,1,0:T(8,128)(2,1)S(1)} %get-tuple-element.101.rest_0_.own), channel_id=1, source_target_pairs={{0,8},{2,10},{4,12},{6,14},{8,0},{10,2},{12,4},{14,6},{1,9},{3,11}... | collective-permute-start | bytes 331784 | tf_op jit(solution)/shard_map/ppermute | solution.py:269
  137.5 3.6 %collective-permute-done.18.other = bf16[3,16,1152]{2,1,0:T(8,128)(2,1)S(1)} collective-permute-done((bf16[3,16,1152]{2,1,0:T(8,128)(2,1)S(1)}, bf16[3,16,1152]{2,1,0:T(8,128)(2,1)S(1)}, u32[]{:S(2)}, u32[]{:S(2)}) %collective-permute-start.18) | collective-permute-done | bytes 110624 | tf_op jit(solution)/shard_map/ppermute | solution.py:269
  141.1 2.0 %collective-permute-start.20 = (bf16[3,32,1152]{2,1,0:T(8,128)(2,1)S(1)}, bf16[3,32,1152]{2,1,0:T(8,128)(2,1)S(1)}, u32[]{:S(2)}, u32[]{:S(2)}) collective-permute-start(bf16[3,32,1152]{2,1,0:T(8,128)(2,1)S(1)} %join.14.rest_4_.own), channel_id=1, source_target_pairs={{0,4},{2,6},{4,0},{6,2},{8,12},{10,14},{12,8},{14,10},{1,5},{3,7},... | collective-permute-start | bytes 663560 | tf_op jit(solution)/shard_map/ppermute | solution.py:269
  143.1 11.6 %back.5 = (f32[264,1024]{1,0:T(8,128)S(1)}, bf16[1024,7168]{1,0:T(8,128)(2,1)}, bf16[1024,7168]{1,0:T(8,128)(2,1)}, bf16[7168,1024]{1,0:T(8,128)(2,1)}) custom-call(bf16[3,64,2048]{2,1,0:T(8,128)(2,1)S(1)} %join.11.rest_0_.own, bf16[3,64,2048]{2,1,0:T(8,128)(2,1)S(1)} %collective-permute-done.21.other, ...), custom_call_target="tpu_custom_call", output_to_operand_aliasing={{1}: (8, {}), {2}: (9, {}), {3}: (10, {})} | custom-call | tf_op jit(solution)/shard_map/back/pallas_call | solution.py:288
  155.5 11.6 %back.6 = (f32[264,1024]{1,0:T(8,128)S(1)}, bf16[1024,7168]{1,0:T(8,128)(2,1)}, bf16[1024,7168]{1,0:T(8,128)(2,1)}, bf16[7168,1024]{1,0:T(8,128)(2,1)}) custom-call(bf16[3,64,2048]{2,1,0:T(8,128)(2,1)S(1)} %join.13.rest_0_.own, bf16[3,64,2048]{2,1,0:T(8,128)(2,1)S(1)} %collective-permute-done.23.other, ...), custom_call_target="tpu_custom_call", output_to_operand_aliasing={{1}: (8, {}), {2}: (9, {}), {3}: (10, {})} | custom-call | tf_op jit(solution)/shard_map/back/pallas_call | solution.py:288
  167.1 6.3 %back.7 = (f32[264,1024]{1,0:T(8,128)S(1)}, bf16[1024,7168]{1,0:T(8,128)(2,1)}, bf16[1024,7168]{1,0:T(8,128)(2,1)}, bf16[7168,1024]{1,0:T(8,128)(2,1)}) custom-call(bf16[3,64,1152]{2,1,0:T(8,128)(2,1)S(1)} %join.15.rest_4_.own, ...), custom_call_target="tpu_custom_call", output_to_operand_aliasing={{1}: (8, {}), {2}: (9, {}), {3}: (10, {})} | custom-call | tf_op jit(solution)/shard_map/back/pallas_call | solution.py:288
  173.5 2.7 %collective-permute-done.24.other = f32[264,1024]{1,0:T(8,128)S(1)} collective-permute-done((f32[264,1024]{1,0:T(8,128)S(1)}, f32[264,1024]{1,0:T(8,128)S(1)}, u32[]{:S(2)}, u32[]{:S(2)}) %collective-permute-start.24) | collective-permute-done | bytes 1081376 | tf_op jit(solution)/shard_map/ppermute | solution.py:273
  176.2 1.7 end.1
  (62 shorter events, 16.3 us)
Async XLA Ops:
  0.6 1.0 copy-start
  1.7 0.9 copy-start.1
  2.6 0.7 copy-start.2
  3.3 0.7 copy-start.4
  4.0 0.7 copy-start.6
  10.0 22.4 %collective-permute-start.1 = (bf16[3,64,2176]{2,1,0:T(8,128)(2,1)S(1)}, bf16[3,64,2176]{2,1,0:T(8,128)(2,1)S(1)}, u32[]{:S(2)}, u32[]{:S(2)}) collective-permute-start(bf16[3,64,2176]{2,1,0:T(8,128)(2,1)S(1)} %get-tuple-element.69), channel_id=1, source_target_pairs={{0,2},{2,0},{4,6},{6,4},{8,10},{10,8},{12,14},{14,12},{1,3},{3,1},... | collective-permute-start | bytes 2506760 | tf_op jit(solution)/shard_map/ppermute | solution.py:269
  19.2 30.1 %collective-permute-start = (bf16[3,64,2048]{2,1,0:T(8,128)(2,1)S(1)}, bf16[3,64,2048]{2,1,0:T(8,128)(2,1)S(1)}, u32[]{:S(2)}, u32[]{:S(2)}) collective-permute-start(bf16[3,64,2048]{2,1,0:T(8,128)(2,1)S(1)} %get-tuple-element.67), channel_id=1, source_target_pairs={{0,2},{2,0},{4,6},{6,4},{8,10},{10,8},{12,14},{14,12},{1,3},{3,1},... | collective-permute-start | bytes 2359304 | tf_op jit(solution)/shard_map/ppermute | solution.py:269
  32.6 10.1 %collective-permute-start.2 = (bf16[3,32,2176]{2,1,0:T(8,128)(2,1)S(1)}, bf16[3,32,2176]{2,1,0:T(8,128)(2,1)S(1)}, u32[]{:S(2)}, u32[]{:S(2)}) collective-permute-start(bf16[3,32,2176]{2,1,0:T(8,128)(2,1)S(1)} %get-tuple-element.71), channel_id=1, source_target_pairs={{0,4},{2,6},{4,0},{6,2},{8,12},{10,14},{12,8},{14,10},{1,5},{3,7},... | collective-permute-start | bytes 1253384 | tf_op jit(solution)/shard_map/ppermute | solution.py:269
  40.9 32.5 %collective-permute-start.4 = (bf16[3,64,2048]{2,1,0:T(8,128)(2,1)S(1)}, bf16[3,64,2048]{2,1,0:T(8,128)(2,1)S(1)}, u32[]{:S(2)}, u32[]{:S(2)}) collective-permute-start(bf16[3,64,2048]{2,1,0:T(8,128)(2,1)S(1)} %get-tuple-element.77), channel_id=1, source_target_pairs={{0,2},{2,0},{4,6},{6,4},{8,10},{10,8},{12,14},{14,12},{1,3},{3,1},... | collective-permute-start | bytes 2359304 | tf_op jit(solution)/shard_map/ppermute | solution.py:269
  42.7 10.9 %collective-permute-start.6 = (bf16[3,16,2176]{2,1,0:T(8,128)(2,1)S(1)}, bf16[3,16,2176]{2,1,0:T(8,128)(2,1)S(1)}, u32[]{:S(2)}, u32[]{:S(2)}) collective-permute-start(bf16[3,16,2176]{2,1,0:T(8,128)(2,1)S(1)} %get-tuple-element.79), channel_id=1, source_target_pairs={{0,8},{2,10},{4,12},{6,14},{8,0},{10,2},{12,4},{14,6},{1,9},{3,11}... | collective-permute-start | bytes 626696 | tf_op jit(solution)/shard_map/ppermute | solution.py:269
  54.0 10.4 %collective-permute-start.7 = (bf16[3,16,2048]{2,1,0:T(8,128)(2,1)S(1)}, bf16[3,16,2048]{2,1,0:T(8,128)(2,1)S(1)}, u32[]{:S(2)}, u32[]{:S(2)}) collective-permute-start(bf16[3,16,2048]{2,1,0:T(8,128)(2,1)S(1)} %get-tuple-element.80.own.rest_0_), channel_id=1, source_target_pairs={{0,8},{2,10},{4,12},{6,14},{8,0},{10,2},{12,4},{14,6},{1,9},{3,11}... | collective-permute-start | bytes 589832 | tf_op jit(solution)/shard_map/ppermute | solution.py:269
  57.2 16.1 %collective-permute-start.5 = (bf16[3,32,2048]{2,1,0:T(8,128)(2,1)S(1)}, bf16[3,32,2048]{2,1,0:T(8,128)(2,1)S(1)}, u32[]{:S(2)}, u32[]{:S(2)}) collective-permute-start(bf16[3,32,2048]{2,1,0:T(8,128)(2,1)S(1)} %get-tuple-element.78), channel_id=1, source_target_pairs={{0,4},{2,6},{4,0},{6,2},{8,12},{10,14},{12,8},{14,10},{1,5},{3,7},... | collective-permute-start | bytes 1179656 | tf_op jit(solution)/shard_map/ppermute | solution.py:269
  64.5 21.4 %collective-permute-start.10 = (bf16[3,32,2048]{2,1,0:T(8,128)(2,1)S(1)}, bf16[3,32,2048]{2,1,0:T(8,128)(2,1)S(1)}, u32[]{:S(2)}, u32[]{:S(2)}) collective-permute-start(bf16[3,32,2048]{2,1,0:T(8,128)(2,1)S(1)} %join.8.rest_0_.own), channel_id=1, source_target_pairs={{0,4},{2,6},{4,0},{6,2},{8,12},{10,14},{12,8},{14,10},{1,5},{3,7},... | collective-permute-start | bytes 1179656 | tf_op jit(solution)/shard_map/ppermute | solution.py:269
  73.3 12.6 %collective-permute-start.9 = (bf16[3,16,2048]{2,1,0:T(8,128)(2,1)S(1)}, bf16[3,16,2048]{2,1,0:T(8,128)(2,1)S(1)}, u32[]{:S(2)}, u32[]{:S(2)}) collective-permute-start(bf16[3,16,2048]{2,1,0:T(8,128)(2,1)S(1)} %get-tuple-element.84), channel_id=1, source_target_pairs={{0,8},{2,10},{4,12},{6,14},{8,0},{10,2},{12,4},{14,6},{1,9},{3,11}... | collective-permute-start | bytes 589832 | tf_op jit(solution)/shard_map/ppermute | solution.py:269
  73.6 22.7 %collective-permute-start.8 = (bf16[3,32,2048]{2,1,0:T(8,128)(2,1)S(1)}, bf16[3,32,2048]{2,1,0:T(8,128)(2,1)S(1)}, u32[]{:S(2)}, u32[]{:S(2)}) collective-permute-start(bf16[3,32,2048]{2,1,0:T(8,128)(2,1)S(1)} %get-tuple-element.83), channel_id=1, source_target_pairs={{0,4},{2,6},{4,0},{6,2},{8,12},{10,14},{12,8},{14,10},{1,5},{3,7},... | collective-permute-start | bytes 1179656 | tf_op jit(solution)/shard_map/ppermute | solution.py:269
  76.1 22.2 %collective-permute-start.3 = (bf16[3,64,1024]{2,1,0:T(8,128)(2,1)S(1)}, bf16[3,64,1024]{2,1,0:T(8,128)(2,1)S(1)}, u32[]{:S(2)}, u32[]{:S(2)}) collective-permute-start(bf16[3,64,1024]{2,1,0:T(8,128)(2,1)S(1)} %get-tuple-element.76), channel_id=1, source_target_pairs={{0,2},{2,0},{4,6},{6,4},{8,10},{10,8},{12,14},{14,12},{1,3},{3,1},... | collective-permute-start | bytes 1179656 | tf_op jit(solution)/shard_map/ppermute | solution.py:269
  86.3 9.9 %collective-permute-start.11 = (bf16[3,16,2048]{2,1,0:T(8,128)(2,1)S(1)}, bf16[3,16,2048]{2,1,0:T(8,128)(2,1)S(1)}, u32[]{:S(2)}, u32[]{:S(2)}) collective-permute-start(bf16[3,16,2048]{2,1,0:T(8,128)(2,1)S(1)} %get-tuple-element.87.own.rest_0_), channel_id=1, source_target_pairs={{0,8},{2,10},{4,12},{6,14},{8,0},{10,2},{12,4},{14,6},{1,9},{3,11}... | collective-permute-start | bytes 589832 | tf_op jit(solution)/shard_map/ppermute | solution.py:269
  96.2 18.5 %collective-permute-start.17 = (bf16[3,32,2048]{2,1,0:T(8,128)(2,1)S(1)}, bf16[3,32,2048]{2,1,0:T(8,128)(2,1)S(1)}, u32[]{:S(2)}, u32[]{:S(2)}) collective-permute-start(bf16[3,32,2048]{2,1,0:T(8,128)(2,1)S(1)} %join.10.rest_0_.own), channel_id=1, source_target_pairs={{0,4},{2,6},{4,0},{6,2},{8,12},{10,14},{12,8},{14,10},{1,5},{3,7},... | collective-permute-start | bytes 1179656 | tf_op jit(solution)/shard_map/ppermute | solution.py:269
  96.4 13.7 %collective-permute-start.13 = (bf16[3,16,2048]{2,1,0:T(8,128)(2,1)S(1)}, bf16[3,16,2048]{2,1,0:T(8,128)(2,1)S(1)}, u32[]{:S(2)}, u32[]{:S(2)}) collective-permute-start(bf16[3,16,2048]{2,1,0:T(8,128)(2,1)S(1)} %get-tuple-element.91), channel_id=1, source_target_pairs={{0,8},{2,10},{4,12},{6,14},{8,0},{10,2},{12,4},{14,6},{1,9},{3,11}... | collective-permute-start | bytes 589832 | tf_op jit(solution)/shard_map/ppermute | solution.py:269
  96.7 25.9 %collective-permute-start.15 = (bf16[3,64,2048]{2,1,0:T(8,128)(2,1)S(1)}, bf16[3,64,2048]{2,1,0:T(8,128)(2,1)S(1)}, u32[]{:S(2)}, u32[]{:S(2)}) collective-permute-start(bf16[3,64,2048]{2,1,0:T(8,128)(2,1)S(1)} %join.9.rest_0_.own), channel_id=1, source_target_pairs={{0,2},{2,0},{4,6},{6,4},{8,10},{10,8},{12,14},{14,12},{1,3},{3,1},... | collective-permute-start | bytes 2359304 | tf_op jit(solution)/shard_map/ppermute | solution.py:269
  98.4 16.3 %collective-permute-start.12 = (bf16[3,32,1024]{2,1,0:T(8,128)(2,1)S(1)}, bf16[3,32,1024]{2,1,0:T(8,128)(2,1)S(1)}, u32[]{:S(2)}, u32[]{:S(2)}) collective-permute-start(bf16[3,32,1024]{2,1,0:T(8,128)(2,1)S(1)} %get-tuple-element.90), channel_id=1, source_target_pairs={{0,4},{2,6},{4,0},{6,2},{8,12},{10,14},{12,8},{14,10},{1,5},{3,7},... | collective-permute-start | bytes 589832 | tf_op jit(solution)/shard_map/ppermute | solution.py:269
  110.5 8.6 %collective-permute-start.16 = (bf16[3,16,2048]{2,1,0:T(8,128)(2,1)S(1)}, bf16[3,16,2048]{2,1,0:T(8,128)(2,1)S(1)}, u32[]{:S(2)}, u32[]{:S(2)}) collective-permute-start(bf16[3,16,2048]{2,1,0:T(8,128)(2,1)S(1)} %get-tuple-element.94.rest_0_.own), channel_id=1, source_target_pairs={{0,8},{2,10},{4,12},{6,14},{8,0},{10,2},{12,4},{14,6},{1,9},{3,11}... | collective-permute-start | bytes 589832 | tf_op jit(solution)/shard_map/ppermute | solution.py:269
  114.8 28.3 %collective-permute-start.21 = (bf16[3,64,2048]{2,1,0:T(8,128)(2,1)S(1)}, bf16[3,64,2048]{2,1,0:T(8,128)(2,1)S(1)}, u32[]{:S(2)}, u32[]{:S(2)}) collective-permute-start(bf16[3,64,2048]{2,1,0:T(8,128)(2,1)S(1)} %join.11.rest_0_.own), channel_id=1, source_target_pairs={{0,2},{2,0},{4,6},{6,4},{8,10},{10,8},{12,14},{14,12},{1,3},{3,1},... | collective-permute-start | bytes 2359304 | tf_op jit(solution)/shard_map/ppermute | solution.py:269
  119.1 14.8 %collective-permute-start.19 = (bf16[3,32,2048]{2,1,0:T(8,128)(2,1)S(1)}, bf16[3,32,2048]{2,1,0:T(8,128)(2,1)S(1)}, u32[]{:S(2)}, u32[]{:S(2)}) collective-permute-start(bf16[3,32,2048]{2,1,0:T(8,128)(2,1)S(1)} %join.12.rest_0_.own), channel_id=1, source_target_pairs={{0,4},{2,6},{4,0},{6,2},{8,12},{10,14},{12,8},{14,10},{1,5},{3,7},... | collective-permute-start | bytes 1179656 | tf_op jit(solution)/shard_map/ppermute | solution.py:269
  121.9 11.1 %collective-permute-start.14 = (bf16[3,16,1024]{2,1,0:T(8,128)(2,1)S(1)}, bf16[3,16,1024]{2,1,0:T(8,128)(2,1)S(1)}, u32[]{:S(2)}, u32[]{:S(2)}) collective-permute-start(bf16[3,16,1024]{2,1,0:T(8,128)(2,1)S(1)} %get-tuple-element.96), channel_id=1, source_target_pairs={{0,8},{2,10},{4,12},{6,14},{8,0},{10,2},{12,4},{14,6},{1,9},{3,11}... | collective-permute-start | bytes 294920 | tf_op jit(solution)/shard_map/ppermute | solution.py:269
  133.9 21.5 %collective-permute-start.23 = (bf16[3,64,2048]{2,1,0:T(8,128)(2,1)S(1)}, bf16[3,64,2048]{2,1,0:T(8,128)(2,1)S(1)}, u32[]{:S(2)}, u32[]{:S(2)}) collective-permute-start(bf16[3,64,2048]{2,1,0:T(8,128)(2,1)S(1)} %join.13.rest_0_.own), channel_id=1, source_target_pairs={{0,2},{2,0},{4,6},{6,4},{8,10},{10,8},{12,14},{14,12},{1,3},{3,1},... | collective-permute-start | bytes 2359304 | tf_op jit(solution)/shard_map/ppermute | solution.py:269
  135.4 5.6 %collective-permute-start.18 = (bf16[3,16,1152]{2,1,0:T(8,128)(2,1)S(1)}, bf16[3,16,1152]{2,1,0:T(8,128)(2,1)S(1)}, u32[]{:S(2)}, u32[]{:S(2)}) collective-permute-start(bf16[3,16,1152]{2,1,0:T(8,128)(2,1)S(1)} %get-tuple-element.101.rest_0_.own), channel_id=1, source_target_pairs={{0,8},{2,10},{4,12},{6,14},{8,0},{10,2},{12,4},{14,6},{1,9},{3,11}... | collective-permute-start | bytes 331784 | tf_op jit(solution)/shard_map/ppermute | solution.py:269
  141.1 13.6 %collective-permute-start.20 = (bf16[3,32,1152]{2,1,0:T(8,128)(2,1)S(1)}, bf16[3,32,1152]{2,1,0:T(8,128)(2,1)S(1)}, u32[]{:S(2)}, u32[]{:S(2)}) collective-permute-start(bf16[3,32,1152]{2,1,0:T(8,128)(2,1)S(1)} %join.14.rest_4_.own), channel_id=1, source_target_pairs={{0,4},{2,6},{4,0},{6,2},{8,12},{10,14},{12,8},{14,10},{1,5},{3,7},... | collective-permute-start | bytes 663560 | tf_op jit(solution)/shard_map/ppermute | solution.py:269
  154.8 12.3 %collective-permute-start.22 = (bf16[3,64,1152]{2,1,0:T(8,128)(2,1)S(1)}, bf16[3,64,1152]{2,1,0:T(8,128)(2,1)S(1)}, u32[]{:S(2)}, u32[]{:S(2)}) collective-permute-start(bf16[3,64,1152]{2,1,0:T(8,128)(2,1)S(1)} %join.15.rest_4_.own), channel_id=1, source_target_pairs={{0,2},{2,0},{4,6},{6,4},{8,10},{10,8},{12,14},{14,12},{1,3},{3,1},... | collective-permute-start | bytes 1327112 | tf_op jit(solution)/shard_map/ppermute | solution.py:269
  167.1 9.1 %copy-start.3 = (f32[1024]{0:T(1024)S(1)}, f32[1024]{0:T(1024)}, u32[]{:S(2)}) copy-start(f32[1024]{0:T(1024)} %param.11) | copy-start | bytes 12292
  167.1 9.1 %copy-start.5 = (s32[128]{0:T(128)S(1)}, s32[128]{0:T(128)}, u32[]{:S(2)}) copy-start(s32[128]{0:T(128)} %param.9) | copy-start | bytes 1540
  173.4 2.8 %collective-permute-start.24 = (f32[264,1024]{1,0:T(8,128)S(1)}, f32[264,1024]{1,0:T(8,128)S(1)}, u32[]{:S(2)}, u32[]{:S(2)}) collective-permute-start(f32[264,1024]{1,0:T(8,128)S(1)} %get-tuple-element.113.own), channel_id=1, source_target_pairs={{0,1},{1,0},{2,3},{3,2},{4,5},{5,4},{6,7},{7,6},{8,9},{9,8},{10,11... | collective-permute-start | bytes 3244040 | tf_op jit(solution)/shard_map/ppermute | solution.py:273

commit v4 on v3

--- a/solution.py
+++ b/solution.py
@@ -13,35 +13,14 @@
 COUNTS = (2, 2, 2, 1)
 SWAPPED = (False, False, False, False)
 ORDER = (
-    ("F", 1),
-    ("H", 0, 0),
-    ("F", 2),
-    ("H", 0, 1),
-    ("H", 1, 0),
-    ("F", 3),
-    ("W", 0),
-    ("J", 0, 2),
-    ("H", 1, 1),
-    ("H", 2, 0),
-    ("J", 0, 1),
-    ("W", 1),
-    ("J", 1, 2),
-    ("H", 2, 1),
-    ("H", 3, 0),
-    ("W", 2),
-    ("H", 3, 1),
-    ("J", 1, 1),
-    ("J", 2, 2),
-    ("B", 0),
-    ("W", 3),
-    ("J", 2, 1),
-    ("J", 3, 2),
-    ("B", 1),
-    ("J", 3, 1),
-    ("B", 2),
-    ("B", 3),
+    ("F", 2), ("F", 1), ("H", 0, 0), ("H", 0, 1), ("H", 1, 0), ("F", 3), ("W", 0), ("H", 2, 0), ("J", 0, 2),
+    ("H", 1, 1), ("H", 2, 1), ("H", 3, 0), ("W", 1), ("J", 0, 1), ("J", 1, 2), ("H", 3, 1), ("W", 2),
+    ("A", "W", 2), ("J", 1, 1), ("J", 2, 2), ("B", 0), ("W", 3), ("J", 2, 1), ("J", 3, 2), ("B", 1),
+    ("J", 3, 1), ("B", 2), ("B", 3),
 )
-COSTS = (0,) * len(ORDER)
+COSTS = (
+    0, 20, 0, 0, 8, 8, 0, 0, 8, 0, 0, 0, 0, 40, 100, 3, 20, 0, 0, 40, 0, 40, 100, 20, 0, 0, 0, 0,
+)
 START_MIB, FORE_MIB, BACK_MIB = 44, 44, 44
 NN = (((1,), (0,)), ((), ()))
 NT = (((1,), (1,)), ((), ()))

time: 178 us -> 174 us (0.978)
  waiting for transfers between devices: 67.4 us -> 62.6 us
    ppermute x24, waiting for transfers between devices: 64.7 us -> 59.9 us  [swap(): return lax.ppermute(x, 'width', [(i, i ^ 1 << step) for i in range(ways)])]
  transfers between devices with their start and end apart: 25 -> 25, of which waited for: 12 -> 11; matrix products, arithmetic and copies ran while one was open for 0% -> 0% of each run, Pallas kernels for 30% -> 31%
where the time goes in v4:
time: 174 us
  Pallas kernels  66.6 us (38%)
  waiting for transfers between devices  62.6 us (36%)
  starting transfers between devices  39.9 us (23%)
  local copies, waits for them, and re-layouts  3.99 us (2%)
    pallas_call x28, Pallas kernels, kernel(): pl.pallas_call(body, out_shape=out_shape, in_specs=list(in_specs) + [ANY]...  64.9 us
    ppermute x24, waiting for transfers between devices, swap(): return lax.ppermute(x, 'width', [(i, i ^ 1 << step) for i in range(ways)])  59.9 us
    ppermute x24, starting transfers between devices, swap(): return lax.ppermute(x, 'width', [(i, i ^ 1 << step) for i in range(ways)])  39.9 us
    unnamed x14, local copies, waits for them, and re-layouts  3.99 us
  transfers between devices with their start and end apart: 25, of which 11 were waited for; matrix products, arithmetic and copies ran while one was open for 0% of the time, Pallas kernels for 31%

profile of v4, /device:TPU:0, one launch (start us, length us, event | category | flops | bytes accessed | tf_op | source)
XLA Modules:
  0.0 174.0 jit_solution(4126990576662752289)
XLA Ops:
  4.6 5.3 %start.1 = (bf16[128,1024]{1,0:T(8,128)(2,1)S(1)}, bf16[128,1024]{1,0:T(8,128)(2,1)S(1)}, bf16[128,1024]{1,0:T(8,128)(2,1)S(1)}, bf16[1024,128]{1,0:T(8,128)(2,1...) custom-call(s32[1]{0:T(128)} %bitcast.label, s32[1,128]{1,0:T(1,128)S(1)} %bitcast.7, ...), custom_call_target="tpu_custom_call" | custom-call | tf_op jit(solution)/shard_map/start/pallas_call | solution.py:267
  10.0 3.0 %collective-permute-start.1 = (bf16[3,64,2176]{2,1,0:T(8,128)(2,1)S(1)}, bf16[3,64,2176]{2,1,0:T(8,128)(2,1)S(1)}, u32[]{:S(2)}, u32[]{:S(2)}) collective-permute-start(bf16[3,64,2176]{2,1,0:T(8,128)(2,1)S(1)} %get-tuple-element.70), channel_id=1, source_target_pairs={{0,2},{2,0},{4,6},{6,4},{8,10},{10,8},{12,14},{14,12},{1,3},{3,1},... | collective-permute-start | bytes 2506760 | tf_op jit(solution)/shard_map/ppermute | solution.py:248
  13.0 6.2 %fore.3 = (f32[3,64,2048]{2,1,0:T(8,128)S(1)}, bf16[3,64,2048]{2,1,0:T(8,128)(2,1)S(1)}) custom-call(bf16[128,1024]{1,0:T(8,128)(2,1)S(1)} %get-tuple-element.63.normed, bf16[128,1024]{1,0:T(8,128)(2,1)S(1)} %get-tuple-element.64.dout, bf16[7168,1024]{1,0:T(8,128)(2,1)} %w_down.15, bf16[1024,7168]{1,0:T(8,128)(2,1)} %w_gate.15, bf16[1024,7168]{1,0:T(8,128)(2,1)} %w_up.15, ...), custom_call_target="tpu_custom_call" | custom-call | tf_op jit(solution)/shard_map/fore/pallas_call | solution.py:267
  19.2 6.2 %fore.4 = (f32[3,64,2048]{2,1,0:T(8,128)S(1)}, bf16[3,64,2048]{2,1,0:T(8,128)(2,1)S(1)}) custom-call(bf16[128,1024]{1,0:T(8,128)(2,1)S(1)} %get-tuple-element.63.normed, bf16[128,1024]{1,0:T(8,128)(2,1)S(1)} %get-tuple-element.64.dout, bf16[7168,1024]{1,0:T(8,128)(2,1)} %w_down.15, bf16[1024,7168]{1,0:T(8,128)(2,1)} %w_gate.15, bf16[1024,7168]{1,0:T(8,128)(2,1)} %w_up.15, ...), custom_call_target="tpu_custom_call" | custom-call | bytes 20000000 | tf_op jit(solution)/shard_map/fore/pallas_call | solution.py:267
  25.5 2.0 %collective-permute-start.4 = (bf16[3,64,2048]{2,1,0:T(8,128)(2,1)S(1)}, bf16[3,64,2048]{2,1,0:T(8,128)(2,1)S(1)}, u32[]{:S(2)}, u32[]{:S(2)}) collective-permute-start(bf16[3,64,2048]{2,1,0:T(8,128)(2,1)S(1)} %get-tuple-element.77), channel_id=1, source_target_pairs={{0,2},{2,0},{4,6},{6,4},{8,10},{10,8},{12,14},{14,12},{1,3},{3,1},... | collective-permute-start | bytes 2359304 | tf_op jit(solution)/shard_map/ppermute | solution.py:248
  27.5 5.0 %collective-permute-done.1.received = bf16[3,64,2176]{2,1,0:T(8,128)(2,1)S(1)} collective-permute-done((bf16[3,64,2176]{2,1,0:T(8,128)(2,1)S(1)}, bf16[3,64,2176]{2,1,0:T(8,128)(2,1)S(1)}, u32[]{:S(2)}, u32[]{:S(2)}) %collective-permute-start.1) | collective-permute-done | bytes 835616 | tf_op jit(solution)/shard_map/ppermute | solution.py:248
  32.6 2.2 %collective-permute-start.2 = (bf16[3,32,2176]{2,1,0:T(8,128)(2,1)S(1)}, bf16[3,32,2176]{2,1,0:T(8,128)(2,1)S(1)}, u32[]{:S(2)}, u32[]{:S(2)}) collective-permute-start(bf16[3,32,2176]{2,1,0:T(8,128)(2,1)S(1)} %get-tuple-element.72), channel_id=1, source_target_pairs={{0,4},{2,6},{4,0},{6,2},{8,12},{10,14},{12,8},{14,10},{1,5},{3,7},... | collective-permute-start | bytes 1253384 | tf_op jit(solution)/shard_map/ppermute | solution.py:248
  34.8 7.9 %collective-permute-done.2.received = bf16[3,32,2176]{2,1,0:T(8,128)(2,1)S(1)} collective-permute-done((bf16[3,32,2176]{2,1,0:T(8,128)(2,1)S(1)}, bf16[3,32,2176]{2,1,0:T(8,128)(2,1)S(1)}, u32[]{:S(2)}, u32[]{:S(2)}) %collective-permute-start.2) | collective-permute-done | bytes 417824 | tf_op jit(solution)/shard_map/ppermute | solution.py:248
  42.7 3.0 %collective-permute-start.5 = (bf16[3,16,2176]{2,1,0:T(8,128)(2,1)S(1)}, bf16[3,16,2176]{2,1,0:T(8,128)(2,1)S(1)}, u32[]{:S(2)}, u32[]{:S(2)}) collective-permute-start(bf16[3,16,2176]{2,1,0:T(8,128)(2,1)S(1)} %get-tuple-element.78), channel_id=1, source_target_pairs={{0,8},{2,10},{4,12},{6,14},{8,0},{10,2},{12,4},{14,6},{1,9},{3,11}... | collective-permute-start | bytes 626696 | tf_op jit(solution)/shard_map/ppermute | solution.py:248
  45.7 3.6 %collective-permute-done.received = bf16[3,64,2048]{2,1,0:T(8,128)(2,1)S(1)} collective-permute-done((bf16[3,64,2048]{2,1,0:T(8,128)(2,1)S(1)}, bf16[3,64,2048]{2,1,0:T(8,128)(2,1)S(1)}, u32[]{:S(2)}, u32[]{:S(2)}) %collective-permute-start) | collective-permute-done | bytes 786464 | tf_op jit(solution)/shard_map/ppermute | solution.py:248
  49.5 2.2 %collective-permute-start.7 = (bf16[3,32,2048]{2,1,0:T(8,128)(2,1)S(1)}, bf16[3,32,2048]{2,1,0:T(8,128)(2,1)S(1)}, u32[]{:S(2)}, u32[]{:S(2)}) collective-permute-start(bf16[3,32,2048]{2,1,0:T(8,128)(2,1)S(1)} %get-tuple-element.82), channel_id=1, source_target_pairs={{0,4},{2,6},{4,0},{6,2},{8,12},{10,14},{12,8},{14,10},{1,5},{3,7},... | collective-permute-start | bytes 1179656 | tf_op jit(solution)/shard_map/ppermute | solution.py:248
  51.7 4.2 %fore.5 = (f32[3,64,1024]{2,1,0:T(8,128)S(1)}, bf16[3,64,1024]{2,1,0:T(8,128)(2,1)S(1)}) custom-call(bf16[128,1024]{1,0:T(8,128)(2,1)S(1)} %get-tuple-element.63.normed, bf16[128,1024]{1,0:T(8,128)(2,1)S(1)} %get-tuple-element.64.dout, bf16[7168,1024]{1,0:T(8,128)(2,1)} %w_down.15, bf16[1024,7168]{1,0:T(8,128)(2,1)} %w_gate.15, bf16[1024,7168]{1,0:T(8,128)(2,1)} %w_up.15, ...), custom_call_target="tpu_custom_call" | custom-call | bytes 8000000 | tf_op jit(solution)/shard_map/fore/pallas_call | solution.py:267
  56.3 2.6 %collective-permute-start.8 = (bf16[3,16,2048]{2,1,0:T(8,128)(2,1)S(1)}, bf16[3,16,2048]{2,1,0:T(8,128)(2,1)S(1)}, u32[]{:S(2)}, u32[]{:S(2)}) collective-permute-start(bf16[3,16,2048]{2,1,0:T(8,128)(2,1)S(1)} %get-tuple-element.79.rest_0_.own), channel_id=1, source_target_pairs={{0,8},{2,10},{4,12},{6,14},{8,0},{10,2},{12,4},{14,6},{1,9},{3,11}... | collective-permute-start | bytes 589832 | tf_op jit(solution)/shard_map/ppermute | solution.py:248
  58.9 6.4 %collective-permute-done.4.received = bf16[3,64,2048]{2,1,0:T(8,128)(2,1)S(1)} collective-permute-done((bf16[3,64,2048]{2,1,0:T(8,128)(2,1)S(1)}, bf16[3,64,2048]{2,1,0:T(8,128)(2,1)S(1)}, u32[]{:S(2)}, u32[]{:S(2)}) %collective-permute-start.4) | collective-permute-done | bytes 786464 | tf_op jit(solution)/shard_map/ppermute | solution.py:248
  65.4 1.9 %collective-permute-start.6 = (bf16[3,32,2048]{2,1,0:T(8,128)(2,1)S(1)}, bf16[3,32,2048]{2,1,0:T(8,128)(2,1)S(1)}, u32[]{:S(2)}, u32[]{:S(2)}) collective-permute-start(bf16[3,32,2048]{2,1,0:T(8,128)(2,1)S(1)} %get-tuple-element.81), channel_id=1, source_target_pairs={{0,4},{2,6},{4,0},{6,2},{8,12},{10,14},{12,8},{14,10},{1,5},{3,7},... | collective-permute-start | bytes 1179656 | tf_op jit(solution)/shard_map/ppermute | solution.py:248
  68.9 2.6 %collective-permute-start.10 = (bf16[3,16,2048]{2,1,0:T(8,128)(2,1)S(1)}, bf16[3,16,2048]{2,1,0:T(8,128)(2,1)S(1)}, u32[]{:S(2)}, u32[]{:S(2)}) collective-permute-start(bf16[3,16,2048]{2,1,0:T(8,128)(2,1)S(1)} %get-tuple-element.87), channel_id=1, source_target_pairs={{0,8},{2,10},{4,12},{6,14},{8,0},{10,2},{12,4},{14,6},{1,9},{3,11}... | collective-permute-start | bytes 589832 | tf_op jit(solution)/shard_map/ppermute | solution.py:248
  72.0 9.7 %collective-permute-done.6.received = bf16[3,32,2048]{2,1,0:T(8,128)(2,1)S(1)} collective-permute-done((bf16[3,32,2048]{2,1,0:T(8,128)(2,1)S(1)}, bf16[3,32,2048]{2,1,0:T(8,128)(2,1)S(1)}, u32[]{:S(2)}, u32[]{:S(2)}) %collective-permute-start.6) | collective-permute-done | bytes 393248 | tf_op jit(solution)/shard_map/ppermute | solution.py:248
  82.3 2.6 %collective-permute-start.11 = (bf16[3,16,2048]{2,1,0:T(8,128)(2,1)S(1)}, bf16[3,16,2048]{2,1,0:T(8,128)(2,1)S(1)}, u32[]{:S(2)}, u32[]{:S(2)}) collective-permute-start(bf16[3,16,2048]{2,1,0:T(8,128)(2,1)S(1)} %get-tuple-element.90.rest_0_.own), channel_id=1, source_target_pairs={{0,8},{2,10},{4,12},{6,14},{8,0},{10,2},{12,4},{14,6},{1,9},{3,11}... | collective-permute-start | bytes 589832 | tf_op jit(solution)/shard_map/ppermute | solution.py:248
  84.8 1.9 %collective-permute-start.9 = (bf16[3,32,1024]{2,1,0:T(8,128)(2,1)S(1)}, bf16[3,32,1024]{2,1,0:T(8,128)(2,1)S(1)}, u32[]{:S(2)}, u32[]{:S(2)}) collective-permute-start(bf16[3,32,1024]{2,1,0:T(8,128)(2,1)S(1)} %get-tuple-element.86), channel_id=1, source_target_pairs={{0,4},{2,6},{4,0},{6,2},{8,12},{10,14},{12,8},{14,10},{1,5},{3,7},... | collective-permute-start | bytes 589832 | tf_op jit(solution)/shard_map/ppermute | solution.py:248
  87.9 10.7 %collective-permute-done.12.other = bf16[3,32,2048]{2,1,0:T(8,128)(2,1)S(1)} collective-permute-done((bf16[3,32,2048]{2,1,0:T(8,128)(2,1)S(1)}, bf16[3,32,2048]{2,1,0:T(8,128)(2,1)S(1)}, u32[]{:S(2)}, u32[]{:S(2)}) %collective-permute-start.12) | collective-permute-done | bytes 393248 | tf_op jit(solution)/shard_map/ppermute | solution.py:248
  98.8 1.8 %collective-permute-start.15 = (bf16[3,64,2048]{2,1,0:T(8,128)(2,1)S(1)}, bf16[3,64,2048]{2,1,0:T(8,128)(2,1)S(1)}, u32[]{:S(2)}, u32[]{:S(2)}) collective-permute-start(bf16[3,64,2048]{2,1,0:T(8,128)(2,1)S(1)} %join.9.rest_0_.own), channel_id=1, source_target_pairs={{0,2},{2,0},{4,6},{6,4},{8,10},{10,8},{12,14},{14,12},{1,3},{3,1},... | collective-permute-start | bytes 2359304 | tf_op jit(solution)/shard_map/ppermute | solution.py:248
  100.6 2.2 %collective-permute-done.9.received = bf16[3,32,1024]{2,1,0:T(8,128)(2,1)S(1)} collective-permute-done((bf16[3,32,1024]{2,1,0:T(8,128)(2,1)S(1)}, bf16[3,32,1024]{2,1,0:T(8,128)(2,1)S(1)}, u32[]{:S(2)}, u32[]{:S(2)}) %collective-permute-start.9) | collective-permute-done | bytes 196640 | tf_op jit(solution)/shard_map/ppermute | solution.py:248
  103.2 2.7 %collective-permute-start.16 = (bf16[3,16,2048]{2,1,0:T(8,128)(2,1)S(1)}, bf16[3,16,2048]{2,1,0:T(8,128)(2,1)S(1)}, u32[]{:S(2)}, u32[]{:S(2)}) collective-permute-start(bf16[3,16,2048]{2,1,0:T(8,128)(2,1)S(1)} %get-tuple-element.99.rest_0_.own), channel_id=1, source_target_pairs={{0,8},{2,10},{4,12},{6,14},{8,0},{10,2},{12,4},{14,6},{1,9},{3,11}... | collective-permute-start | bytes 589832 | tf_op jit(solution)/shard_map/ppermute | solution.py:248
  105.9 6.9 %collective-permute-done.16.rest_1_.other = bf16[3,16,2048]{2,1,0:T(8,128)(2,1)S(1)} collective-permute-done((bf16[3,16,2048]{2,1,0:T(8,128)(2,1)S(1)}, bf16[3,16,2048]{2,1,0:T(8,128)(2,1)S(1)}, u32[]{:S(2)}, u32[]{:S(2)}) %collective-permute-start.16) | collective-permute-done | bytes 196640 | tf_op jit(solution)/shard_map/ppermute | solution.py:248
  115.3 2.6 %collective-permute-start.19 = (bf16[3,32,2048]{2,1,0:T(8,128)(2,1)S(1)}, bf16[3,32,2048]{2,1,0:T(8,128)(2,1)S(1)}, u32[]{:S(2)}, u32[]{:S(2)}) collective-permute-start(bf16[3,32,2048]{2,1,0:T(8,128)(2,1)S(1)} %join.12.rest_0_.own), channel_id=1, source_target_pairs={{0,4},{2,6},{4,0},{6,2},{8,12},{10,14},{12,8},{14,10},{1,5},{3,7},... | collective-permute-start | bytes 1179656 | tf_op jit(solution)/shard_map/ppermute | solution.py:248
  119.5 10.4 %back.4 = (f32[264,1024]{1,0:T(8,128)S(1)}, bf16[1024,7168]{1,0:T(8,128)(2,1)}, bf16[1024,7168]{1,0:T(8,128)(2,1)}, bf16[7168,1024]{1,0:T(8,128)(2,1)}) custom-call(bf16[3,64,2048]{2,1,0:T(8,128)(2,1)S(1)} %join.9.rest_0_.own, bf16[3,64,2048]{2,1,0:T(8,128)(2,1)S(1)} %collective-permute-done.15.other, bf16[1024,128]{1,0:T(8,128)(2,1)S(1)} %get-tuple-element.98.flipped, ...), custom_call_target="tpu_custom_call" | custom-call | tf_op jit(solution)/shard_map/back/pallas_call | solution.py:267
  130.8 1.8 %collective-permute-start.23 = (bf16[3,64,2048]{2,1,0:T(8,128)(2,1)S(1)}, bf16[3,64,2048]{2,1,0:T(8,128)(2,1)S(1)}, u32[]{:S(2)}, u32[]{:S(2)}) collective-permute-start(bf16[3,64,2048]{2,1,0:T(8,128)(2,1)S(1)} %join.13.rest_0_.own), channel_id=1, source_target_pairs={{0,2},{2,0},{4,6},{6,4},{8,10},{10,8},{12,14},{14,12},{1,3},{3,1},... | collective-permute-start | bytes 2359304 | tf_op jit(solution)/shard_map/ppermute | solution.py:248
  132.7 6.6 %collective-permute-done.18.other = bf16[3,16,1152]{2,1,0:T(8,128)(2,1)S(1)} collective-permute-done((bf16[3,16,1152]{2,1,0:T(8,128)(2,1)S(1)}, bf16[3,16,1152]{2,1,0:T(8,128)(2,1)S(1)}, u32[]{:S(2)}, u32[]{:S(2)}) %collective-permute-start.18) | collective-permute-done | bytes 110624 | tf_op jit(solution)/shard_map/ppermute | solution.py:248
  139.6 11.6 %back.5 = (f32[264,1024]{1,0:T(8,128)S(1)}, bf16[1024,7168]{1,0:T(8,128)(2,1)}, bf16[1024,7168]{1,0:T(8,128)(2,1)}, bf16[7168,1024]{1,0:T(8,128)(2,1)}) custom-call(bf16[3,64,2048]{2,1,0:T(8,128)(2,1)S(1)} %join.11.rest_0_.own, bf16[3,64,2048]{2,1,0:T(8,128)(2,1)S(1)} %collective-permute-done.21.other, ...), custom_call_target="tpu_custom_call", output_to_operand_aliasing={{1}: (8, {}), {2}: (9, {}), {3}: (10, {})} | custom-call | tf_op jit(solution)/shard_map/back/pallas_call | solution.py:267
  151.6 11.6 %back.6 = (f32[264,1024]{1,0:T(8,128)S(1)}, bf16[1024,7168]{1,0:T(8,128)(2,1)}, bf16[1024,7168]{1,0:T(8,128)(2,1)}, bf16[7168,1024]{1,0:T(8,128)(2,1)}) custom-call(bf16[3,64,2048]{2,1,0:T(8,128)(2,1)S(1)} %join.13.rest_0_.own, bf16[3,64,2048]{2,1,0:T(8,128)(2,1)S(1)} %collective-permute-done.23.other, ...), custom_call_target="tpu_custom_call", output_to_operand_aliasing={{1}: (8, {}), {2}: (9, {}), {3}: (10, {})} | custom-call | tf_op jit(solution)/shard_map/back/pallas_call | solution.py:267
  163.2 6.3 %back.7 = (f32[264,1024]{1,0:T(8,128)S(1)}, bf16[1024,7168]{1,0:T(8,128)(2,1)}, bf16[1024,7168]{1,0:T(8,128)(2,1)}, bf16[7168,1024]{1,0:T(8,128)(2,1)}) custom-call(bf16[3,64,1152]{2,1,0:T(8,128)(2,1)S(1)} %join.15.rest_4_.own, ...), custom_call_target="tpu_custom_call", output_to_operand_aliasing={{1}: (8, {}), {2}: (9, {}), {3}: (10, {})} | custom-call | tf_op jit(solution)/shard_map/back/pallas_call | solution.py:267
  169.6 2.7 %collective-permute-done.24.other = f32[264,1024]{1,0:T(8,128)S(1)} collective-permute-done((f32[264,1024]{1,0:T(8,128)S(1)}, f32[264,1024]{1,0:T(8,128)S(1)}, u32[]{:S(2)}, u32[]{:S(2)}) %collective-permute-start.24) | collective-permute-done | bytes 1081376 | tf_op jit(solution)/shard_map/ppermute | solution.py:252
  (62 shorter events, 16.8 us)
Async XLA Ops:
  0.6 1.0 copy-start
  1.7 0.9 copy-start.1
  2.6 0.7 copy-start.2
  3.3 0.7 copy-start.4
  4.0 0.7 copy-start.6
  10.0 22.4 %collective-permute-start.1 = (bf16[3,64,2176]{2,1,0:T(8,128)(2,1)S(1)}, bf16[3,64,2176]{2,1,0:T(8,128)(2,1)S(1)}, u32[]{:S(2)}, u32[]{:S(2)}) collective-permute-start(bf16[3,64,2176]{2,1,0:T(8,128)(2,1)S(1)} %get-tuple-element.70), channel_id=1, source_target_pairs={{0,2},{2,0},{4,6},{6,4},{8,10},{10,8},{12,14},{14,12},{1,3},{3,1},... | collective-permute-start | bytes 2506760 | tf_op jit(solution)/shard_map/ppermute | solution.py:248
  25.4 23.9 %collective-permute-start = (bf16[3,64,2048]{2,1,0:T(8,128)(2,1)S(1)}, bf16[3,64,2048]{2,1,0:T(8,128)(2,1)S(1)}, u32[]{:S(2)}, u32[]{:S(2)}) collective-permute-start(bf16[3,64,2048]{2,1,0:T(8,128)(2,1)S(1)} %get-tuple-element.68), channel_id=1, source_target_pairs={{0,2},{2,0},{4,6},{6,4},{8,10},{10,8},{12,14},{14,12},{1,3},{3,1},... | collective-permute-start | bytes 2359304 | tf_op jit(solution)/shard_map/ppermute | solution.py:248
  25.5 39.8 %collective-permute-start.4 = (bf16[3,64,2048]{2,1,0:T(8,128)(2,1)S(1)}, bf16[3,64,2048]{2,1,0:T(8,128)(2,1)S(1)}, u32[]{:S(2)}, u32[]{:S(2)}) collective-permute-start(bf16[3,64,2048]{2,1,0:T(8,128)(2,1)S(1)} %get-tuple-element.77), channel_id=1, source_target_pairs={{0,2},{2,0},{4,6},{6,4},{8,10},{10,8},{12,14},{14,12},{1,3},{3,1},... | collective-permute-start | bytes 2359304 | tf_op jit(solution)/shard_map/ppermute | solution.py:248
  32.6 10.1 %collective-permute-start.2 = (bf16[3,32,2176]{2,1,0:T(8,128)(2,1)S(1)}, bf16[3,32,2176]{2,1,0:T(8,128)(2,1)S(1)}, u32[]{:S(2)}, u32[]{:S(2)}) collective-permute-start(bf16[3,32,2176]{2,1,0:T(8,128)(2,1)S(1)} %get-tuple-element.72), channel_id=1, source_target_pairs={{0,4},{2,6},{4,0},{6,2},{8,12},{10,14},{12,8},{14,10},{1,5},{3,7},... | collective-permute-start | bytes 1253384 | tf_op jit(solution)/shard_map/ppermute | solution.py:248
  42.7 13.2 %collective-permute-start.5 = (bf16[3,16,2176]{2,1,0:T(8,128)(2,1)S(1)}, bf16[3,16,2176]{2,1,0:T(8,128)(2,1)S(1)}, u32[]{:S(2)}, u32[]{:S(2)}) collective-permute-start(bf16[3,16,2176]{2,1,0:T(8,128)(2,1)S(1)} %get-tuple-element.78), channel_id=1, source_target_pairs={{0,8},{2,10},{4,12},{6,14},{8,0},{10,2},{12,4},{14,6},{1,9},{3,11}... | collective-permute-start | bytes 626696 | tf_op jit(solution)/shard_map/ppermute | solution.py:248
  49.5 19.4 %collective-permute-start.7 = (bf16[3,32,2048]{2,1,0:T(8,128)(2,1)S(1)}, bf16[3,32,2048]{2,1,0:T(8,128)(2,1)S(1)}, u32[]{:S(2)}, u32[]{:S(2)}) collective-permute-start(bf16[3,32,2048]{2,1,0:T(8,128)(2,1)S(1)} %get-tuple-element.82), channel_id=1, source_target_pairs={{0,4},{2,6},{4,0},{6,2},{8,12},{10,14},{12,8},{14,10},{1,5},{3,7},... | collective-permute-start | bytes 1179656 | tf_op jit(solution)/shard_map/ppermute | solution.py:248
  56.3 12.5 %collective-permute-start.8 = (bf16[3,16,2048]{2,1,0:T(8,128)(2,1)S(1)}, bf16[3,16,2048]{2,1,0:T(8,128)(2,1)S(1)}, u32[]{:S(2)}, u32[]{:S(2)}) collective-permute-start(bf16[3,16,2048]{2,1,0:T(8,128)(2,1)S(1)} %get-tuple-element.79.rest_0_.own), channel_id=1, source_target_pairs={{0,8},{2,10},{4,12},{6,14},{8,0},{10,2},{12,4},{14,6},{1,9},{3,11}... | collective-permute-start | bytes 589832 | tf_op jit(solution)/shard_map/ppermute | solution.py:248
  65.4 16.3 %collective-permute-start.6 = (bf16[3,32,2048]{2,1,0:T(8,128)(2,1)S(1)}, bf16[3,32,2048]{2,1,0:T(8,128)(2,1)S(1)}, u32[]{:S(2)}, u32[]{:S(2)}) collective-permute-start(bf16[3,32,2048]{2,1,0:T(8,128)(2,1)S(1)} %get-tuple-element.81), channel_id=1, source_target_pairs={{0,4},{2,6},{4,0},{6,2},{8,12},{10,14},{12,8},{14,10},{1,5},{3,7},... | collective-permute-start | bytes 1179656 | tf_op jit(solution)/shard_map/ppermute | solution.py:248
  67.3 14.5 %collective-permute-start.3 = (bf16[3,64,1024]{2,1,0:T(8,128)(2,1)S(1)}, bf16[3,64,1024]{2,1,0:T(8,128)(2,1)S(1)}, u32[]{:S(2)}, u32[]{:S(2)}) collective-permute-start(bf16[3,64,1024]{2,1,0:T(8,128)(2,1)S(1)} %get-tuple-element.76), channel_id=1, source_target_pairs={{0,2},{2,0},{4,6},{6,4},{8,10},{10,8},{12,14},{14,12},{1,3},{3,1},... | collective-permute-start | bytes 1179656 | tf_op jit(solution)/shard_map/ppermute | solution.py:248
  68.9 13.0 %collective-permute-start.10 = (bf16[3,16,2048]{2,1,0:T(8,128)(2,1)S(1)}, bf16[3,16,2048]{2,1,0:T(8,128)(2,1)S(1)}, u32[]{:S(2)}, u32[]{:S(2)}) collective-permute-start(bf16[3,16,2048]{2,1,0:T(8,128)(2,1)S(1)} %get-tuple-element.87), channel_id=1, source_target_pairs={{0,8},{2,10},{4,12},{6,14},{8,0},{10,2},{12,4},{14,6},{1,9},{3,11}... | collective-permute-start | bytes 589832 | tf_op jit(solution)/shard_map/ppermute | solution.py:248
  71.6 27.0 %collective-permute-start.12 = (bf16[3,32,2048]{2,1,0:T(8,128)(2,1)S(1)}, bf16[3,32,2048]{2,1,0:T(8,128)(2,1)S(1)}, u32[]{:S(2)}, u32[]{:S(2)}) collective-permute-start(bf16[3,32,2048]{2,1,0:T(8,128)(2,1)S(1)} %join.8.rest_0_.own), channel_id=1, source_target_pairs={{0,4},{2,6},{4,0},{6,2},{8,12},{10,14},{12,8},{14,10},{1,5},{3,7},... | collective-permute-start | bytes 1179656 | tf_op jit(solution)/shard_map/ppermute | solution.py:248
  82.3 16.4 %collective-permute-start.11 = (bf16[3,16,2048]{2,1,0:T(8,128)(2,1)S(1)}, bf16[3,16,2048]{2,1,0:T(8,128)(2,1)S(1)}, u32[]{:S(2)}, u32[]{:S(2)}) collective-permute-start(bf16[3,16,2048]{2,1,0:T(8,128)(2,1)S(1)} %get-tuple-element.90.rest_0_.own), channel_id=1, source_target_pairs={{0,8},{2,10},{4,12},{6,14},{8,0},{10,2},{12,4},{14,6},{1,9},{3,11}... | collective-permute-start | bytes 589832 | tf_op jit(solution)/shard_map/ppermute | solution.py:248
  84.8 18.0 %collective-permute-start.9 = (bf16[3,32,1024]{2,1,0:T(8,128)(2,1)S(1)}, bf16[3,32,1024]{2,1,0:T(8,128)(2,1)S(1)}, u32[]{:S(2)}, u32[]{:S(2)}) collective-permute-start(bf16[3,32,1024]{2,1,0:T(8,128)(2,1)S(1)} %get-tuple-element.86), channel_id=1, source_target_pairs={{0,4},{2,6},{4,0},{6,2},{8,12},{10,14},{12,8},{14,10},{1,5},{3,7},... | collective-permute-start | bytes 589832 | tf_op jit(solution)/shard_map/ppermute | solution.py:248
  86.7 16.2 %collective-permute-start.14 = (bf16[3,16,2048]{2,1,0:T(8,128)(2,1)S(1)}, bf16[3,16,2048]{2,1,0:T(8,128)(2,1)S(1)}, u32[]{:S(2)}, u32[]{:S(2)}) collective-permute-start(bf16[3,16,2048]{2,1,0:T(8,128)(2,1)S(1)} %get-tuple-element.93), channel_id=1, source_target_pairs={{0,8},{2,10},{4,12},{6,14},{8,0},{10,2},{12,4},{14,6},{1,9},{3,11}... | collective-permute-start | bytes 589832 | tf_op jit(solution)/shard_map/ppermute | solution.py:248
  98.7 15.0 %collective-permute-start.17 = (bf16[3,32,2048]{2,1,0:T(8,128)(2,1)S(1)}, bf16[3,32,2048]{2,1,0:T(8,128)(2,1)S(1)}, u32[]{:S(2)}, u32[]{:S(2)}) collective-permute-start(bf16[3,32,2048]{2,1,0:T(8,128)(2,1)S(1)} %join.10.rest_0_.own), channel_id=1, source_target_pairs={{0,4},{2,6},{4,0},{6,2},{8,12},{10,14},{12,8},{14,10},{1,5},{3,7},... | collective-permute-start | bytes 1179656 | tf_op jit(solution)/shard_map/ppermute | solution.py:248
  98.8 20.7 %collective-permute-start.15 = (bf16[3,64,2048]{2,1,0:T(8,128)(2,1)S(1)}, bf16[3,64,2048]{2,1,0:T(8,128)(2,1)S(1)}, u32[]{:S(2)}, u32[]{:S(2)}) collective-permute-start(bf16[3,64,2048]{2,1,0:T(8,128)(2,1)S(1)} %join.9.rest_0_.own), channel_id=1, source_target_pairs={{0,2},{2,0},{4,6},{6,4},{8,10},{10,8},{12,14},{14,12},{1,3},{3,1},... | collective-permute-start | bytes 2359304 | tf_op jit(solution)/shard_map/ppermute | solution.py:248
  103.2 9.5 %collective-permute-start.16 = (bf16[3,16,2048]{2,1,0:T(8,128)(2,1)S(1)}, bf16[3,16,2048]{2,1,0:T(8,128)(2,1)S(1)}, u32[]{:S(2)}, u32[]{:S(2)}) collective-permute-start(bf16[3,16,2048]{2,1,0:T(8,128)(2,1)S(1)} %get-tuple-element.99.rest_0_.own), channel_id=1, source_target_pairs={{0,8},{2,10},{4,12},{6,14},{8,0},{10,2},{12,4},{14,6},{1,9},{3,11}... | collective-permute-start | bytes 589832 | tf_op jit(solution)/shard_map/ppermute | solution.py:248
  113.8 25.9 %collective-permute-start.21 = (bf16[3,64,2048]{2,1,0:T(8,128)(2,1)S(1)}, bf16[3,64,2048]{2,1,0:T(8,128)(2,1)S(1)}, u32[]{:S(2)}, u32[]{:S(2)}) collective-permute-start(bf16[3,64,2048]{2,1,0:T(8,128)(2,1)S(1)} %join.11.rest_0_.own), channel_id=1, source_target_pairs={{0,2},{2,0},{4,6},{6,4},{8,10},{10,8},{12,14},{14,12},{1,3},{3,1},... | collective-permute-start | bytes 2359304 | tf_op jit(solution)/shard_map/ppermute | solution.py:248
  115.3 15.5 %collective-permute-start.19 = (bf16[3,32,2048]{2,1,0:T(8,128)(2,1)S(1)}, bf16[3,32,2048]{2,1,0:T(8,128)(2,1)S(1)}, u32[]{:S(2)}, u32[]{:S(2)}) collective-permute-start(bf16[3,32,2048]{2,1,0:T(8,128)(2,1)S(1)} %join.12.rest_0_.own), channel_id=1, source_target_pairs={{0,4},{2,6},{4,0},{6,2},{8,12},{10,14},{12,8},{14,10},{1,5},{3,7},... | collective-permute-start | bytes 1179656 | tf_op jit(solution)/shard_map/ppermute | solution.py:248
  117.9 12.0 %collective-permute-start.13 = (bf16[3,16,1024]{2,1,0:T(8,128)(2,1)S(1)}, bf16[3,16,1024]{2,1,0:T(8,128)(2,1)S(1)}, u32[]{:S(2)}, u32[]{:S(2)}) collective-permute-start(bf16[3,16,1024]{2,1,0:T(8,128)(2,1)S(1)} %get-tuple-element.92), channel_id=1, source_target_pairs={{0,8},{2,10},{4,12},{6,14},{8,0},{10,2},{12,4},{14,6},{1,9},{3,11}... | collective-permute-start | bytes 294920 | tf_op jit(solution)/shard_map/ppermute | solution.py:248
  130.8 20.8 %collective-permute-start.23 = (bf16[3,64,2048]{2,1,0:T(8,128)(2,1)S(1)}, bf16[3,64,2048]{2,1,0:T(8,128)(2,1)S(1)}, u32[]{:S(2)}, u32[]{:S(2)}) collective-permute-start(bf16[3,64,2048]{2,1,0:T(8,128)(2,1)S(1)} %join.13.rest_0_.own), channel_id=1, source_target_pairs={{0,2},{2,0},{4,6},{6,4},{8,10},{10,8},{12,14},{14,12},{1,3},{3,1},... | collective-permute-start | bytes 2359304 | tf_op jit(solution)/shard_map/ppermute | solution.py:248
  132.6 6.7 %collective-permute-start.18 = (bf16[3,16,1152]{2,1,0:T(8,128)(2,1)S(1)}, bf16[3,16,1152]{2,1,0:T(8,128)(2,1)S(1)}, u32[]{:S(2)}, u32[]{:S(2)}) collective-permute-start(bf16[3,16,1152]{2,1,0:T(8,128)(2,1)S(1)} %get-tuple-element.101.rest_0_.own), channel_id=1, source_target_pairs={{0,8},{2,10},{4,12},{6,14},{8,0},{10,2},{12,4},{14,6},{1,9},{3,11}... | collective-permute-start | bytes 331784 | tf_op jit(solution)/shard_map/ppermute | solution.py:248
  139.4 11.9 %collective-permute-start.20 = (bf16[3,32,1152]{2,1,0:T(8,128)(2,1)S(1)}, bf16[3,32,1152]{2,1,0:T(8,128)(2,1)S(1)}, u32[]{:S(2)}, u32[]{:S(2)}) collective-permute-start(bf16[3,32,1152]{2,1,0:T(8,128)(2,1)S(1)} %join.14.rest_4_.own), channel_id=1, source_target_pairs={{0,4},{2,6},{4,0},{6,2},{8,12},{10,14},{12,8},{14,10},{1,5},{3,7},... | collective-permute-start | bytes 663560 | tf_op jit(solution)/shard_map/ppermute | solution.py:248
  151.3 11.9 %collective-permute-start.22 = (bf16[3,64,1152]{2,1,0:T(8,128)(2,1)S(1)}, bf16[3,64,1152]{2,1,0:T(8,128)(2,1)S(1)}, u32[]{:S(2)}, u32[]{:S(2)}) collective-permute-start(bf16[3,64,1152]{2,1,0:T(8,128)(2,1)S(1)} %join.15.rest_4_.own), channel_id=1, source_target_pairs={{0,2},{2,0},{4,6},{6,4},{8,10},{10,8},{12,14},{14,12},{1,3},{3,1},... | collective-permute-start | bytes 1327112 | tf_op jit(solution)/shard_map/ppermute | solution.py:248
  163.2 9.1 %copy-start.3 = (f32[1024]{0:T(1024)S(1)}, f32[1024]{0:T(1024)}, u32[]{:S(2)}) copy-start(f32[1024]{0:T(1024)} %param.11) | copy-start | bytes 12292
  163.2 9.1 %copy-start.5 = (s32[128]{0:T(128)S(1)}, s32[128]{0:T(128)}, u32[]{:S(2)}) copy-start(s32[128]{0:T(128)} %param.9) | copy-start | bytes 1540
  169.5 2.8 %collective-permute-start.24 = (f32[264,1024]{1,0:T(8,128)S(1)}, f32[264,1024]{1,0:T(8,128)S(1)}, u32[]{:S(2)}, u32[]{:S(2)}) collective-permute-start(f32[264,1024]{1,0:T(8,128)S(1)} %get-tuple-element.113.own), channel_id=1, source_target_pairs={{0,1},{1,0},{2,3},{3,2},{4,5},{5,4},{6,7},{7,6},{8,9},{9,8},{10,11... | collective-permute-start | bytes 3244040 | tf_op jit(solution)/shard_map/ppermute | solution.py:252
